TPU v7x, 256 devices: a whole 4x4x8 slice. The times are simulated.
256 devices in a mesh: ctx: 32 (over z, y_lo, core), tp: 8 (over x, y_hi).
Axes of the slice: x: 4, y: 4 (y_hi: 2, y_lo: 2; y = y_hi * 2 + y_lo), z: 8, core: 2. Of those that a mesh axis runs over, the one named last changes fastest.
Arguments:
- tokens: bfloat16 [16384, 4096], P('ctx', 'tp'), may hold values from -6 to 6
- w_in: bfloat16 [3, 4096, 4096], P(None, 'ctx', 'tp'), may hold values from -0.09375 to 0.09375
- short_taps: float32 [3, 4096, 3], P(None, 'tp'), may hold values from -3 to 3
- filters: bfloat16 [256, 16384], P('tp', 'ctx'), may hold values from 0 to 0.5
- skip: float32 [4096], P('tp'), may hold values from 0.5 to 1.5
- w_out: bfloat16 [4096, 4096], P('tp', 'ctx'), may hold values from -0.09375 to 0.09375
Outputs:
- mixed: bfloat16 [16384, 4096], P('ctx', 'tp')
All inputs are finite; a program needn't handle non-finite values.
Results may differ from a plain program's by a relative error of at most 0.015.
Values may be sent and summed in bfloat16 or wider, within the bound.
No kernel may reach another device: no remote copies, remote signals or barrier semaphores. Data moves between devices by JAX's collectives and lax.ppermute only.
A program may use at most 64 MiB of HBM per device.

v0:
```python
import math

import jax
import jax.numpy as jnp
from jax import lax
from jax.sharding import PartitionSpec as P

PRECISE = lax.Precision.HIGH


def from_behind(block, axis, distance):
    devices = range(lax.axis_size(axis))
    route = [(i - distance, i) for i in devices if i - distance in devices]
    return lax.ppermute(block, axis, route)


def dft_tables(length):
    index = jnp.arange(length, dtype=jnp.int32)
    angle = 2.0 * math.pi / length * (index[:, None] * index[None, :] % length).astype(jnp.float32)
    return (jnp.cos(angle), jnp.sin(angle))


def twiddle_tables(source_matrix_lines, cols, total):
    row_index = jnp.arange(source_matrix_lines, dtype=jnp.int32)
    col_index = jnp.arange(cols, dtype=jnp.int32)
    angle = (
        2.0
        * math.pi
        / total
        * (row_index[:, None] * col_index[None, :] % total).astype(jnp.float32)
    )
    return (jnp.cos(angle), jnp.sin(angle))


def factor_length(total):
    best = 1
    for factor in range(1, math.isqrt(total) + 1):
        if total % factor == 0 and total // factor % 2 == 0:
            best = factor
    return (total // best, best)


def left_mult(table, array):
    return jnp.einsum("kn,cnm->ckm", table, array, precision=PRECISE)


def right_mult(array, table):
    return jnp.einsum("ckn,nm->ckm", array, table, precision=PRECISE)


def causal_conv(signal, kernel):
    count, length = signal.shape
    kernel_count = kernel.shape[0]
    share = count // kernel_count
    total = 2 * length
    source_matrix_lines, cols = factor_length(total)
    cos_a, sin_a = dft_tables(source_matrix_lines)
    cos_b, sin_b = dft_tables(cols)
    tw_cos, tw_sin = twiddle_tables(source_matrix_lines, cols, total)
    stacked = jnp.concatenate([signal, kernel], axis=0)
    padded = jnp.pad(stacked, ((0, 0), (0, length))).reshape(
        count + kernel_count, source_matrix_lines, cols
    )
    first_re = left_mult(cos_a, padded)
    first_im = -left_mult(sin_a, padded)
    turned_re = first_re * tw_cos + first_im * tw_sin
    turned_im = first_im * tw_cos - first_re * tw_sin
    spec_re = right_mult(turned_re, cos_b) + right_mult(turned_im, sin_b)
    spec_im = right_mult(turned_im, cos_b) - right_mult(turned_re, sin_b)
    sig_re = spec_re[:count].reshape(kernel_count, share, source_matrix_lines, cols)
    sig_im = spec_im[:count].reshape(kernel_count, share, source_matrix_lines, cols)
    ker_re = spec_re[count:][:, None]
    ker_im = spec_im[count:][:, None]
    prod_re = (sig_re * ker_re - sig_im * ker_im).reshape(count, source_matrix_lines, cols)
    prod_im = (sig_re * ker_im + sig_im * ker_re).reshape(count, source_matrix_lines, cols)
    back_re = right_mult(prod_re, cos_b) - right_mult(prod_im, sin_b)
    back_im = right_mult(prod_im, cos_b) + right_mult(prod_re, sin_b)
    reverted_re = back_re * tw_cos - back_im * tw_sin
    reverted_im = back_im * tw_cos + back_re * tw_sin
    result = (left_mult(cos_a, reverted_re) - left_mult(sin_a, reverted_im))[
        :, : source_matrix_lines // 2
    ]
    return (result / total).reshape(count, length)


def convolve(pieces):
    signal, kernel = pieces
    shape = signal.shape
    flat_signal = signal.reshape(-1, shape[-1]).astype(jnp.float32)
    flat_kernel = kernel.reshape(-1, shape[-1]).astype(jnp.float32)
    return causal_conv(flat_signal, flat_kernel).astype(jnp.bfloat16).reshape(shape)


def local(tokens, w_in, short_taps, filters, skip, w_out):
    features = lax.all_gather(tokens, "tp", axis=1, tiled=True)
    tok_rows = features.shape[0]
    chan_count = w_in.shape[2]
    outputs = []
    for picked_entry_place in range(3):
        outputs.append(
            lax.dot_general(
                lax.all_gather(w_in[picked_entry_place], "ctx", axis=0, tiled=True),
                features,
                (((0,), (1,)), ((), ())),
                preferred_element_type=jnp.float32,
            )
        )
    projected = jnp.stack(outputs).astype(jnp.bfloat16)
    tap_count = short_taps.shape[2]
    earlier = from_behind(projected[:, :, tok_rows - (tap_count - 1) :], "ctx", 1)
    extended = jnp.concatenate([earlier, projected], axis=2).astype(jnp.float32)
    smoothed = jnp.zeros(projected.shape, jnp.float32)
    for lag in range(tap_count):
        begin = tap_count - 1 - lag
        smoothed = (
            smoothed + short_taps[:, :, lag : lag + 1] * extended[:, :, begin : begin + tok_rows]
        )
    query_gate = smoothed[0]
    mixed_in = (smoothed[1] * smoothed[2]).astype(jnp.bfloat16)
    ctx_count = lax.axis_size("ctx")
    group_rows = filters.shape[0]
    per_group = chan_count // group_rows
    local_groups = group_rows // ctx_count
    blocks = (
        mixed_in.reshape(ctx_count, local_groups, per_group, tok_rows),
        filters.reshape(ctx_count, local_groups, 1, tok_rows),
    )
    convolved = convolve(
        (
            lax.all_to_all(blocks[0], "ctx", split_axis=0, concat_axis=3, tiled=True),
            lax.all_to_all(blocks[1], "ctx", split_axis=0, concat_axis=3, tiled=True),
        )
    )
    returned = lax.all_to_all(convolved, "ctx", split_axis=3, concat_axis=0, tiled=True).reshape(
        chan_count, tok_rows
    )
    gated = (
        query_gate * (returned.astype(jnp.float32) + skip[:, None] * mixed_in.astype(jnp.float32))
    ).astype(jnp.bfloat16)
    partial_out = lax.dot_general(
        gated,
        lax.all_gather(w_out, "ctx", axis=1, tiled=True),
        (((0,), (0,)), ((), ())),
        preferred_element_type=jnp.float32,
    )
    return lax.psum_scatter(partial_out.astype(jnp.bfloat16), "tp", scatter_dimension=1, tiled=True)


def solution(mesh):
    return jax.shard_map(
        local,
        mesh=mesh,
        in_specs=(
            P("ctx", "tp"),
            P(None, "ctx", "tp"),
            P(None, "tp", None),
            P("tp", "ctx"),
            P("tp"),
            P("tp", "ctx"),
        ),
        out_specs=P("ctx", "tp"),
        check_vma=False,
    )
```

profile of v0, /device:TPU:8, one launch (start us, length us, event | category | flops | bytes accessed | tf_op | source)
XLA Modules:
  0.0 649.1 jit_solution(18124099798492770852)
XLA Ops:
  13.0 10.1 %all-to-all-start.1 = ((bf16[32,2,256]{2,1,0:T(2,128)(2,1)}), bf16[32,2,256]{2,1,0:T(2,128)(2,1)S(1)}, u32[]{:S(2)}, u32[]{:S(2)}) async-start(bf16[32,2,256]{2,1,0:T(2,128)(2,1)} %reshape.148), calls=%async_computation.1 | async-start | bytes 65536 | tf_op jit(solution)/shard_map/all_to_all | solution.py:131
  23.9 71.2 %all-gather.9.cloned.1.call-done = bf16[512,4096]{1,0:T(8,128)(2,1)} async-done(((bf16[512,512]{1,0:T(8,128)(2,1)}), bf16[512,4096]{1,0:T(8,128)(2,1)}) %all-gather.9.cloned.1.call-update) | async-done | bytes 4194320 | tf_op jit(solution)/shard_map/all_gather | solution.py:95
  95.1 67.9 %all-gather.17.cloned.1.call-done = bf16[1,4096,512]{2,1,0:T(8,128)(2,1)} async-done(((bf16[1,128,512]{2,1,0:T(8,128)(2,1)}), bf16[1,4096,512]{2,1,0:T(8,128)(2,1)}) %all-gather.17.cloned.1.call-update) | async-done | bytes 4194320 | tf_op jit(solution)/shard_map/all_gather | solution.py:102
  163.0 5.8 fusion.32
  168.8 62.6 %all-gather.15.cloned.1.call-done = bf16[1,4096,512]{2,1,0:T(8,128)(2,1)} async-done(((bf16[1,128,512]{2,1,0:T(8,128)(2,1)}), bf16[1,4096,512]{2,1,0:T(8,128)(2,1)}) %all-gather.15.cloned.1.call-update) | async-done | bytes 4194320 | tf_op jit(solution)/shard_map/all_gather | solution.py:102
  231.4 5.8 fusion.35
  237.2 62.4 %all-gather.13.cloned.1.call-done = bf16[1,4096,512]{2,1,0:T(8,128)(2,1)} async-done(((bf16[1,128,512]{2,1,0:T(8,128)(2,1)}), bf16[1,4096,512]{2,1,0:T(8,128)(2,1)}) %all-gather.13.cloned.1.call-update) | async-done | bytes 4194320 | tf_op jit(solution)/shard_map/all_gather | solution.py:102
  299.6 5.8 fusion.38
  307.5 2.8 collective-permute-done
  314.7 9.0 %all-to-all-start = ((bf16[32,1,16,512]{3,2,1,0:T(8,128)(2,1)}), bf16[32,1,16,512]{3,2,1,0:T(8,128)(2,1)}, u32[]{:S(2)}, u32[]{:S(2)}) async-start(bf16[32,1,16,512]{3,2,1,0:T(8,128)(2,1)} %bitcast.142), calls=%async_computation | async-start | bytes 1048576 | tf_op jit(solution)/shard_map/all_to_all | solution.py:130
  327.7 13.8 %all-to-all-done = bf16[32,1,16,512]{3,2,1,0:T(8,128)(2,1)} async-done(((bf16[32,1,16,512]{3,2,1,0:T(8,128)(2,1)}), bf16[32,1,16,512]{3,2,1,0:T(8,128)(2,1)}, u32[]{:S(2)}, u32[]{:S(2)}) %all-to-all-start) | async-done | bytes 524320 | tf_op jit(solution)/shard_map/all_to_all | solution.py:130
  349.9 2.3 convolution_add_fusion
  354.5 2.4 convolution_subtract_fusion
  362.3 2.8 fusion.12
  365.1 3.0 subtract_bitcast_fusion
  373.2 15.5 %copy.82 = bf16[1,1,16,16384]{2,1,0,3:T(2,128)(2,1)} copy(bf16[1,1,16,16384]{3,2,1,0:T(8,128)(2,1)} %convert_element_type.140) | data formatting | bytes 1048576 | tf_op jit(solution)/shard_map/convert_element_type | solution.py:91
  388.7 90.7 %reduce.1 = bf16[16384,16]{1,0:T(8,128)(2,1)} reduce(bf16[16384,1,1,16]{3,2,1,0:T(2,128)(2,1)} %bitcast.134, bf16[]{:T(256)} %broadcast.138), dimensions={1,2}, to_apply=%bitcast.127.reduce_sub_computation | reduce | bytes 1048578
  479.4 7.1 %reshape.150 = bf16[32,2,4096]{2,1,0:T(2,128)(2,1)} reshape(bf16[16384,16]{1,0:T(8,128)(2,1)} %reduce.1) | data formatting | bytes 1048576
  486.5 22.8 %all_to_all.12 = bf16[32,2,4096]{2,1,0:T(2,128)(2,1)} all-to-all(bf16[32,2,4096]{2,1,0:T(2,128)(2,1)} %reshape.150), channel_id=1, replica_groups=mesh['ctx'=32,'tp'=8] {'ctx'}, dimensions={0} | all-to-all | bytes 1048576 | tf_op jit(solution)/shard_map/all_to_all | solution.py:134
  509.3 18.3 %reshape.151 = bf16[16384,1,1,16]{3,2,1,0:T(2,128)(2,1)} reshape(bf16[32,2,4096]{2,1,0:T(2,128)(2,1)} %all_to_all.12) | data formatting | bytes 1048576
  527.6 16.2 %copy.83 = bf16[1,1,16,16384]{3,2,1,0:T(8,128)(2,1)} copy(bf16[1,1,16,16384]{2,1,0,3:T(2,128)(2,1)} %bitcast.135) | data formatting | bytes 1048576 | tf_op jit(solution)/shard_map/all_to_all | solution.py:134
  546.6 2.5 copy.85
  549.2 7.0 %convolution_convert_fusion = bf16[512,4096]{1,0:T(8,128)(2,1)} fusion(bf16[512,4096]{1,0:T(8,128)(2,1)} %all-gather.11.cloned.1.call-done, f32[3,512,512]{1,2,0:T(8,128)S(1)} %fusion.8, f32[512,512]{0,1:T(8,128)} %copy.85, bf16[1,512,512]{1,2,0:T(8,128)(2,1)} %fusion.42, f32[512]{0:T(512)S(1)} %copy-done.2), kind=kOutput, calls=%fused_computation | convolution fusion | flops 2150891520 | bytes 11012096 | tf_op jit(solution)/shard_map/dot_general | solution.py:140
  556.2 85.8 %reduce-scatter.2.cloned.1.call-done = bf16[512,512]{1,0:T(8,128)(2,1)} async-done(((bf16[512,4096]{1,0:T(8,128)(2,1)}), bf16[512,512]{1,0:T(8,128)(2,1)}) %reduce-scatter.2.cloned.1.call-update) | async-done | bytes 524304 | tf_op jit(solution)/shard_map/reduce_scatter | solution.py:146
  (55 shorter events, 41.7 us)
Async XLA Ops:
  6.5 88.6 %all-gather.9.cloned.1.call-start = ((), (), s32[]{:S(2)}) async-start(), calls=%async_computation.4 | async-start | bytes 4718592 | tf_op jit(solution)/shard_map/all_gather | solution.py:95
  7.3 155.7 %all-gather.17.cloned.1.call-start = ((), (), s32[]{:S(2)}) async-start(), calls=%async_computation.9 | async-start | bytes 4325376 | tf_op jit(solution)/shard_map/all_gather | solution.py:102
  9.1 222.2 %all-gather.15.cloned.1.call-start = ((), (), s32[]{:S(2)}) async-start(), calls=%async_computation.8 | async-start | bytes 4325376 | tf_op jit(solution)/shard_map/all_gather | solution.py:102
  9.8 289.7 %all-gather.13.cloned.1.call-start = ((), (), s32[]{:S(2)}) async-start(), calls=%async_computation.7 | async-start | bytes 4325376 | tf_op jit(solution)/shard_map/all_gather | solution.py:102
  13.0 301.7 %all-to-all-start.1 = ((bf16[32,2,256]{2,1,0:T(2,128)(2,1)}), bf16[32,2,256]{2,1,0:T(2,128)(2,1)S(1)}, u32[]{:S(2)}, u32[]{:S(2)}) async-start(bf16[32,2,256]{2,1,0:T(2,128)(2,1)} %reshape.148), calls=%async_computation.1 | async-start | bytes 65536 | tf_op jit(solution)/shard_map/all_to_all | solution.py:131
  305.4 4.9 collective-permute-start
  314.7 9.6 %copy-start.1 = (bf16[32,2,256]{2,1,0:T(2,128)(2,1)}, bf16[32,2,256]{2,1,0:T(2,128)(2,1)S(1)}, u32[]{:S(2)}) copy-start(bf16[32,2,256]{2,1,0:T(2,128)(2,1)S(1)} %all-to-all-done.1) | copy-start | bytes 98308
  314.7 26.7 %all-to-all-start = ((bf16[32,1,16,512]{3,2,1,0:T(8,128)(2,1)}), bf16[32,1,16,512]{3,2,1,0:T(8,128)(2,1)}, u32[]{:S(2)}, u32[]{:S(2)}) async-start(bf16[32,1,16,512]{3,2,1,0:T(8,128)(2,1)} %bitcast.142), calls=%async_computation | async-start | bytes 1048576 | tf_op jit(solution)/shard_map/all_to_all | solution.py:130
  323.7 225.5 %all-gather.11.cloned.1.call-start = ((), (), s32[]{:S(2)}) async-start(), calls=%async_computation.5 | async-start | bytes 4325376 | tf_op jit(solution)/shard_map/all_gather | solution.py:142
  324.3 317.7 %reduce-scatter.2.cloned.1.call-start = ((), (), s32[]{:S(2)}) async-start(), calls=%async_computation.6 | async-start | bytes 4718592 | tf_op jit(solution)/shard_map/reduce_scatter | solution.py:146
  361.0 1.4 copy-start
  545.0 4.2 copy-start.2
Sparse Core Ops, SparseCore 0:
  9.8 85.2 all-gather.8
  97.0 65.9 all-gather.16
  164.9 66.4 all-gather.14
  233.1 66.4 all-gather.12
  326.0 73.0 all-gather.10
  556.3 85.6 reduce-scatter.1
where the time goes:
time: 660 us; the launch traced here: 649 us
  waiting for transfers between devices  369 us (56%)
  other arithmetic  96.9 us (15%)
  local copies, waits for them, and re-layouts  76.2 us (12%)
  matrix products  48.4 us (7%)
  blocking collectives  22.8 us (3%)
  starting transfers between devices  21.9 us (3%)
  between operations  14 us (2%)
    all_gather x3, waiting for transfers between devices, local(): lax.all_gather(w_in[picked_entry_place], 'ctx', axis=0, tiled=True)  193 us
    unnamed x1, other arithmetic  90.7 us
    reduce_scatter x1, waiting for transfers between devices, local(): lax.psum_scatter(partial_out.astype(jnp.bfloat16), 'tp', scatter_dimensio...  85.8 us
    all_gather x1, waiting for transfers between devices, local(): features = lax.all_gather(tokens, 'tp', axis=1, tiled=True)  71.2 us
    unnamed x15, local copies, waits for them, and re-layouts  30.1 us
    all_to_all x1, blocking collectives, local(): lax.all_to_all(convolved, 'ctx', split_axis=3, concat_axis=0, tiled=True)  22.8 us
    convert_element_type x3, local copies, waits for them, and re-layouts, convolve(): causal_conv(flat_signal, flat_kernel).astype(jnp.bfloat16).reshape(shape)  19.7 us
    dot_general x3, matrix products, local(): lax.dot_general(lax.all_gather(w_in[picked_entry_place], 'ctx', axis=0, t...  17.4 us
  transfers between devices with their start and end apart: 9, of which 7 were waited for; matrix products, arithmetic and copies ran while one was open for 33% of the time, Pallas kernels for 0%

commit v1 on v0

v1 whole, which is shorter than its diff:
```python
import functools

import jax
import jax.numpy as jnp
from jax import lax
from jax.experimental import pallas as pl
from jax.experimental.pallas import tpu as pltpu
from jax.sharding import PartitionSpec as P

F32 = jnp.float32
BF16 = jnp.bfloat16
ANY = pl.BlockSpec(memory_space=pl.ANY)
VMEM = pl.BlockSpec(memory_space=pltpu.VMEM)
VMEM_LIMIT = 48 * 1024 * 1024

NZ, NX = 8, 4
CTX = NZ * 4
TP = NX * 2
TAIL = 16


def barrier(*arrays):
    return lax.optimization_barrier(arrays)


def shift_z(block, step):
    route = [(i, (i + 4 * step) % CTX) for i in range(CTX)]
    return lax.ppermute(block, "ctx", route)


def swap_ctx(block, mask):
    return lax.ppermute(block, "ctx", [(i, i ^ mask) for i in range(CTX)])


def swap_core(block):
    return swap_ctx(block, 1)


def swap_ylo(block):
    return swap_ctx(block, 2)


def shift_x(block, step):
    route = [(j, (j + 2 * step) % TP) for j in range(TP)]
    return lax.ppermute(block, "tp", route)


def swap_yhi(block):
    return lax.ppermute(block, "tp", [(j, j ^ 1) for j in range(TP)])


def gather_z(block):
    groups = [[4 * z + rest for z in range(NZ)] for rest in range(4)]
    return lax.all_gather(block, "ctx", axis=0, tiled=False, axis_index_groups=groups)


def gather_tp(own):
    rows = own.shape[0]
    half = rows // 2
    near = swap_yhi(own)
    own_right, own_left = shift_x(own, 1), shift_x(own, -1)
    near_right, near_left = shift_x(near, 1), shift_x(near, -1)
    far_right = shift_x(jnp.concatenate([own_right[:half], near_right[:half]]), 1)
    far_left = shift_x(jnp.concatenate([own_left[half:], near_left[half:]]), -1)
    return [own, near, own_right, own_left, near_right, near_left, far_right, far_left]


def piece_copies(pieces, dst, first_row, sem):
    me = lax.axis_index("tp")
    x, y = me // 2, me % 2
    width = pieces[0].shape[1]
    rows = pieces[0].shape[0]
    half = rows // 2

    def place(dx, dy, begin, count):
        there = ((x + dx + NX) % NX) * 2 + (y + dy) % 2
        lanes = pl.ds(pl.multiple_of(there * width, width), width)
        return dst.at[pl.ds(first_row + begin, count), lanes]

    whole = [(0, 0), (0, 1), (-1, 0), (1, 0), (-1, 1), (1, 1)]
    copies = []
    for ref, (dx, dy) in zip(pieces[:6], whole):
        copies.append((ref, place(dx, dy, 0, rows)))
    for ref, begin in ((pieces[6], 0), (pieces[7], half)):
        for dy in (0, 1):
            copies.append((ref.at[pl.ds(dy * half, half)], place(2, dy, begin, half)))
    return [pltpu.make_async_copy(src, to, sem) for src, to in copies]


def weight_slots():
    me = lax.axis_index("ctx")
    return (me // 2) % 2, me % 2


def project_kernel(n_proj, width, *refs):
    pieces = refs[:8]
    tail, mine, other, taps = refs[8:12]
    outs = refs[12:-6]
    tok, wts, part, tok_sem, tail_sem, w_sems = refs[-6:]
    rows = pieces[0].shape[0]
    total = wts.shape[3]
    chan = total // n_proj
    n_tiles = chan // width
    y, core = weight_slots()

    copies = piece_copies(pieces, tok, TAIL, tok_sem)
    for j in range(TP):
        copies.append(
            pltpu.make_async_copy(tail.at[j], tok.at[pl.ds(0, TAIL), pl.ds(j * 512, 512)], tail_sem)
        )
    for copy in copies:
        copy.start()
    w_copies = []
    for tile in range(n_tiles):
        group = []
        for proj in range(n_proj):
            lanes = pl.ds(proj * chan + tile * width, width)
            for ref, dc in ((mine, 0), (other, 1)):
                for dy in (0, 1):
                    slot = ((y + dy) % 2) * 2 + (core + dc) % 2
                    group.append(
                        pltpu.make_async_copy(
                            ref.at[:, dy, :, lanes], wts.at[:, slot, :, lanes], w_sems.at[tile]
                        )
                    )
        for copy in group:
            copy.start()
        w_copies.append(group)
    for copy in copies:
        copy.wait()
    for tile in range(n_tiles):
        for copy in w_copies[tile]:
            copy.wait()
        smooth = []
        for proj in range(n_proj):
            lanes = pl.ds(proj * chan + tile * width, width)
            weights = wts[:, :, :, lanes].reshape(-1, width)
            product = jnp.dot(tok[...], weights, preferred_element_type=F32)
            part[proj] = product.astype(BF16).astype(F32)
            cols = pl.ds(tile * width, width)
            value = taps[proj, 0:1, cols] * part[proj, pl.ds(TAIL, rows), :]
            value = value + taps[proj, 1:2, cols] * part[proj, pl.ds(TAIL - 1, rows), :]
            value = value + taps[proj, 2:3, cols] * part[proj, pl.ds(TAIL - 2, rows), :]
            smooth.append(value)
        cols = pl.ds(tile * width, width)
        if n_proj == 1:
            outs[0][:, cols] = smooth[0]
        else:
            mixed = smooth[0] * smooth[1]
            outs[0][:, cols] = mixed.astype(BF16)
            turned = mixed.T.astype(BF16)
            for a in range(2):
                block = turned[:, 256 * a : 256 * a + 256].reshape(width // 16, 16, 256)
                outs[1][pl.ds(tile * (width // 16), width // 16), pl.ds(16 * a, 16), :] = block


def project(pieces, tail, mine, other, taps, out_shapes):
    n_proj = taps.shape[0]
    total = mine.shape[-1]
    width = 256
    n_tiles = total // n_proj // width
    rows = pieces[0].shape[0]
    depth = TP * pieces[0].shape[1]
    return pl.pallas_call(
        functools.partial(project_kernel, n_proj, width),
        out_shape=out_shapes,
        in_specs=[ANY] * 8 + [ANY, ANY, ANY, VMEM],
        out_specs=[VMEM] * len(out_shapes),
        scratch_shapes=[
            pltpu.VMEM((TAIL + rows, depth), BF16),
            pltpu.VMEM((NZ, 4, depth // CTX, total), BF16),
            pltpu.VMEM((n_proj, TAIL + rows, width), F32),
            pltpu.SemaphoreType.DMA,
            pltpu.SemaphoreType.DMA,
            pltpu.SemaphoreType.DMA((n_tiles,)),
        ],
        compiler_params=pltpu.CompilerParams(vmem_limit_bytes=VMEM_LIMIT),
        name="project%d" % n_proj,
    )(*pieces, tail, mine, other, taps)


def toeplitz_kernel(seg_ref, out_ref):
    low = lax.broadcasted_iota(jnp.int32, (128, 128), 1) >= lax.broadcasted_iota(
        jnp.int32, (128, 128), 0
    )

    def turn(m):
        row = jnp.broadcast_to(seg_ref[pl.ds(m, 1), :], (128, 128))
        return pltpu.roll(row, 0, 1, stride=1, stride_axis=0)

    def body(d, before):
        even = turn(2 * d)
        odd = turn(2 * d + 1)
        first = jnp.where(low, even, before).astype(BF16)
        second = jnp.where(low, odd, even).astype(BF16)
        out_ref[d, 0:128, 0:128] = first
        out_ref[d, 128:256, 128:256] = first
        out_ref[d, 0:128, 128:256] = second

        @pl.when(d < 63)
        def _():
            out_ref[d + 1, 128:256, 0:128] = second

        return odd

    out_ref[0, 128:256, 0:128] = jnp.zeros((128, 128), BF16)
    lax.fori_loop(0, 64, body, jnp.zeros((128, 128), F32))


def toeplitz(segments):
    return pl.pallas_call(
        toeplitz_kernel,
        out_shape=jax.ShapeDtypeStruct((64, 256, 256), BF16),
        in_specs=[VMEM],
        out_specs=VMEM,
        compiler_params=pltpu.CompilerParams(vmem_limit_bytes=VMEM_LIMIT),
        name="toeplitz",
    )(segments)


FOLD = 4


def conv_kernel(x_ref, h_hbm, y_ref, wide, acc, h_ref, sems):
    rows = x_ref.shape[0]
    steps = h_ref.shape[0]
    copies = [pltpu.make_async_copy(h_hbm.at[g], h_ref.at[g], sems.at[g]) for g in range(steps)]
    for copy in copies:
        copy.start()
    for k in range(FOLD):
        if k:
            wide[0 : 16 * k, 256 * k : 256 * k + 256] = jnp.zeros((16 * k, 256), BF16)
        wide[16 * k : rows, 256 * k : 256 * k + 256] = x_ref[0 : rows - 16 * k, :]
    for g in range(steps):
        copies[g].wait()
        skip = 16 * FOLD * g
        product = jnp.dot(wide[0 : rows - skip, :], h_ref[g], preferred_element_type=F32)
        if g == 0:
            acc[...] = product
        else:
            acc[skip:rows, :] += product
    y_ref[...] = acc[...].astype(BF16)


def conv(x, table):
    rows = x.shape[0]
    steps = 64 // FOLD
    return pl.pallas_call(
        conv_kernel,
        out_shape=jax.ShapeDtypeStruct((rows, 256), BF16),
        in_specs=[VMEM, ANY],
        out_specs=VMEM,
        scratch_shapes=[
            pltpu.VMEM((rows, FOLD * 256), BF16),
            pltpu.VMEM((rows, 256), F32),
            pltpu.VMEM((steps, FOLD * 256, 256), BF16),
            pltpu.SemaphoreType.DMA((steps,)),
        ],
        compiler_params=pltpu.CompilerParams(vmem_limit_bytes=VMEM_LIMIT),
        name="conv",
    )(x, table.reshape(steps, FOLD * 256, 256))


def gate_kernel(back_ref, mixed_ref, query_ref, skip_ref, out_ref):
    chan = mixed_ref.shape[1]
    for a in range(2):
        block = back_ref[:, 16 * a : 16 * a + 16, :].reshape(chan, 256)
        turned = block.astype(F32).T
        here = pl.ds(256 * a, 256)
        mixed = mixed_ref[here, :].astype(F32)
        out_ref[here, :] = (query_ref[here, :] * (turned + skip_ref[...] * mixed)).astype(BF16)


def gate(back, mixed, query, skip):
    return pl.pallas_call(
        gate_kernel,
        out_shape=jax.ShapeDtypeStruct(mixed.shape, BF16),
        in_specs=[VMEM] * 4,
        out_specs=VMEM,
        compiler_params=pltpu.CompilerParams(vmem_limit_bytes=VMEM_LIMIT),
        name="gate",
    )(back, mixed, query, skip)


def output_kernel(*refs):
    pieces = refs[:8]
    mine, other, out_ref, act, wts, act_sem, w_sem = refs[8:]
    y, core = weight_slots()
    copies = piece_copies(pieces, act, 0, act_sem)
    depth, width = mine.shape[2:]
    for ref, dc in ((mine, 0), (other, 1)):
        for dy in (0, 1):
            slot = ((y + dy) % 2) * 2 + (core + dc) % 2
            lanes = pl.ds(pl.multiple_of(slot * width, width), width)
            copies.append(pltpu.make_async_copy(ref.at[:, dy], wts.at[:, :, lanes], w_sem))
    for copy in copies:
        copy.start()
    for copy in copies:
        copy.wait()
    weights = wts[...].reshape(-1, wts.shape[2])
    out_ref[...] = jnp.dot(act[...], weights, preferred_element_type=F32).astype(BF16)


def output(pieces, mine, other):
    rows, part = pieces[0].shape
    depth, width = mine.shape[2:]
    return pl.pallas_call(
        output_kernel,
        out_shape=jax.ShapeDtypeStruct((rows, 4 * width), BF16),
        in_specs=[ANY] * 10,
        out_specs=VMEM,
        scratch_shapes=[
            pltpu.VMEM((rows, TP * part), BF16),
            pltpu.VMEM((NZ, depth, 4 * width), BF16),
            pltpu.SemaphoreType.DMA,
            pltpu.SemaphoreType.DMA,
        ],
        compiler_params=pltpu.CompilerParams(vmem_limit_bytes=VMEM_LIMIT),
        name="output",
    )(*pieces, mine, other)


def gather_weights(block):
    pair = jnp.stack([block, swap_ylo(block)])
    mine = gather_z(pair)
    return mine, swap_core(mine)


def local(tokens, w_in, short_taps, filters, skip, w_out):
    rows, _ = tokens.shape
    chan = w_in.shape[2]
    taps = short_taps.transpose(0, 2, 1)

    kv = jnp.concatenate([w_in[1], w_in[2]], axis=1)
    kv_mine, kv_other = gather_weights(kv)

    before = lax.ppermute(tokens[rows - TAIL :], "ctx", [(i, i + 1) for i in range(CTX - 1)])
    pieces = gather_tp(tokens)
    tail = lax.all_gather(before, "tp", axis=0, tiled=False)

    filt = lax.all_to_all(filters.reshape(CTX, 1, -1), "ctx", 0, 0, tiled=True)
    table = toeplitz(filt.reshape(128, 128).astype(F32))

    mixed, blocks = project(
        pieces,
        tail,
        kv_mine,
        kv_other,
        taps[1:],
        [
            jax.ShapeDtypeStruct((rows, chan), BF16),
            jax.ShapeDtypeStruct((CTX, 32, 256), BF16),
        ],
    )
    sent = lax.all_to_all(blocks, "ctx", 0, 0, tiled=True)

    q_mine, q_other = gather_weights(w_in[0])
    (query,) = project(
        pieces, tail, q_mine, q_other, taps[:1], [jax.ShapeDtypeStruct((rows, chan), F32)]
    )

    result = conv(sent.reshape(CTX * 32, 256), table)
    back = lax.all_to_all(result.reshape(CTX, 32, 256), "ctx", 0, 0, tiled=True)
    gated = gate(back, mixed, query, skip[None, :])

    route = []
    for z in range(NZ):
        for r in range(4):
            for j in range(TP):
                route.append(((4 * z + r) * TP + j, (4 * j + r) * TP + z))
    turned = lax.ppermute(w_out, ("ctx", "tp"), route)
    o_mine, o_other = gather_weights(turned)
    return output(gather_tp(gated), o_mine, o_other)


def solution(mesh):
    return jax.shard_map(
        local,
        mesh=mesh,
        in_specs=(
            P("ctx", "tp"),
            P(None, "ctx", "tp"),
            P(None, "tp", None),
            P("tp", "ctx"),
            P("tp"),
            P("tp", "ctx"),
        ),
        out_specs=P("ctx", "tp"),
        check_vma=False,
    )
```

time: 660 us -> 309 us (0.47); the launches traced: 649 us -> 308 us
  waiting for transfers between devices: 369 us -> 130 us
  other arithmetic: 96.9 us -> 4.86 us
  local copies, waits for them, and re-layouts: 76.2 us -> 7.25 us
  starting transfers between devices: 21.9 us -> 72.6 us
  matrix products: 48.4 us -> 0 us
  Pallas kernels: 0 us -> 45.2 us
  blocking collectives: 22.8 us -> 34.4 us
    all_gather x5 -> x3, waiting for transfers between devices: 264 us -> 52 us  [gather_z(): lax.all_gather(block, 'ctx', axis=0, tiled=False, axis_index_groups=groups)]
    unnamed x1 -> x0, other arithmetic: 90.7 us -> none
    reduce_scatter x1 -> x0, waiting for transfers between devices: 85.8 us -> none  [local(): lax.psum_scatter(partial_out.astype(jnp.bfloat16), 'tp', scatter_dimensio...]
    ppermute x1 -> x22, waiting for transfers between devices: 2.78 us -> 62.6 us  [the longest x12 32.9 us: shift_x(): return lax.ppermute(block, 'tp', route)]
    ppermute x1 -> x22, starting transfers between devices: 2.14 us -> 52.9 us  [the longest x12 28.3 us: shift_x(): return lax.ppermute(block, 'tp', route)]
    dot_general x16 -> x0, matrix products: 48.4 us -> none  [the longest x3 17.4 us: local(): lax.dot_general(lax.all_gather(w_in[picked_entry_place], 'ctx', axis=0, t...]
    pallas_call x0 -> x6, Pallas kernels: none -> 45.2 us  [the longest x2 15.9 us: project(): pl.pallas_call(functools.partial(project_kernel, n_proj, width), out_shap...]
    all_gather x0 -> x1, blocking collectives: none -> 34.4 us  [local(): tail = lax.all_gather(before, 'tp', axis=0, tiled=False)]
  transfers between devices with their start and end apart: 9 -> 28, of which waited for: 7 -> 12; matrix products, arithmetic and copies ran while one was open for 33% -> 2% of each run, Pallas kernels for 0% -> 13%
where the time goes in v1:
time: 309 us; the launch traced here: 308 us
  waiting for transfers between devices  130 us (42%)
  starting transfers between devices  72.6 us (23%)
  Pallas kernels  45.2 us (15%)
  blocking collectives  34.4 us (11%)
  between operations  13.4 us (4%)
  local copies, waits for them, and re-layouts  7.25 us (2%)
  other arithmetic  4.86 us (2%)
    all_gather x3, waiting for transfers between devices, gather_z(): lax.all_gather(block, 'ctx', axis=0, tiled=False, axis_index_groups=groups)  52 us
    all_gather x1, blocking collectives, local(): tail = lax.all_gather(before, 'tp', axis=0, tiled=False)  34.4 us
    ppermute x12, waiting for transfers between devices, shift_x(): return lax.ppermute(block, 'tp', route)  32.9 us
    ppermute x12, starting transfers between devices, shift_x(): return lax.ppermute(block, 'tp', route)  28.3 us
    ppermute x2, starting transfers between devices, swap_yhi(): return lax.ppermute(block, 'tp', [(j, j ^ 1) for j in range(TP)])  18 us
    pallas_call x2, Pallas kernels, project(): pl.pallas_call(functools.partial(project_kernel, n_proj, width), out_shap...  15.9 us
    ppermute x6, waiting for transfers between devices, swap_ctx(): return lax.ppermute(block, 'ctx', [(i, i ^ mask) for i in range(CTX)])  15.7 us
    ppermute x2, waiting for transfers between devices, swap_yhi(): return lax.ppermute(block, 'tp', [(j, j ^ 1) for j in range(TP)])  14 us
  transfers between devices with their start and end apart: 28, of which 12 were waited for; matrix products, arithmetic and copies ran while one was open for 2% of the time, Pallas kernels for 13%

profile of v1, /device:TPU:8, one launch (start us, length us, event | category | flops | bytes accessed | tf_op | source)
XLA Modules:
  0.0 308.0 jit_solution(10416828898397555754)
XLA Ops:
  10.0 5.9 %collective-permute-done.8 = bf16[128,1024]{1,0:T(8,128)(2,1)S(1)} collective-permute-done((bf16[128,1024]{1,0:T(8,128)(2,1)S(1)}, bf16[128,1024]{1,0:T(8,128)(2,1)S(1)}, u32[]{:S(2)}, u32[]{:S(2)}) %collective-permute-start.8) | collective-permute-done | bytes 262176 | tf_op jit(solution)/shard_map/ppermute | solution.py:32
  17.4 4.5 %collective-permute-done.10 = bf16[128,512]{1,0:T(8,128)(2,1)S(1)} collective-permute-done((bf16[128,512]{1,0:T(8,128)(2,1)S(1)}, bf16[128,512]{1,0:T(8,128)(2,1)S(1)}, u32[]{:S(2)}, u32[]{:S(2)}) %collective-permute-start.10) | collective-permute-done | bytes 131104 | tf_op jit(solution)/shard_map/ppermute | solution.py:32
  22.6 51.9 %all-gather.8.cloned.1.call-done = bf16[16,128,1024]{2,1,0:T(8,128)(2,1)} async-done(((bf16[2,128,1024]{2,1,0:T(8,128)(2,1)}), bf16[16,128,1024]{2,1,0:T(8,128)(2,1)}) %all-gather.8.cloned.1.call-update) | async-done | bytes 4194320 | tf_op jit(solution)/shard_map/all_gather | solution.py:54
  75.9 5.4 %collective-permute-done.20 = bf16[512,128]{1,0:T(8,128)(2,1)S(1)} collective-permute-done((bf16[512,128]{1,0:T(8,128)(2,1)S(1)}, bf16[512,128]{1,0:T(8,128)(2,1)S(1)}, u32[]{:S(2)}, u32[]{:S(2)}) %collective-permute-start.20) | collective-permute-done | bytes 131104 | tf_op jit(solution)/shard_map/ppermute | solution.py:32
  82.0 17.9 %collective-permute-start = (bf16[512,512]{1,0:T(8,128)(2,1)S(1)}, bf16[512,512]{1,0:T(8,128)(2,1)S(1)}, u32[]{:S(2)}, u32[]{:S(2)}) collective-permute-start(bf16[512,512]{1,0:T(8,128)(2,1)S(1)} %copy-done), channel_id=1, source_target_pairs={{0,1},{1,0},{2,3},{3,2},{4,5},{5,4},{6,7},{7,6},{8,9},{9,8},{10,11... | collective-permute-start | bytes 1572872 | tf_op jit(solution)/shard_map/ppermute | solution.py:49
  99.9 8.9 %collective-permute-start.2 = (bf16[512,512]{1,0:T(8,128)(2,1)S(1)}, bf16[512,512]{1,0:T(8,128)(2,1)S(1)}, u32[]{:S(2)}, u32[]{:S(2)}) collective-permute-start(bf16[512,512]{1,0:T(8,128)(2,1)S(1)} %copy-done), channel_id=1, source_target_pairs={{0,6},{1,7},{2,0},{3,1},{4,2},{5,3},{6,4},{7,5},{8,14},{9,15},{10,... | collective-permute-start | bytes 1572872 | tf_op jit(solution)/shard_map/ppermute | solution.py:45
  110.6 9.6 %collective-permute-start.4 = (bf16[512,512]{1,0:T(8,128)(2,1)S(1)}, bf16[512,512]{1,0:T(8,128)(2,1)S(1)}, u32[]{:S(2)}, u32[]{:S(2)}) collective-permute-start(bf16[512,512]{1,0:T(8,128)(2,1)S(1)} %collective-permute-done.refs_1_), channel_id=1, source_target_pairs={{0,6},{1,7},{2,0},{3,1},{4,2},{5,3},{6,4},{7,5},{8,14},{9,15},{10,... | collective-permute-start | bytes 1572872 | tf_op jit(solution)/shard_map/ppermute | solution.py:45
  120.2 10.9 %collective-permute-done.3.refs_4_ = bf16[512,512]{1,0:T(8,128)(2,1)S(1)} collective-permute-done((bf16[512,512]{1,0:T(8,128)(2,1)S(1)}, bf16[512,512]{1,0:T(8,128)(2,1)S(1)}, u32[]{:S(2)}, u32[]{:S(2)}) %collective-permute-start.3) | collective-permute-done | bytes 524320 | tf_op jit(solution)/shard_map/ppermute | solution.py:45
  132.8 3.2 %collective-permute-start.6 = (bf16[512,512]{1,0:T(8,128)(2,1)}, bf16[512,512]{1,0:T(8,128)(2,1)}, u32[]{:S(2)}, u32[]{:S(2)}) collective-permute-start(bf16[512,512]{1,0:T(8,128)(2,1)} %pad_maximum_fusion.1), channel_id=1, source_target_pairs={{0,6},{1,7},{2,0},{3,1},{4,2},{5,3},{6,4},{7,5},{8,14},{9,15},{10,... | collective-permute-start | bytes 1572872 | tf_op jit(solution)/shard_map/ppermute | solution.py:45
  140.0 6.6 %all-to-all-start.1 = ((bf16[32,2,256]{2,1,0:T(2,128)(2,1)}), bf16[32,2,256]{2,1,0:T(2,128)(2,1)S(1)}, u32[]{:S(2)}, u32[]{:S(2)}) async-start(bf16[32,2,256]{2,1,0:T(2,128)(2,1)} %reshape.24), calls=%async_computation.1 | async-start | bytes 65536 | tf_op jit(solution)/shard_map/all_to_all | solution.py:341
  146.7 34.4 %all-gather = bf16[128,512]{1,0:T(8,128)(2,1)S(1)} all-gather(bf16[16,512]{1,0:T(8,128)(2,1)S(1)} %collective-permute-done.7), channel_id=2, replica_groups=mesh['ctx'=32,'tp'=8] {'tp'}, dimensions={0}, use_global_device_ids=true | all-gather | bytes 147456 | tf_op jit(solution)/shard_map/all_gather | solution.py:339
  181.1 8.6 %project2.1 = (bf16[512,512]{1,0:T(8,128)(2,1)S(1)}, bf16[32,32,256]{2,1,0:T(8,128)(2,1)S(1)}) custom-call(bf16[512,512]{1,0:T(8,128)(2,1)S(1)} %copy-done, bf16[512,512]{1,0:T(8,128)(2,1)S(1)} %collective-permute-done.refs_1_, bf16[512,512]{1,0:T(8,128)(2,1)S(1)} %collective-permute-done.1.refs_2_, bf16[512,512]{1,0:T(8,128)(2,1)S(1)} %collective-permute-done.2.refs_3_, ...), custom_call_target="tpu_custom_call" | custom-call | tf_op jit(solution)/shard_map/project2/pallas_call | solution.py:164
  191.3 8.3 %all-to-all-start = ((bf16[32,32,256]{2,1,0:T(8,128)(2,1)}), bf16[32,32,256]{2,1,0:T(8,128)(2,1)S(1)}, u32[]{:S(2)}, u32[]{:S(2)}) async-start(bf16[32,32,256]{2,1,0:T(8,128)(2,1)} %copy-done.4), calls=%async_computation | async-start | bytes 1048576 | tf_op jit(solution)/shard_map/all_to_all | solution.py:355
  199.7 9.9 %toeplitz.1 = bf16[64,256,256]{2,1,0:T(8,128)(2,1)} custom-call(f32[128,128]{1,0:T(8,128)S(1)} %bitcast.26), custom_call_target="tpu_custom_call" | custom-call | tf_op jit(solution)/shard_map/toeplitz/pallas_call | solution.py:211
  209.6 7.7 %all-to-all-done = bf16[32,32,256]{2,1,0:T(8,128)(2,1)S(1)} async-done(((bf16[32,32,256]{2,1,0:T(8,128)(2,1)}), bf16[32,32,256]{2,1,0:T(8,128)(2,1)S(1)}, u32[]{:S(2)}, u32[]{:S(2)}) %all-to-all-start) | async-done | bytes 524320 | tf_op jit(solution)/shard_map/all_to_all | solution.py:355
  217.3 12.2 %conv.1 = bf16[1024,256]{1,0:T(8,128)(2,1)} custom-call(bf16[1024,256]{1,0:T(8,128)(2,1)S(1)} %bitcast.23, bf16[16,1024,256]{2,1,0:T(8,128)(2,1)} %bitcast.28), custom_call_target="tpu_custom_call" | custom-call | tf_op jit(solution)/shard_map/conv/pallas_call | solution.py:248
  229.6 4.8 %all-to-all-start.2 = ((bf16[32,32,256]{2,1,0:T(8,128)(2,1)}), bf16[32,32,256]{2,1,0:T(8,128)(2,1)}, u32[]{:S(2)}, u32[]{:S(2)}) async-start(bf16[32,32,256]{2,1,0:T(8,128)(2,1)} %bitcast.11), calls=%async_computation.2 | async-start | bytes 1048576 | tf_op jit(solution)/shard_map/all_to_all | solution.py:363
  236.9 7.3 %project1.1.query_ref = f32[512,512]{1,0:T(8,128)S(1)} custom-call(bf16[512,512]{1,0:T(8,128)(2,1)S(1)} %copy-done.1, bf16[512,512]{1,0:T(8,128)(2,1)S(1)} %copy-done.3, bf16[512,512]{1,0:T(8,128)(2,1)S(1)} %collective-permute-done.1.refs_2_, bf16[512,512]{1,0:T(8,128)(2,1)S(1)} %collective-permute-done.2.refs_3_, ...), custom_call_target="tpu_custom_call" | custom-call | tf_op jit(solution)/shard_map/project1/pallas_call | solution.py:164
  244.2 8.0 %all-to-all-done.2.back_ref = bf16[32,32,256]{2,1,0:T(8,128)(2,1)} async-done(((bf16[32,32,256]{2,1,0:T(8,128)(2,1)}), bf16[32,32,256]{2,1,0:T(8,128)(2,1)}, u32[]{:S(2)}, u32[]{:S(2)}) %all-to-all-start.2) | async-done | bytes 524320 | tf_op jit(solution)/shard_map/all_to_all | solution.py:363
  256.9 12.3 %collective-permute-done.12.refs_1_ = bf16[512,512]{1,0:T(8,128)(2,1)S(1)} collective-permute-done((bf16[512,512]{1,0:T(8,128)(2,1)S(1)}, bf16[512,512]{1,0:T(8,128)(2,1)S(1)}, u32[]{:S(2)}, u32[]{:S(2)}) %collective-permute-start.12) | collective-permute-done | bytes 524320 | tf_op jit(solution)/shard_map/ppermute | solution.py:49
  271.3 10.1 %collective-permute-done.16.refs_5_ = bf16[512,512]{1,0:T(8,128)(2,1)S(1)} collective-permute-done((bf16[512,512]{1,0:T(8,128)(2,1)S(1)}, bf16[512,512]{1,0:T(8,128)(2,1)S(1)}, u32[]{:S(2)}, u32[]{:S(2)}) %collective-permute-start.16) | collective-permute-done | bytes 524320 | tf_op jit(solution)/shard_map/ppermute | solution.py:45
  283.7 9.1 %collective-permute-done.18.refs_7_ = bf16[512,512]{1,0:T(8,128)(2,1)S(1)} collective-permute-done((bf16[512,512]{1,0:T(8,128)(2,1)S(1)}, bf16[512,512]{1,0:T(8,128)(2,1)S(1)}, u32[]{:S(2)}, u32[]{:S(2)}) %collective-permute-start.18) | collective-permute-done | bytes 524320 | tf_op jit(solution)/shard_map/ppermute | solution.py:45
  292.8 2.8 collective-permute-done.17.refs_6_
  295.6 5.9 %output.1 = bf16[512,512]{1,0:T(8,128)(2,1)} custom-call(bf16[512,512]{1,0:T(8,128)(2,1)S(1)} %gate.1.refs_0_, bf16[512,512]{1,0:T(8,128)(2,1)S(1)} %collective-permute-done.12.refs_1_, bf16[512,512]{1,0:T(8,128)(2,1)S(1)} %collective-permute-done.13.refs_2_, bf16[512,512]{1,0:T(8,128)(2,1)S(1)} %collective-permute-done.14.refs_3_, ...), custom_call_target="tpu_custom_call" | custom-call | tf_op jit(solution)/shard_map/output/pallas_call | solution.py:307
  (89 shorter events, 28.6 us)
Async XLA Ops:
  6.5 68.0 %all-gather.8.cloned.1.call-start = ((), (), s32[]{:S(2)}) async-start(), calls=%async_computation.3 | async-start | bytes 4718592 | tf_op jit(solution)/shard_map/all_gather | solution.py:54
  16.7 121.3 %all-gather.10.cloned.1.call-start = ((), (), s32[]{:S(2)}) async-start(), calls=%async_computation.4 | async-start | bytes 2359296 | tf_op jit(solution)/shard_map/all_gather | solution.py:54
  22.6 211.8 %all-gather.12.cloned.1.call-start = ((), (), s32[]{:S(2)}) async-start(), calls=%async_computation.5 | async-start | bytes 2359296 | tf_op jit(solution)/shard_map/all_gather | solution.py:54
  74.6 106.5 %collective-permute-start.9 = (bf16[8,2,128,1024]{3,2,1,0:T(8,128)(2,1)}, bf16[8,2,128,1024]{3,2,1,0:T(8,128)(2,1)}, u32[]{:S(2)}, u32[]{:S(2)}) collective-permute-start(bf16[8,2,128,1024]{3,2,1,0:T(8,128)(2,1)} %bitcast.29), channel_id=1, source_target_pairs={{0,8},{8,0},{16,24},{24,16},{32,40},{40,32},{48,56},{56,48},{64,72... | collective-permute-start | bytes 12582920 | tf_op jit(solution)/shard_map/ppermute | solution.py:32
  82.0 28.5 %collective-permute-start = (bf16[512,512]{1,0:T(8,128)(2,1)S(1)}, bf16[512,512]{1,0:T(8,128)(2,1)S(1)}, u32[]{:S(2)}, u32[]{:S(2)}) collective-permute-start(bf16[512,512]{1,0:T(8,128)(2,1)S(1)} %copy-done), channel_id=1, source_target_pairs={{0,1},{1,0},{2,3},{3,2},{4,5},{5,4},{6,7},{7,6},{8,9},{9,8},{10,11... | collective-permute-start | bytes 1572872 | tf_op jit(solution)/shard_map/ppermute | solution.py:49
  99.9 20.2 %collective-permute-start.1 = (bf16[512,512]{1,0:T(8,128)(2,1)S(1)}, bf16[512,512]{1,0:T(8,128)(2,1)S(1)}, u32[]{:S(2)}, u32[]{:S(2)}) collective-permute-start(bf16[512,512]{1,0:T(8,128)(2,1)S(1)} %copy-done), channel_id=1, source_target_pairs={{0,2},{1,3},{2,4},{3,5},{4,6},{5,7},{6,0},{7,1},{8,10},{9,11},{10,... | collective-permute-start | bytes 1572872 | tf_op jit(solution)/shard_map/ppermute | solution.py:45
  99.9 20.3 %collective-permute-start.2 = (bf16[512,512]{1,0:T(8,128)(2,1)S(1)}, bf16[512,512]{1,0:T(8,128)(2,1)S(1)}, u32[]{:S(2)}, u32[]{:S(2)}) collective-permute-start(bf16[512,512]{1,0:T(8,128)(2,1)S(1)} %copy-done), channel_id=1, source_target_pairs={{0,6},{1,7},{2,0},{3,1},{4,2},{5,3},{6,4},{7,5},{8,14},{9,15},{10,... | collective-permute-start | bytes 1572872 | tf_op jit(solution)/shard_map/ppermute | solution.py:45
  110.5 20.5 %collective-permute-start.3 = (bf16[512,512]{1,0:T(8,128)(2,1)S(1)}, bf16[512,512]{1,0:T(8,128)(2,1)S(1)}, u32[]{:S(2)}, u32[]{:S(2)}) collective-permute-start(bf16[512,512]{1,0:T(8,128)(2,1)S(1)} %collective-permute-done.refs_1_), channel_id=1, source_target_pairs={{0,2},{1,3},{2,4},{3,5},{4,6},{5,7},{6,0},{7,1},{8,10},{9,11},{10,... | collective-permute-start | bytes 1572872 | tf_op jit(solution)/shard_map/ppermute | solution.py:45
  110.6 21.4 %collective-permute-start.4 = (bf16[512,512]{1,0:T(8,128)(2,1)S(1)}, bf16[512,512]{1,0:T(8,128)(2,1)S(1)}, u32[]{:S(2)}, u32[]{:S(2)}) collective-permute-start(bf16[512,512]{1,0:T(8,128)(2,1)S(1)} %collective-permute-done.refs_1_), channel_id=1, source_target_pairs={{0,6},{1,7},{2,0},{3,1},{4,2},{5,3},{6,4},{7,5},{8,14},{9,15},{10,... | collective-permute-start | bytes 1572872 | tf_op jit(solution)/shard_map/ppermute | solution.py:45
  131.9 49.1 %collective-permute-start.5 = (bf16[512,512]{1,0:T(8,128)(2,1)}, bf16[512,512]{1,0:T(8,128)(2,1)}, u32[]{:S(2)}, u32[]{:S(2)}) collective-permute-start(bf16[512,512]{1,0:T(8,128)(2,1)} %pad_maximum_fusion), channel_id=1, source_target_pairs={{0,2},{1,3},{2,4},{3,5},{4,6},{5,7},{6,0},{7,1},{8,10},{9,11},{10,... | collective-permute-start | bytes 1572872 | tf_op jit(solution)/shard_map/ppermute | solution.py:45
  132.8 48.2 %collective-permute-start.6 = (bf16[512,512]{1,0:T(8,128)(2,1)}, bf16[512,512]{1,0:T(8,128)(2,1)}, u32[]{:S(2)}, u32[]{:S(2)}) collective-permute-start(bf16[512,512]{1,0:T(8,128)(2,1)} %pad_maximum_fusion.1), channel_id=1, source_target_pairs={{0,6},{1,7},{2,0},{3,1},{4,2},{5,3},{6,4},{7,5},{8,14},{9,15},{10,... | collective-permute-start | bytes 1572872 | tf_op jit(solution)/shard_map/ppermute | solution.py:45
  136.1 10.6 %collective-permute-start.7 = (bf16[16,512]{1,0:T(8,128)(2,1)S(1)}, bf16[16,512]{1,0:T(8,128)(2,1)S(1)}, u32[]{:S(2)}, u32[]{:S(2)}) collective-permute-start(bf16[16,512]{1,0:T(8,128)(2,1)S(1)} %slice.46), channel_id=1, source_target_pairs={{0,8},{8,16},{16,24},{24,32},{32,40},{40,48},{48,56},{56,64},{64,7... | collective-permute-start | bytes 49160 | tf_op jit(solution)/shard_map/ppermute | solution.py:337
  138.0 96.8 %collective-permute-start.11 = (bf16[8,2,128,512]{3,2,1,0:T(8,128)(2,1)}, bf16[8,2,128,512]{3,2,1,0:T(8,128)(2,1)}, u32[]{:S(2)}, u32[]{:S(2)}) collective-permute-start(bf16[8,2,128,512]{3,2,1,0:T(8,128)(2,1)} %bitcast.33), channel_id=1, source_target_pairs={{0,8},{8,0},{16,24},{24,16},{32,40},{40,32},{48,56},{56,48},{64,72... | collective-permute-start | bytes 6291464 | tf_op jit(solution)/shard_map/ppermute | solution.py:32
  140.0 51.3 %all-to-all-start.1 = ((bf16[32,2,256]{2,1,0:T(2,128)(2,1)}), bf16[32,2,256]{2,1,0:T(2,128)(2,1)S(1)}, u32[]{:S(2)}, u32[]{:S(2)}) async-start(bf16[32,2,256]{2,1,0:T(2,128)(2,1)} %reshape.24), calls=%async_computation.1 | async-start | bytes 65536 | tf_op jit(solution)/shard_map/all_to_all | solution.py:341
  191.3 26.0 %all-to-all-start = ((bf16[32,32,256]{2,1,0:T(8,128)(2,1)}), bf16[32,32,256]{2,1,0:T(8,128)(2,1)S(1)}, u32[]{:S(2)}, u32[]{:S(2)}) async-start(bf16[32,32,256]{2,1,0:T(8,128)(2,1)} %copy-done.4), calls=%async_computation | async-start | bytes 1048576 | tf_op jit(solution)/shard_map/all_to_all | solution.py:355
  229.6 22.6 %all-to-all-start.2 = ((bf16[32,32,256]{2,1,0:T(8,128)(2,1)}), bf16[32,32,256]{2,1,0:T(8,128)(2,1)}, u32[]{:S(2)}, u32[]{:S(2)}) async-start(bf16[32,32,256]{2,1,0:T(8,128)(2,1)} %bitcast.11), calls=%async_computation.2 | async-start | bytes 1048576 | tf_op jit(solution)/shard_map/all_to_all | solution.py:363
  234.4 49.3 %collective-permute-start.21 = (bf16[8,2,512,128]{3,2,1,0:T(8,128)(2,1)}, bf16[8,2,512,128]{3,2,1,0:T(8,128)(2,1)}, u32[]{:S(2)}, u32[]{:S(2)}) collective-permute-start(bf16[8,2,512,128]{3,2,1,0:T(8,128)(2,1)} %bitcast.31), channel_id=1, source_target_pairs={{0,8},{8,0},{16,24},{24,16},{32,40},{40,32},{48,56},{56,48},{64,72... | collective-permute-start | bytes 6291464 | tf_op jit(solution)/shard_map/ppermute | solution.py:32
  254.5 14.7 %collective-permute-start.12 = (bf16[512,512]{1,0:T(8,128)(2,1)S(1)}, bf16[512,512]{1,0:T(8,128)(2,1)S(1)}, u32[]{:S(2)}, u32[]{:S(2)}) collective-permute-start(bf16[512,512]{1,0:T(8,128)(2,1)S(1)} %gate.1.refs_0_), channel_id=1, source_target_pairs={{0,1},{1,0},{2,3},{3,2},{4,5},{5,4},{6,7},{7,6},{8,9},{9,8},{10,11... | collective-permute-start | bytes 1572872 | tf_op jit(solution)/shard_map/ppermute | solution.py:49
  254.6 16.6 %collective-permute-start.14 = (bf16[512,512]{1,0:T(8,128)(2,1)S(1)}, bf16[512,512]{1,0:T(8,128)(2,1)S(1)}, u32[]{:S(2)}, u32[]{:S(2)}) collective-permute-start(bf16[512,512]{1,0:T(8,128)(2,1)S(1)} %gate.1.refs_0_), channel_id=1, source_target_pairs={{0,6},{1,7},{2,0},{3,1},{4,2},{5,3},{6,4},{7,5},{8,14},{9,15},{10,... | collective-permute-start | bytes 1572872 | tf_op jit(solution)/shard_map/ppermute | solution.py:45
  256.9 14.3 %collective-permute-start.13 = (bf16[512,512]{1,0:T(8,128)(2,1)S(1)}, bf16[512,512]{1,0:T(8,128)(2,1)S(1)}, u32[]{:S(2)}, u32[]{:S(2)}) collective-permute-start(bf16[512,512]{1,0:T(8,128)(2,1)S(1)} %gate.1.refs_0_), channel_id=1, source_target_pairs={{0,2},{1,3},{2,4},{3,5},{4,6},{5,7},{6,0},{7,1},{8,10},{9,11},{10,... | collective-permute-start | bytes 1572872 | tf_op jit(solution)/shard_map/ppermute | solution.py:45
  269.2 12.2 %collective-permute-start.16 = (bf16[512,512]{1,0:T(8,128)(2,1)S(1)}, bf16[512,512]{1,0:T(8,128)(2,1)S(1)}, u32[]{:S(2)}, u32[]{:S(2)}) collective-permute-start(bf16[512,512]{1,0:T(8,128)(2,1)S(1)} %collective-permute-done.12.refs_1_), channel_id=1, source_target_pairs={{0,6},{1,7},{2,0},{3,1},{4,2},{5,3},{6,4},{7,5},{8,14},{9,15},{10,... | collective-permute-start | bytes 1572872 | tf_op jit(solution)/shard_map/ppermute | solution.py:45
  269.8 13.5 %collective-permute-start.15 = (bf16[512,512]{1,0:T(8,128)(2,1)S(1)}, bf16[512,512]{1,0:T(8,128)(2,1)S(1)}, u32[]{:S(2)}, u32[]{:S(2)}) collective-permute-start(bf16[512,512]{1,0:T(8,128)(2,1)S(1)} %collective-permute-done.12.refs_1_), channel_id=1, source_target_pairs={{0,2},{1,3},{2,4},{3,5},{4,6},{5,7},{6,0},{7,1},{8,10},{9,11},{10,... | collective-permute-start | bytes 1572872 | tf_op jit(solution)/shard_map/ppermute | solution.py:45
  281.4 11.3 %collective-permute-start.18 = (bf16[512,512]{1,0:T(8,128)(2,1)S(1)}, bf16[512,512]{1,0:T(8,128)(2,1)S(1)}, u32[]{:S(2)}, u32[]{:S(2)}) collective-permute-start(bf16[512,512]{1,0:T(8,128)(2,1)S(1)} %pad_maximum_fusion.4), channel_id=1, source_target_pairs={{0,6},{1,7},{2,0},{3,1},{4,2},{5,3},{6,4},{7,5},{8,14},{9,15},{10,... | collective-permute-start | bytes 1572872 | tf_op jit(solution)/shard_map/ppermute | solution.py:45
  283.4 12.3 %collective-permute-start.17 = (bf16[512,512]{1,0:T(8,128)(2,1)S(1)}, bf16[512,512]{1,0:T(8,128)(2,1)S(1)}, u32[]{:S(2)}, u32[]{:S(2)}) collective-permute-start(bf16[512,512]{1,0:T(8,128)(2,1)S(1)} %pad_maximum_fusion.3), channel_id=1, source_target_pairs={{0,2},{1,3},{2,4},{3,5},{4,6},{5,7},{6,0},{7,1},{8,10},{9,11},{10,... | collective-permute-start | bytes 1572872 | tf_op jit(solution)/shard_map/ppermute | solution.py:45
  (15 other events, 374.0 us)
Sparse Core Ops, SparseCore 0:
  16.8 57.6 all-gather.7
  76.4 43.7 all-gather.9
  122.0 37.6 all-gather.11

commit v2 on v1

--- a/solution.py
+++ b/solution.py
@@ -9,9 +9,9 @@
 
 F32 = jnp.float32
 BF16 = jnp.bfloat16
-ANY = pl.BlockSpec(memory_space=pl.ANY)
+HBM = pl.BlockSpec(memory_space=pltpu.HBM)
 VMEM = pl.BlockSpec(memory_space=pltpu.VMEM)
-VMEM_LIMIT = 48 * 1024 * 1024
+MIB = 1024 * 1024
 
 NZ, NX = 8, 4
 CTX = NZ * 4
@@ -55,8 +55,7 @@
 
 
 def gather_tp(own):
-    rows = own.shape[0]
-    half = rows // 2
+    half = own.shape[0] // 2
     near = swap_yhi(own)
     own_right, own_left = shift_x(own, 1), shift_x(own, -1)
     near_right, near_left = shift_x(near, 1), shift_x(near, -1)
@@ -89,25 +88,77 @@
 
 def weight_slots():
     me = lax.axis_index("ctx")
-    return (me // 2) % 2, me % 2
-
-
-def project_kernel(n_proj, width, *refs):
+    return me // 4, (me // 2) % 2, me % 2
+
+
+def weight_copies(weights, wts, lanes):
+    z, y, core = weight_slots()
+    copies = []
+    for dc, ref in enumerate(weights):
+        for dy in (0, 1):
+            slot = ((y + dy) % 2) * 2 + (core + dc) % 2
+            src = ref.at[:, dy, pl.ds(0, wts.shape[2]), lanes]
+            copies.append((src, wts.at[:, slot, :, lanes]))
+    return copies
+
+
+def pack_kernel(moves, *refs):
+    *sources, out, sem = refs
+    copies = [
+        pltpu.make_async_copy(sources[k].at[src], out.at[dst], sem) for k, src, dst in moves
+    ]
+    for copy in copies:
+        copy.start()
+    for copy in copies:
+        copy.wait()
+
+
+def pack(sources, shape, moves, name):
+    return pl.pallas_call(
+        functools.partial(pack_kernel, moves),
+        out_shape=jax.ShapeDtypeStruct(shape, sources[0].dtype),
+        in_specs=[HBM] * len(sources),
+        out_specs=VMEM,
+        scratch_shapes=[pltpu.SemaphoreType.DMA],
+        compiler_params=pltpu.CompilerParams(vmem_limit_bytes=8 * MIB),
+        name=name,
+    )(*sources)
+
+
+def last_rows(pieces):
+    rows, width = pieces[0].shape
+    half = rows // 2
+    moves = [(k, (pl.ds(rows - TAIL, TAIL),), (k,)) for k in range(6)]
+    moves.append((6, (pl.ds(half - TAIL, TAIL),), (6,)))
+    moves.append((6, (pl.ds(rows - TAIL, TAIL),), (7,)))
+    return pack([*pieces[:6], pieces[7]], (TP, TAIL, width), moves, "tail")
+
+
+def tail_places(tail, dst):
+    me = lax.axis_index("tp")
+    x, y = me // 2, me % 2
+    width = tail.shape[2]
+    offsets = [(0, 0), (0, 1), (-1, 0), (1, 0), (-1, 1), (1, 1), (2, 0), (2, 1)]
+    places = []
+    for k, (dx, dy) in enumerate(offsets):
+        there = ((x + dx + NX) % NX) * 2 + (y + dy) % 2
+        lanes = pl.ds(pl.multiple_of(there * width, width), width)
+        places.append((tail.at[k], dst.at[pl.ds(0, TAIL), lanes]))
+    return places
+
+
+def project_kernel(n_proj, n_out, width, *refs):
     pieces = refs[:8]
-    tail, mine, other, taps = refs[8:12]
-    outs = refs[12:-6]
+    tail, *weights, taps = refs[8:-6 - n_out]
+    outs = refs[-6 - n_out : -6]
     tok, wts, part, tok_sem, tail_sem, w_sems = refs[-6:]
     rows = pieces[0].shape[0]
     total = wts.shape[3]
     chan = total // n_proj
     n_tiles = chan // width
-    y, core = weight_slots()
-
     copies = piece_copies(pieces, tok, TAIL, tok_sem)
-    for j in range(TP):
-        copies.append(
-            pltpu.make_async_copy(tail.at[j], tok.at[pl.ds(0, TAIL), pl.ds(j * 512, 512)], tail_sem)
-        )
+    for ref, to in tail_places(tail, tok):
+        copies.append(pltpu.make_async_copy(ref, to, tail_sem))
     for copy in copies:
         copy.start()
     w_copies = []
@@ -115,14 +166,8 @@
         group = []
         for proj in range(n_proj):
             lanes = pl.ds(proj * chan + tile * width, width)
-            for ref, dc in ((mine, 0), (other, 1)):
-                for dy in (0, 1):
-                    slot = ((y + dy) % 2) * 2 + (core + dc) % 2
-                    group.append(
-                        pltpu.make_async_copy(
-                            ref.at[:, dy, :, lanes], wts.at[:, slot, :, lanes], w_sems.at[tile]
-                        )
-                    )
+            for src, to in weight_copies(weights, wts, lanes):
+                group.append(pltpu.make_async_copy(src, to, w_sems.at[tile]))
         for copy in group:
             copy.start()
         w_copies.append(group)
@@ -154,17 +199,17 @@
                 outs[1][pl.ds(tile * (width // 16), width // 16), pl.ds(16 * a, 16), :] = block
 
 
-def project(pieces, tail, mine, other, taps, out_shapes):
+def project(pieces, tail, weights, taps, out_shapes):
     n_proj = taps.shape[0]
-    total = mine.shape[-1]
+    total = weights[0].shape[-1]
     width = 256
     n_tiles = total // n_proj // width
     rows = pieces[0].shape[0]
     depth = TP * pieces[0].shape[1]
     return pl.pallas_call(
-        functools.partial(project_kernel, n_proj, width),
+        functools.partial(project_kernel, n_proj, len(out_shapes), width),
         out_shape=out_shapes,
-        in_specs=[ANY] * 8 + [ANY, ANY, ANY, VMEM],
+        in_specs=[HBM] * (9 + len(weights)) + [VMEM],
         out_specs=[VMEM] * len(out_shapes),
         scratch_shapes=[
             pltpu.VMEM((TAIL + rows, depth), BF16),
@@ -174,12 +219,33 @@
             pltpu.SemaphoreType.DMA,
             pltpu.SemaphoreType.DMA((n_tiles,)),
         ],
-        compiler_params=pltpu.CompilerParams(vmem_limit_bytes=VMEM_LIMIT),
+        compiler_params=pltpu.CompilerParams(vmem_limit_bytes=60 * MIB),
         name="project%d" % n_proj,
-    )(*pieces, tail, mine, other, taps)
-
-
-def toeplitz_kernel(seg_ref, out_ref):
+    )(*pieces, tail, *weights, taps)
+
+
+def toeplitz_kernel(mine, other, out_hbm, out_ref, rows_ref, seg_ref, row_sem, sem):
+    _, y, core = weight_slots()
+    group = lax.axis_index("ctx")
+    width = rows_ref.shape[3]
+    lanes = pl.ds(pl.multiple_of(group // 16 * width, width), width)
+    filter_rows = pl.ds(mine.shape[2] - 16, 16)
+    copies = []
+    for dc, ref in enumerate((mine, other)):
+        for dy in (0, 1):
+            slot = ((y + dy) % 2) * 2 + (core + dc) % 2
+            src = ref.at[:, dy, filter_rows, lanes]
+            copies.append(pltpu.make_async_copy(src, rows_ref.at[:, slot], row_sem))
+    for copy in copies:
+        copy.start()
+    for copy in copies:
+        copy.wait()
+    chosen = lax.broadcasted_iota(jnp.int32, (16, width), 0) == group % 16
+    for k in range(CTX):
+        block = rows_ref[k // 4, k % 4].astype(F32)
+        row = jnp.sum(jnp.where(chosen, block, 0.0), axis=0, keepdims=True)
+        for q in range(4):
+            seg_ref[4 * k + q : 4 * k + q + 1, :] = row[:, 128 * q : 128 * q + 128]
     low = lax.broadcasted_iota(jnp.int32, (128, 128), 1) >= lax.broadcasted_iota(
         jnp.int32, (128, 128), 0
     )
@@ -191,31 +257,43 @@
     def body(d, before):
         even = turn(2 * d)
         odd = turn(2 * d + 1)
-        first = jnp.where(low, even, before).astype(BF16)
+        same = jnp.where(low, even, before).astype(BF16)
         second = jnp.where(low, odd, even).astype(BF16)
-        out_ref[d, 0:128, 0:128] = first
-        out_ref[d, 128:256, 128:256] = first
+        out_ref[d, 0:128, 0:128] = same
+        out_ref[d, 128:256, 128:256] = same
         out_ref[d, 0:128, 128:256] = second
-
-        @pl.when(d < 63)
-        def _():
-            out_ref[d + 1, 128:256, 0:128] = second
-
+        out_ref[d + 1, 128:256, 0:128] = second
         return odd
 
+    def copy_out(g):
+        here = pl.ds(g * 8, 8)
+        return pltpu.make_async_copy(out_ref.at[here], out_hbm.at[here], sem.at[g])
+
     out_ref[0, 128:256, 0:128] = jnp.zeros((128, 128), BF16)
-    lax.fori_loop(0, 64, body, jnp.zeros((128, 128), F32))
-
-
-def toeplitz(segments):
+    before = jnp.zeros((128, 128), F32)
+    for g in range(8):
+        before = lax.fori_loop(g * 8, g * 8 + 8, body, before)
+        copy_out(g).start()
+    for g in range(8):
+        copy_out(g).wait()
+
+
+def toeplitz(weights):
     return pl.pallas_call(
         toeplitz_kernel,
         out_shape=jax.ShapeDtypeStruct((64, 256, 256), BF16),
-        in_specs=[VMEM],
-        out_specs=VMEM,
-        compiler_params=pltpu.CompilerParams(vmem_limit_bytes=VMEM_LIMIT),
+        in_specs=[HBM] * 2,
+        out_specs=HBM,
+        scratch_shapes=[
+            pltpu.VMEM((65, 256, 256), BF16),
+            pltpu.VMEM((NZ, 4, 16, 512), BF16),
+            pltpu.VMEM((128, 128), F32),
+            pltpu.SemaphoreType.DMA,
+            pltpu.SemaphoreType.DMA((8,)),
+        ],
+        compiler_params=pltpu.CompilerParams(vmem_limit_bytes=60 * MIB),
         name="toeplitz",
-    )(segments)
+    )(*weights)
 
 
 FOLD = 4
@@ -248,7 +326,7 @@
     return pl.pallas_call(
         conv_kernel,
         out_shape=jax.ShapeDtypeStruct((rows, 256), BF16),
-        in_specs=[VMEM, ANY],
+        in_specs=[VMEM, HBM],
         out_specs=VMEM,
         scratch_shapes=[
             pltpu.VMEM((rows, FOLD * 256), BF16),
@@ -256,7 +334,7 @@
             pltpu.VMEM((steps, FOLD * 256, 256), BF16),
             pltpu.SemaphoreType.DMA((steps,)),
         ],
-        compiler_params=pltpu.CompilerParams(vmem_limit_bytes=VMEM_LIMIT),
+        compiler_params=pltpu.CompilerParams(vmem_limit_bytes=60 * MIB),
         name="conv",
     )(x, table.reshape(steps, FOLD * 256, 256))
 
@@ -277,7 +355,7 @@
         out_shape=jax.ShapeDtypeStruct(mixed.shape, BF16),
         in_specs=[VMEM] * 4,
         out_specs=VMEM,
-        compiler_params=pltpu.CompilerParams(vmem_limit_bytes=VMEM_LIMIT),
+        compiler_params=pltpu.CompilerParams(vmem_limit_bytes=8 * MIB),
         name="gate",
     )(back, mixed, query, skip)
 
@@ -285,7 +363,7 @@
 def output_kernel(*refs):
     pieces = refs[:8]
     mine, other, out_ref, act, wts, act_sem, w_sem = refs[8:]
-    y, core = weight_slots()
+    z, y, core = weight_slots()
     copies = piece_copies(pieces, act, 0, act_sem)
     depth, width = mine.shape[2:]
     for ref, dc in ((mine, 0), (other, 1)):
@@ -307,7 +385,7 @@
     return pl.pallas_call(
         output_kernel,
         out_shape=jax.ShapeDtypeStruct((rows, 4 * width), BF16),
-        in_specs=[ANY] * 10,
+        in_specs=[HBM] * 10,
         out_specs=VMEM,
         scratch_shapes=[
             pltpu.VMEM((rows, TP * part), BF16),
@@ -315,62 +393,70 @@
             pltpu.SemaphoreType.DMA,
             pltpu.SemaphoreType.DMA,
         ],
-        compiler_params=pltpu.CompilerParams(vmem_limit_bytes=VMEM_LIMIT),
+        compiler_params=pltpu.CompilerParams(vmem_limit_bytes=60 * MIB),
         name="output",
     )(*pieces, mine, other)
 
 
-def gather_weights(block):
-    pair = jnp.stack([block, swap_ylo(block)])
-    mine = gather_z(pair)
-    return mine, swap_core(mine)
+def pair_ylo(own):
+    return jnp.stack([own, swap_ylo(own)])
 
 
 def local(tokens, w_in, short_taps, filters, skip, w_out):
     rows, _ = tokens.shape
-    chan = w_in.shape[2]
+    depth, chan = w_in.shape[1:]
     taps = short_taps.transpose(0, 2, 1)
 
     kv = jnp.concatenate([w_in[1], w_in[2]], axis=1)
-    kv_mine, kv_other = gather_weights(kv)
-
-    before = lax.ppermute(tokens[rows - TAIL :], "ctx", [(i, i + 1) for i in range(CTX - 1)])
+    filt = jnp.concatenate([filters[:16], filters[16:]], axis=1)
+    kv_mine = gather_z(pair_ylo(jnp.concatenate([kv, filt])))
     pieces = gather_tp(tokens)
-    tail = lax.all_gather(before, "tp", axis=0, tiled=False)
-
-    filt = lax.all_to_all(filters.reshape(CTX, 1, -1), "ctx", 0, 0, tiled=True)
-    table = toeplitz(filt.reshape(128, 128).astype(F32))
-
+    tail = last_rows(pieces)
+    tail = lax.ppermute(tail, "ctx", [(i, i + 1) for i in range(CTX - 1)])
+
+    kv_mine, tail, *pieces = barrier(kv_mine, tail, *pieces)
+    w_in, w_out, kv_mine = barrier(w_in, w_out, kv_mine)
+    kv_other = swap_core(kv_mine)
+    q_pair = pair_ylo(w_in[0])
+    route = []
+    for z in range(NZ):
+        for r in range(4):
+            for j in range(TP):
+                route.append(((4 * z + r) * TP + j, (4 * j + r) * TP + z))
+    w_out = lax.ppermute(w_out, ("ctx", "tp"), route)
     mixed, blocks = project(
         pieces,
         tail,
-        kv_mine,
-        kv_other,
+        (kv_mine, kv_other),
         taps[1:],
         [
             jax.ShapeDtypeStruct((rows, chan), BF16),
             jax.ShapeDtypeStruct((CTX, 32, 256), BF16),
         ],
     )
+
+    q_pair, w_out, blocks = barrier(q_pair, w_out, blocks)
+    q_mine = gather_z(q_pair)
+    o_pair = pair_ylo(w_out)
     sent = lax.all_to_all(blocks, "ctx", 0, 0, tiled=True)
-
-    q_mine, q_other = gather_weights(w_in[0])
+    table = toeplitz((kv_mine, kv_other))
+    o_pair, sent, table = barrier(o_pair, sent, table)
+    result = conv(sent.reshape(CTX * 32, 256), table)
+    q_mine, result = barrier(q_mine, result)
+    back = lax.all_to_all(result.reshape(CTX, 32, 256), "ctx", 0, 0, tiled=True)
     (query,) = project(
-        pieces, tail, q_mine, q_other, taps[:1], [jax.ShapeDtypeStruct((rows, chan), F32)]
+        pieces,
+        tail,
+        (q_mine, swap_core(q_mine)),
+        taps[:1],
+        [jax.ShapeDtypeStruct((rows, chan), F32)],
     )
-
-    result = conv(sent.reshape(CTX * 32, 256), table)
-    back = lax.all_to_all(result.reshape(CTX, 32, 256), "ctx", 0, 0, tiled=True)
     gated = gate(back, mixed, query, skip[None, :])
 
-    route = []
-    for z in range(NZ):
-        for r in range(4):
-            for j in range(TP):
-                route.append(((4 * z + r) * TP + j, (4 * j + r) * TP + z))
-    turned = lax.ppermute(w_out, ("ctx", "tp"), route)
-    o_mine, o_other = gather_weights(turned)
-    return output(gather_tp(gated), o_mine, o_other)
+    o_pair, q_mine = barrier(o_pair, q_mine)
+    o_mine = gather_z(o_pair)
+    o_mine, *gathered = barrier(o_mine, *gather_tp(gated))
+    return output(gathered, o_mine, swap_core(o_mine))
 
 
 def solution(mesh):

time: 309 us -> 241 us (0.78)
  blocking collectives: 34.4 us -> 0 us
  starting transfers between devices: 72.6 us -> 44.3 us
  waiting for transfers between devices: 130 us -> 119 us
  Pallas kernels: 45.2 us -> 49.5 us
  local copies, waits for them, and re-layouts: 7.25 us -> 10.7 us
    all_gather x3, waiting for transfers between devices: 52 us -> 14.1 us  [gather_z(): lax.all_gather(block, 'ctx', axis=0, tiled=False, axis_index_groups=groups)]
    all_gather x1 -> x0, blocking collectives: 34.4 us -> none  [local(): tail = lax.all_gather(before, 'tp', axis=0, tiled=False)]
    ppermute x12, waiting for transfers between devices: 32.9 us -> 49.7 us  [shift_x(): return lax.ppermute(block, 'tp', route)]
    ppermute x2, starting transfers between devices: 18 us -> 5.4 us  [swap_yhi(): return lax.ppermute(block, 'tp', [(j, j ^ 1) for j in range(TP)])]
    ppermute x12, starting transfers between devices: 28.3 us -> 17.8 us  [shift_x(): return lax.ppermute(block, 'tp', route)]
    all_to_all x1 -> x0, starting transfers between devices: 6.59 us -> none  [local(): filt = lax.all_to_all(filters.reshape(CTX, 1, -1), 'ctx', 0, 0, tiled=True)]
    ppermute x2, waiting for transfers between devices: 14 us -> 18.5 us  [swap_yhi(): return lax.ppermute(block, 'tp', [(j, j ^ 1) for j in range(TP)])]
    pallas_call x2 -> x3, Pallas kernels: 15.9 us -> 20.4 us  [the longest x2 20.2 us: project(): pl.pallas_call(functools.partial(project_kernel, n_proj, len(out_shapes),...]
  transfers between devices with their start and end apart: 28 -> 27, of which waited for: 12 -> 18; matrix products, arithmetic and copies ran while one was open for 2% -> 2% of each run, Pallas kernels for 13% -> 18%
where the time goes in v2:
time: 241 us; the launch traced here: 240 us
  waiting for transfers between devices  119 us (49%)
  Pallas kernels  49.5 us (21%)
  starting transfers between devices  44.3 us (18%)
  between operations  13.5 us (6%)
  local copies, waits for them, and re-layouts  10.7 us (4%)
  other arithmetic  2.56 us (1%)
    ppermute x12, waiting for transfers between devices, shift_x(): return lax.ppermute(block, 'tp', route)  49.7 us
    pallas_call x2, Pallas kernels, project(): pl.pallas_call(functools.partial(project_kernel, n_proj, len(out_shapes),...  20.2 us
    ppermute x2, waiting for transfers between devices, swap_yhi(): return lax.ppermute(block, 'tp', [(j, j ^ 1) for j in range(TP)])  18.5 us
    ppermute x12, starting transfers between devices, shift_x(): return lax.ppermute(block, 'tp', route)  17.8 us
    ppermute x6, waiting for transfers between devices, swap_ctx(): return lax.ppermute(block, 'ctx', [(i, i ^ mask) for i in range(CTX)])  15.6 us
    all_gather x3, waiting for transfers between devices, gather_z(): lax.all_gather(block, 'ctx', axis=0, tiled=False, axis_index_groups=groups)  14.1 us
    pallas_call x1, Pallas kernels, conv(): pl.pallas_call(conv_kernel, out_shape=jax.ShapeDtypeStruct((rows, 256), B...  13.3 us
    all_to_all x1, waiting for transfers between devices, local(): sent = lax.all_to_all(blocks, 'ctx', 0, 0, tiled=True)  11.7 us
  transfers between devices with their start and end apart: 27, of which 18 were waited for; matrix products, arithmetic and copies ran while one was open for 2% of the time, Pallas kernels for 18%

profile of v2, /device:TPU:8, one launch (start us, length us, event | category | flops | bytes accessed | tf_op | source)
XLA Modules:
  0.0 239.7 jit_solution(17322589413530285421)
XLA Ops:
  10.7 6.6 %collective-permute-done = bf16[144,1024]{1,0:T(8,128)(2,1)S(1)} collective-permute-done((bf16[144,1024]{1,0:T(8,128)(2,1)S(1)}, bf16[144,1024]{1,0:T(8,128)(2,1)S(1)}, u32[]{:S(2)}, u32[]{:S(2)}) %collective-permute-start) | collective-permute-done | bytes 294944 | tf_op jit(solution)/shard_map/ppermute | solution.py:32
  23.3 9.1 %collective-permute-done.1.refs_1_ = bf16[512,512]{1,0:T(8,128)(2,1)S(1)} collective-permute-done((bf16[512,512]{1,0:T(8,128)(2,1)S(1)}, bf16[512,512]{1,0:T(8,128)(2,1)S(1)}, u32[]{:S(2)}, u32[]{:S(2)}) %collective-permute-start.1) | collective-permute-done | bytes 524320 | tf_op jit(solution)/shard_map/ppermute | solution.py:49
  36.1 8.6 %collective-permute-done.5.refs_5_ = bf16[512,512]{1,0:T(8,128)(2,1)S(1)} collective-permute-done((bf16[512,512]{1,0:T(8,128)(2,1)S(1)}, bf16[512,512]{1,0:T(8,128)(2,1)S(1)}, u32[]{:S(2)}, u32[]{:S(2)}) %collective-permute-start.5) | collective-permute-done | bytes 524320 | tf_op jit(solution)/shard_map/ppermute | solution.py:45
  44.8 3.8 %collective-permute-start.6 = (bf16[512,512]{1,0:T(8,128)(2,1)S(1)}, bf16[512,512]{1,0:T(8,128)(2,1)S(1)}, u32[]{:S(2)}, u32[]{:S(2)}) collective-permute-start(bf16[512,512]{1,0:T(8,128)(2,1)S(1)} %pad_maximum_fusion.1), channel_id=1, source_target_pairs={{0,6},{1,7},{2,0},{3,1},{4,2},{5,3},{6,4},{7,5},{8,14},{9,15},{10,... | collective-permute-start | bytes 1572872 | tf_op jit(solution)/shard_map/ppermute | solution.py:45
  51.4 7.9 %collective-permute-done.4.refs_4_ = bf16[512,512]{1,0:T(8,128)(2,1)S(1)} collective-permute-done((bf16[512,512]{1,0:T(8,128)(2,1)S(1)}, bf16[512,512]{1,0:T(8,128)(2,1)S(1)}, u32[]{:S(2)}, u32[]{:S(2)}) %collective-permute-start.4) | collective-permute-done | bytes 524320 | tf_op jit(solution)/shard_map/ppermute | solution.py:45
  62.1 9.4 %collective-permute-done.8.refs_6_ = bf16[512,512]{1,0:T(8,128)(2,1)S(1)} collective-permute-done((bf16[512,512]{1,0:T(8,128)(2,1)S(1)}, bf16[512,512]{1,0:T(8,128)(2,1)S(1)}, u32[]{:S(2)}, u32[]{:S(2)}) %collective-permute-start.8) | collective-permute-done | bytes 524320 | tf_op jit(solution)/shard_map/ppermute | solution.py:45
  71.5 9.4 %all-gather.7.cloned.1.call-done = bf16[16,144,1024]{2,1,0:T(8,128)(2,1)} async-done(((bf16[2,144,1024]{2,1,0:T(8,128)(2,1)}), bf16[16,144,1024]{2,1,0:T(8,128)(2,1)}) %all-gather.7.cloned.1.call-update) | async-done | bytes 4718608 | tf_op jit(solution)/shard_map/all_gather | solution.py:54
  83.7 4.1 %collective-permute-done.9 = bf16[128,512]{1,0:T(8,128)(2,1)S(1)} collective-permute-done((bf16[128,512]{1,0:T(8,128)(2,1)S(1)}, bf16[128,512]{1,0:T(8,128)(2,1)S(1)}, u32[]{:S(2)}, u32[]{:S(2)}) %collective-permute-start.9) | collective-permute-done | bytes 131104 | tf_op jit(solution)/shard_map/ppermute | solution.py:32
  89.2 10.7 %project2.1 = (bf16[512,512]{1,0:T(8,128)(2,1)}, bf16[32,32,256]{2,1,0:T(8,128)(2,1)}) custom-call(bf16[512,512]{1,0:T(8,128)(2,1)} %refs_0_.3, bf16[512,512]{1,0:T(8,128)(2,1)} %copy-done.5, bf16[512,512]{1,0:T(8,128)(2,1)} %copy-done.2, bf16[512,512]{1,0:T(8,128)(2,1)} %copy-done, bf16[512,512]{1,0:T(8,128)(2,1)} %copy-done.3, bf16[512,512]{1,0:T(8,128)(2,1)} %copy-done.1, ...), custom_call_target="tpu_custom_call" | custom-call | tf_op jit(solution)/shard_map/project2/pallas_call | solution.py:209
  99.9 9.7 %all-to-all-start = ((bf16[32,32,256]{2,1,0:T(8,128)(2,1)}), bf16[32,32,256]{2,1,0:T(8,128)(2,1)S(1)}, u32[]{:S(2)}, u32[]{:S(2)}) async-start(bf16[32,32,256]{2,1,0:T(8,128)(2,1)} %get-tuple-element.53), calls=%async_computation | async-start | bytes 1048576 | tf_op jit(solution)/shard_map/all_to_all | solution.py:441
  110.2 9.0 %toeplitz.1 = bf16[64,256,256]{2,1,0:T(8,128)(2,1)} custom-call(bf16[8,2,144,1024]{3,2,1,0:T(8,128)(2,1)} %bitcast.24, bf16[8,2,144,1024]{3,2,1,0:T(8,128)(2,1)} %collective-permute-done.11.refs_10_.other), custom_call_target="tpu_custom_call" | custom-call | tf_op jit(solution)/shard_map/toeplitz/pallas_call | solution.py:282
  119.9 11.7 %all-to-all-done = bf16[32,32,256]{2,1,0:T(8,128)(2,1)S(1)} async-done(((bf16[32,32,256]{2,1,0:T(8,128)(2,1)}), bf16[32,32,256]{2,1,0:T(8,128)(2,1)S(1)}, u32[]{:S(2)}, u32[]{:S(2)}) %all-to-all-start) | async-done | bytes 524320 | tf_op jit(solution)/shard_map/all_to_all | solution.py:441
  132.4 13.3 %conv.1 = bf16[1024,256]{1,0:T(8,128)(2,1)} custom-call(bf16[1024,256]{1,0:T(8,128)(2,1)} %bitcast.28, bf16[16,1024,256]{2,1,0:T(8,128)(2,1)} %bitcast.21), custom_call_target="tpu_custom_call" | custom-call | tf_op jit(solution)/shard_map/conv/pallas_call | solution.py:326
  145.7 4.7 %all-gather.9.cloned.1.call-done = bf16[16,128,512]{2,1,0:T(8,128)(2,1)} async-done(((bf16[2,128,512]{2,1,0:T(8,128)(2,1)}), bf16[16,128,512]{2,1,0:T(8,128)(2,1)}) %all-gather.9.cloned.1.call-update) | async-done | bytes 2097168 | tf_op jit(solution)/shard_map/all_gather | solution.py:54
  150.4 5.4 %all-to-all-start.1 = ((bf16[32,32,256]{2,1,0:T(8,128)(2,1)}), bf16[32,32,256]{2,1,0:T(8,128)(2,1)S(1)}, u32[]{:S(2)}, u32[]{:S(2)}) async-start(bf16[32,32,256]{2,1,0:T(8,128)(2,1)} %bitcast.27), calls=%async_computation.1 | async-start | bytes 1048576 | tf_op jit(solution)/shard_map/all_to_all | solution.py:446
  157.8 9.6 %project1.1.query_ref = f32[512,512]{1,0:T(8,128)} custom-call(bf16[512,512]{1,0:T(8,128)(2,1)} %refs_0_.3, bf16[512,512]{1,0:T(8,128)(2,1)} %copy-done.5, bf16[512,512]{1,0:T(8,128)(2,1)} %copy-done.2, bf16[512,512]{1,0:T(8,128)(2,1)} %copy-done, bf16[512,512]{1,0:T(8,128)(2,1)} %copy-done.3, bf16[512,512]{1,0:T(8,128)(2,1)} %copy-done.1, ...), custom_call_target="tpu_custom_call" | custom-call | tf_op jit(solution)/shard_map/project1/pallas_call | solution.py:209
  167.3 9.5 %all-to-all-done.1.back_ref = bf16[32,32,256]{2,1,0:T(8,128)(2,1)S(1)} async-done(((bf16[32,32,256]{2,1,0:T(8,128)(2,1)}), bf16[32,32,256]{2,1,0:T(8,128)(2,1)S(1)}, u32[]{:S(2)}, u32[]{:S(2)}) %all-to-all-start.1) | async-done | bytes 524320 | tf_op jit(solution)/shard_map/all_to_all | solution.py:446
  178.3 3.0 %collective-permute-start.14 = (bf16[512,512]{1,0:T(8,128)(2,1)S(1)}, bf16[512,512]{1,0:T(8,128)(2,1)S(1)}, u32[]{:S(2)}, u32[]{:S(2)}) collective-permute-start(bf16[512,512]{1,0:T(8,128)(2,1)S(1)} %gate.1.refs_0_), channel_id=1, source_target_pairs={{0,1},{1,0},{2,3},{3,2},{4,5},{5,4},{6,7},{7,6},{8,9},{9,8},{10,11... | collective-permute-start | bytes 1572872 | tf_op jit(solution)/shard_map/ppermute | solution.py:49
  183.4 9.5 %collective-permute-done.14.refs_1_ = bf16[512,512]{1,0:T(8,128)(2,1)S(1)} collective-permute-done((bf16[512,512]{1,0:T(8,128)(2,1)S(1)}, bf16[512,512]{1,0:T(8,128)(2,1)S(1)}, u32[]{:S(2)}, u32[]{:S(2)}) %collective-permute-start.14) | collective-permute-done | bytes 524320 | tf_op jit(solution)/shard_map/ppermute | solution.py:49
  195.6 9.6 %collective-permute-done.18.refs_5_ = bf16[512,512]{1,0:T(8,128)(2,1)S(1)} collective-permute-done((bf16[512,512]{1,0:T(8,128)(2,1)S(1)}, bf16[512,512]{1,0:T(8,128)(2,1)S(1)}, u32[]{:S(2)}, u32[]{:S(2)}) %collective-permute-start.18) | collective-permute-done | bytes 524320 | tf_op jit(solution)/shard_map/ppermute | solution.py:45
  205.3 3.3 %collective-permute-start.20 = (bf16[512,512]{1,0:T(8,128)(2,1)S(1)}, bf16[512,512]{1,0:T(8,128)(2,1)S(1)}, u32[]{:S(2)}, u32[]{:S(2)}) collective-permute-start(bf16[512,512]{1,0:T(8,128)(2,1)S(1)} %pad_maximum_fusion.4), channel_id=1, source_target_pairs={{0,6},{1,7},{2,0},{3,1},{4,2},{5,3},{6,4},{7,5},{8,14},{9,15},{10,... | collective-permute-start | bytes 1572872 | tf_op jit(solution)/shard_map/ppermute | solution.py:45
  209.3 7.8 %collective-permute-done.20.refs_7_ = bf16[512,512]{1,0:T(8,128)(2,1)S(1)} collective-permute-done((bf16[512,512]{1,0:T(8,128)(2,1)S(1)}, bf16[512,512]{1,0:T(8,128)(2,1)S(1)}, u32[]{:S(2)}, u32[]{:S(2)}) %collective-permute-start.20) | collective-permute-done | bytes 524320 | tf_op jit(solution)/shard_map/ppermute | solution.py:45
  220.9 4.4 %collective-permute-done.21.refs_9_ = bf16[8,2,512,128]{3,2,1,0:T(8,128)(2,1)S(1)} collective-permute-done((bf16[8,2,512,128]{3,2,1,0:T(8,128)(2,1)}, bf16[8,2,512,128]{3,2,1,0:T(8,128)(2,1)S(1)}, u32[]{:S(2)}, u32[]{:S(2)}) %collective-permute-start.21) | collective-permute-done | bytes 2097184 | tf_op jit(solution)/shard_map/ppermute | solution.py:32
  226.6 6.5 %output.1 = bf16[512,512]{1,0:T(8,128)(2,1)} custom-call(bf16[512,512]{1,0:T(8,128)(2,1)} %copy-done.8, bf16[512,512]{1,0:T(8,128)(2,1)} %copy-done.20, bf16[512,512]{1,0:T(8,128)(2,1)} %copy-done.16, bf16[512,512]{1,0:T(8,128)(2,1)} %copy-done.15, bf16[512,512]{1,0:T(8,128)(2,1)} %copy-done.18, bf16[512,512]{1,0:T(8,128)(2,1)} %copy-done.17, ...), custom_call_target="tpu_custom_call" | custom-call | tf_op jit(solution)/shard_map/output/pallas_call | solution.py:385
  (109 shorter events, 39.8 us)
Async XLA Ops:
  6.5 74.4 %all-gather.7.cloned.1.call-start = ((), (), s32[]{:S(2)}) async-start(), calls=%async_computation.2 | async-start | bytes 5308416 | tf_op jit(solution)/shard_map/all_gather | solution.py:54
  8.4 8.8 %collective-permute-start = (bf16[144,1024]{1,0:T(8,128)(2,1)S(1)}, bf16[144,1024]{1,0:T(8,128)(2,1)S(1)}, u32[]{:S(2)}, u32[]{:S(2)}) collective-permute-start(bf16[144,1024]{1,0:T(8,128)(2,1)S(1)} %get-tuple-element.76), channel_id=1, source_target_pairs={{0,16},{8,24},{16,0},{24,8},{32,48},{40,56},{48,32},{56,40},{64,80... | collective-permute-start | bytes 884744 | tf_op jit(solution)/shard_map/ppermute | solution.py:32
  18.1 132.3 %all-gather.9.cloned.1.call-start = ((), (), s32[]{:S(2)}) async-start(), calls=%async_computation.3 | async-start | bytes 2359296 | tf_op jit(solution)/shard_map/all_gather | solution.py:54
  18.2 14.2 %collective-permute-start.1 = (bf16[512,512]{1,0:T(8,128)(2,1)S(1)}, bf16[512,512]{1,0:T(8,128)(2,1)S(1)}, u32[]{:S(2)}, u32[]{:S(2)}) collective-permute-start(bf16[512,512]{1,0:T(8,128)(2,1)S(1)} %copy-done.4), channel_id=1, source_target_pairs={{0,1},{1,0},{2,3},{3,2},{4,5},{5,4},{6,7},{7,6},{8,9},{9,8},{10,11... | collective-permute-start | bytes 1572872 | tf_op jit(solution)/shard_map/ppermute | solution.py:49
  20.6 15.5 %collective-permute-start.3 = (bf16[512,512]{1,0:T(8,128)(2,1)S(1)}, bf16[512,512]{1,0:T(8,128)(2,1)S(1)}, u32[]{:S(2)}, u32[]{:S(2)}) collective-permute-start(bf16[512,512]{1,0:T(8,128)(2,1)S(1)} %copy-done.4), channel_id=1, source_target_pairs={{0,6},{1,7},{2,0},{3,1},{4,2},{5,3},{6,4},{7,5},{8,14},{9,15},{10,... | collective-permute-start | bytes 1572872 | tf_op jit(solution)/shard_map/ppermute | solution.py:45
  32.4 12.3 %collective-permute-start.5 = (bf16[512,512]{1,0:T(8,128)(2,1)S(1)}, bf16[512,512]{1,0:T(8,128)(2,1)S(1)}, u32[]{:S(2)}, u32[]{:S(2)}) collective-permute-start(bf16[512,512]{1,0:T(8,128)(2,1)S(1)} %collective-permute-done.1.refs_1_), channel_id=1, source_target_pairs={{0,6},{1,7},{2,0},{3,1},{4,2},{5,3},{6,4},{7,5},{8,14},{9,15},{10,... | collective-permute-start | bytes 1572872 | tf_op jit(solution)/shard_map/ppermute | solution.py:45
  35.3 16.1 %collective-permute-start.2 = (bf16[512,512]{1,0:T(8,128)(2,1)S(1)}, bf16[512,512]{1,0:T(8,128)(2,1)S(1)}, u32[]{:S(2)}, u32[]{:S(2)}) collective-permute-start(bf16[512,512]{1,0:T(8,128)(2,1)S(1)} %copy-done.4), channel_id=1, source_target_pairs={{0,2},{1,3},{2,4},{3,5},{4,6},{5,7},{6,0},{7,1},{8,10},{9,11},{10,... | collective-permute-start | bytes 1572872 | tf_op jit(solution)/shard_map/ppermute | solution.py:45
  35.3 24.0 %collective-permute-start.4 = (bf16[512,512]{1,0:T(8,128)(2,1)S(1)}, bf16[512,512]{1,0:T(8,128)(2,1)S(1)}, u32[]{:S(2)}, u32[]{:S(2)}) collective-permute-start(bf16[512,512]{1,0:T(8,128)(2,1)S(1)} %collective-permute-done.1.refs_1_), channel_id=1, source_target_pairs={{0,2},{1,3},{2,4},{3,5},{4,6},{5,7},{6,0},{7,1},{8,10},{9,11},{10,... | collective-permute-start | bytes 1572872 | tf_op jit(solution)/shard_map/ppermute | solution.py:45
  44.8 14.8 %collective-permute-start.6 = (bf16[512,512]{1,0:T(8,128)(2,1)S(1)}, bf16[512,512]{1,0:T(8,128)(2,1)S(1)}, u32[]{:S(2)}, u32[]{:S(2)}) collective-permute-start(bf16[512,512]{1,0:T(8,128)(2,1)S(1)} %pad_maximum_fusion.1), channel_id=1, source_target_pairs={{0,6},{1,7},{2,0},{3,1},{4,2},{5,3},{6,4},{7,5},{8,14},{9,15},{10,... | collective-permute-start | bytes 1572872 | tf_op jit(solution)/shard_map/ppermute | solution.py:45
  59.5 12.1 %collective-permute-start.8 = (bf16[512,512]{1,0:T(8,128)(2,1)S(1)}, bf16[512,512]{1,0:T(8,128)(2,1)S(1)}, u32[]{:S(2)}, u32[]{:S(2)}) collective-permute-start(bf16[512,512]{1,0:T(8,128)(2,1)S(1)} %pad_maximum_fusion.2), channel_id=1, source_target_pairs={{0,2},{1,3},{2,4},{3,5},{4,6},{5,7},{6,0},{7,1},{8,10},{9,11},{10,... | collective-permute-start | bytes 1572872 | tf_op jit(solution)/shard_map/ppermute | solution.py:45
  60.2 11.4 %collective-permute-start.7 = (bf16[8,16,512]{2,1,0:T(8,128)(2,1)S(1)}, bf16[8,16,512]{2,1,0:T(8,128)(2,1)S(1)}, u32[]{:S(2)}, u32[]{:S(2)}) collective-permute-start(bf16[8,16,512]{2,1,0:T(8,128)(2,1)S(1)} %tail.1), channel_id=1, source_target_pairs={{0,8},{8,16},{16,24},{24,32},{32,40},{40,48},{48,56},{56,64},{64,7... | collective-permute-start | bytes 393224 | tf_op jit(solution)/shard_map/ppermute | solution.py:415
  80.9 8.3 %collective-permute-start.11 = (bf16[8,2,144,1024]{3,2,1,0:T(8,128)(2,1)}, bf16[8,2,144,1024]{3,2,1,0:T(8,128)(2,1)}, u32[]{:S(2)}, u32[]{:S(2)}) collective-permute-start(bf16[8,2,144,1024]{3,2,1,0:T(8,128)(2,1)} %bitcast.22), channel_id=1, source_target_pairs={{0,8},{8,0},{16,24},{24,16},{32,40},{40,32},{48,56},{56,48},{64,72... | collective-permute-start | bytes 14155784 | tf_op jit(solution)/shard_map/ppermute | solution.py:32
  82.5 17.4 %collective-permute-start.10 = (bf16[512,128]{1,0:T(8,128)(2,1)S(1)}, bf16[512,128]{1,0:T(8,128)(2,1)S(1)}, u32[]{:S(2)}, u32[]{:S(2)}) collective-permute-start(bf16[512,128]{1,0:T(8,128)(2,1)S(1)} %copy-done.23), channel_id=1, source_target_pairs={{0,0},{1,32},{2,64},{3,96},{4,128},{5,160},{6,192},{7,224},{8,8},{... | collective-permute-start | bytes 393224 | tf_op jit(solution)/shard_map/ppermute | solution.py:426
  99.9 31.8 %all-to-all-start = ((bf16[32,32,256]{2,1,0:T(8,128)(2,1)}), bf16[32,32,256]{2,1,0:T(8,128)(2,1)S(1)}, u32[]{:S(2)}, u32[]{:S(2)}) async-start(bf16[32,32,256]{2,1,0:T(8,128)(2,1)} %get-tuple-element.53), calls=%async_computation | async-start | bytes 1048576 | tf_op jit(solution)/shard_map/all_to_all | solution.py:441
  109.6 111.3 %all-gather.11.cloned.1.call-start = ((), (), s32[]{:S(2)}) async-start(), calls=%async_computation.4 | async-start | bytes 2359296 | tf_op jit(solution)/shard_map/all_gather | solution.py:54
  109.7 9.5 %collective-permute-start.12 = (bf16[512,128]{1,0:T(8,128)(2,1)S(1)}, bf16[512,128]{1,0:T(8,128)(2,1)S(1)}, u32[]{:S(2)}, u32[]{:S(2)}) collective-permute-start(bf16[512,128]{1,0:T(8,128)(2,1)S(1)} %collective-permute-done.10), channel_id=1, source_target_pairs={{0,16},{8,24},{16,0},{24,8},{32,48},{40,56},{48,32},{56,40},{64,80... | collective-permute-start | bytes 393224 | tf_op jit(solution)/shard_map/ppermute | solution.py:32
  150.4 26.4 %all-to-all-start.1 = ((bf16[32,32,256]{2,1,0:T(8,128)(2,1)}), bf16[32,32,256]{2,1,0:T(8,128)(2,1)S(1)}, u32[]{:S(2)}, u32[]{:S(2)}) async-start(bf16[32,32,256]{2,1,0:T(8,128)(2,1)} %bitcast.27), calls=%async_computation.1 | async-start | bytes 1048576 | tf_op jit(solution)/shard_map/all_to_all | solution.py:446
  178.3 14.5 %collective-permute-start.14 = (bf16[512,512]{1,0:T(8,128)(2,1)S(1)}, bf16[512,512]{1,0:T(8,128)(2,1)S(1)}, u32[]{:S(2)}, u32[]{:S(2)}) collective-permute-start(bf16[512,512]{1,0:T(8,128)(2,1)S(1)} %gate.1.refs_0_), channel_id=1, source_target_pairs={{0,1},{1,0},{2,3},{3,2},{4,5},{5,4},{6,7},{7,6},{8,9},{9,8},{10,11... | collective-permute-start | bytes 1572872 | tf_op jit(solution)/shard_map/ppermute | solution.py:49
  181.3 13.6 %collective-permute-start.16 = (bf16[512,512]{1,0:T(8,128)(2,1)S(1)}, bf16[512,512]{1,0:T(8,128)(2,1)S(1)}, u32[]{:S(2)}, u32[]{:S(2)}) collective-permute-start(bf16[512,512]{1,0:T(8,128)(2,1)S(1)} %gate.1.refs_0_), channel_id=1, source_target_pairs={{0,6},{1,7},{2,0},{3,1},{4,2},{5,3},{6,4},{7,5},{8,14},{9,15},{10,... | collective-permute-start | bytes 1572872 | tf_op jit(solution)/shard_map/ppermute | solution.py:45
  182.1 13.5 %collective-permute-start.15 = (bf16[512,512]{1,0:T(8,128)(2,1)S(1)}, bf16[512,512]{1,0:T(8,128)(2,1)S(1)}, u32[]{:S(2)}, u32[]{:S(2)}) collective-permute-start(bf16[512,512]{1,0:T(8,128)(2,1)S(1)} %gate.1.refs_0_), channel_id=1, source_target_pairs={{0,2},{1,3},{2,4},{3,5},{4,6},{5,7},{6,0},{7,1},{8,10},{9,11},{10,... | collective-permute-start | bytes 1572872 | tf_op jit(solution)/shard_map/ppermute | solution.py:45
  192.9 12.3 %collective-permute-start.18 = (bf16[512,512]{1,0:T(8,128)(2,1)S(1)}, bf16[512,512]{1,0:T(8,128)(2,1)S(1)}, u32[]{:S(2)}, u32[]{:S(2)}) collective-permute-start(bf16[512,512]{1,0:T(8,128)(2,1)S(1)} %collective-permute-done.14.refs_1_), channel_id=1, source_target_pairs={{0,6},{1,7},{2,0},{3,1},{4,2},{5,3},{6,4},{7,5},{8,14},{9,15},{10,... | collective-permute-start | bytes 1572872 | tf_op jit(solution)/shard_map/ppermute | solution.py:45
  194.9 13.6 %collective-permute-start.17 = (bf16[512,512]{1,0:T(8,128)(2,1)S(1)}, bf16[512,512]{1,0:T(8,128)(2,1)S(1)}, u32[]{:S(2)}, u32[]{:S(2)}) collective-permute-start(bf16[512,512]{1,0:T(8,128)(2,1)S(1)} %collective-permute-done.14.refs_1_), channel_id=1, source_target_pairs={{0,2},{1,3},{2,4},{3,5},{4,6},{5,7},{6,0},{7,1},{8,10},{9,11},{10,... | collective-permute-start | bytes 1572872 | tf_op jit(solution)/shard_map/ppermute | solution.py:45
  205.3 11.9 %collective-permute-start.20 = (bf16[512,512]{1,0:T(8,128)(2,1)S(1)}, bf16[512,512]{1,0:T(8,128)(2,1)S(1)}, u32[]{:S(2)}, u32[]{:S(2)}) collective-permute-start(bf16[512,512]{1,0:T(8,128)(2,1)S(1)} %pad_maximum_fusion.4), channel_id=1, source_target_pairs={{0,6},{1,7},{2,0},{3,1},{4,2},{5,3},{6,4},{7,5},{8,14},{9,15},{10,... | collective-permute-start | bytes 1572872 | tf_op jit(solution)/shard_map/ppermute | solution.py:45
  208.7 12.2 %collective-permute-start.19 = (bf16[512,512]{1,0:T(8,128)(2,1)S(1)}, bf16[512,512]{1,0:T(8,128)(2,1)}, u32[]{:S(2)}, u32[]{:S(2)}) collective-permute-start(bf16[512,512]{1,0:T(8,128)(2,1)S(1)} %pad_maximum_fusion.3), channel_id=1, source_target_pairs={{0,2},{1,3},{2,4},{3,5},{4,6},{5,7},{6,0},{7,1},{8,10},{9,11},{10,... | collective-permute-start | bytes 1572872 | tf_op jit(solution)/shard_map/ppermute | solution.py:45
  (27 other events, 344.2 us)
Sparse Core Ops, SparseCore 0:
  18.3 62.6 all-gather.6
  100.0 50.3 all-gather.8
  152.2 44.3 all-gather.10

commit v3 on v2

--- a/solution.py
+++ b/solution.py
@@ -54,14 +54,17 @@
     return lax.all_gather(block, "ctx", axis=0, tiled=False, axis_index_groups=groups)
 
 
-def gather_tp(own):
+def gather_tp(own, first=None):
     half = own.shape[0] // 2
     near = swap_yhi(own)
+    if first is not None:
+        near, first = barrier(near, first)
     own_right, own_left = shift_x(own, 1), shift_x(own, -1)
     near_right, near_left = shift_x(near, 1), shift_x(near, -1)
     far_right = shift_x(jnp.concatenate([own_right[:half], near_right[:half]]), 1)
     far_left = shift_x(jnp.concatenate([own_left[half:], near_left[half:]]), -1)
-    return [own, near, own_right, own_left, near_right, near_left, far_right, far_left]
+    pieces = [own, near, own_right, own_left, near_right, near_left, far_right, far_left]
+    return pieces, first
 
 
 def piece_copies(pieces, dst, first_row, sem):
@@ -296,47 +299,56 @@
     )(*weights)
 
 
-FOLD = 4
-
-
-def conv_kernel(x_ref, h_hbm, y_ref, wide, acc, h_ref, sems):
-    rows = x_ref.shape[0]
-    steps = h_ref.shape[0]
-    copies = [pltpu.make_async_copy(h_hbm.at[g], h_ref.at[g], sems.at[g]) for g in range(steps)]
-    for copy in copies:
-        copy.start()
-    for k in range(FOLD):
-        if k:
-            wide[0 : 16 * k, 256 * k : 256 * k + 256] = jnp.zeros((16 * k, 256), BF16)
-        wide[16 * k : rows, 256 * k : 256 * k + 256] = x_ref[0 : rows - 16 * k, :]
-    for g in range(steps):
-        copies[g].wait()
-        skip = 16 * FOLD * g
-        product = jnp.dot(wide[0 : rows - skip, :], h_ref[g], preferred_element_type=F32)
-        if g == 0:
-            acc[...] = product
-        else:
-            acc[skip:rows, :] += product
-    y_ref[...] = acc[...].astype(BF16)
+TILE = 128
+LAGS = TILE // 16
+FETCHES = 4
+
+
+def conv_kernel(x_ref, h_hbm, y_ref, h_ref, sems):
+    rows, width = x_ref.shape
+    tiles = rows // TILE
+
+    def fetch(g):
+        count = h_ref.shape[0] // FETCHES
+        here = pl.ds(g * count, count)
+        return pltpu.make_async_copy(h_hbm.at[here], h_ref.at[here], sems.at[g])
+
+    for g in range(FETCHES):
+        fetch(g).start()
+    for tile in range(tiles):
+        if tile % (tiles // FETCHES) == 0:
+            fetch(tile // (tiles // FETCHES)).wait()
+        lags = (tile + 1) * LAGS
+        shifted = []
+        for lag in range(lags):
+            first = tile * TILE - 16 * lag
+            if first >= 0:
+                shifted.append(x_ref[first : first + TILE, :])
+            else:
+                empty = jnp.zeros((-first, width), BF16)
+                shifted.append(jnp.concatenate([empty, x_ref[0 : TILE + first, :]], axis=0))
+        product = jnp.dot(
+            jnp.concatenate(shifted, axis=1),
+            h_ref[0 : lags * width, :],
+            preferred_element_type=F32,
+        )
+        y_ref[tile * TILE : tile * TILE + TILE, :] = product.astype(BF16)
 
 
 def conv(x, table):
-    rows = x.shape[0]
-    steps = 64 // FOLD
+    rows, width = x.shape
     return pl.pallas_call(
         conv_kernel,
-        out_shape=jax.ShapeDtypeStruct((rows, 256), BF16),
+        out_shape=jax.ShapeDtypeStruct((rows, width), BF16),
         in_specs=[VMEM, HBM],
         out_specs=VMEM,
         scratch_shapes=[
-            pltpu.VMEM((rows, FOLD * 256), BF16),
-            pltpu.VMEM((rows, 256), F32),
-            pltpu.VMEM((steps, FOLD * 256, 256), BF16),
-            pltpu.SemaphoreType.DMA((steps,)),
+            pltpu.VMEM((64 * width, width), BF16),
+            pltpu.SemaphoreType.DMA((FETCHES,)),
         ],
         compiler_params=pltpu.CompilerParams(vmem_limit_bytes=60 * MIB),
         name="conv",
-    )(x, table.reshape(steps, FOLD * 256, 256))
+    )(x, table.reshape(64 * width, width))
 
 
 def gate_kernel(back_ref, mixed_ref, query_ref, skip_ref, out_ref):
@@ -360,42 +372,71 @@
     )(back, mixed, query, skip)
 
 
-def output_kernel(*refs):
-    pieces = refs[:8]
-    mine, other, out_ref, act, wts, act_sem, w_sem = refs[8:]
-    z, y, core = weight_slots()
-    copies = piece_copies(pieces, act, 0, act_sem)
-    depth, width = mine.shape[2:]
-    for ref, dc in ((mine, 0), (other, 1)):
-        for dy in (0, 1):
-            slot = ((y + dy) % 2) * 2 + (core + dc) % 2
+def near_parts(pieces):
+    me = lax.axis_index("tp")
+    x, y = me // 2, me % 2
+    offsets = [(0, 0), (0, 1), (-1, 0), (1, 0), (-1, 1), (1, 1)]
+    parts = []
+    for ref, (dx, dy) in zip(pieces, offsets):
+        parts.append((((x + dx + NX) % NX) * 2 + (y + dy) % 2, [(ref, 0)]))
+    return parts
+
+
+def far_parts(pieces):
+    me = lax.axis_index("tp")
+    x, y = me // 2, me % 2
+    half = pieces[0].shape[0] // 2
+    parts = []
+    for dy in (0, 1):
+        rows = pl.ds(dy * half, half)
+        there = ((x + 2) % NX) * 2 + (y + dy) % 2
+        parts.append((there, [(pieces[0].at[rows], 0), (pieces[1].at[rows], half)]))
+    return parts
+
+
+def output_kernel(parts_of, n_pieces, *refs):
+    pieces, (weights, *start) = refs[:n_pieces], refs[n_pieces:-4]
+    out_ref, act, wts, sem = refs[-4:]
+    _, y, core = weight_slots()
+    width = weights.shape[3]
+    depth = wts.shape[1]
+    copies = []
+    for p, (there, sources) in enumerate(parts_of(pieces)):
+        for src, first in sources:
+            to = act.at[pl.ds(first, src.shape[0]), pl.ds(p * depth, depth)]
+            copies.append(pltpu.make_async_copy(src, to, sem))
+        for k in range(4):
+            slot = ((y + k // 2) % 2) * 2 + (core + k % 2) % 2
             lanes = pl.ds(pl.multiple_of(slot * width, width), width)
-            copies.append(pltpu.make_async_copy(ref.at[:, dy], wts.at[:, :, lanes], w_sem))
+            to = wts.at[p, :, lanes]
+            copies.append(pltpu.make_async_copy(weights.at[there, k], to, sem))
     for copy in copies:
         copy.start()
     for copy in copies:
         copy.wait()
-    weights = wts[...].reshape(-1, wts.shape[2])
-    out_ref[...] = jnp.dot(act[...], weights, preferred_element_type=F32).astype(BF16)
-
-
-def output(pieces, mine, other):
-    rows, part = pieces[0].shape
-    depth, width = mine.shape[2:]
+    matrix = wts[...].reshape(-1, wts.shape[2])
+    total = jnp.dot(act[...], matrix, preferred_element_type=F32)
+    if start:
+        total = total + start[0][...]
+    out_ref[...] = total.astype(out_ref.dtype)
+
+
+def output(pieces, parts_of, parts, weights, start, dtype):
+    rows = pieces[0].shape[0]
+    depth, width = weights.shape[2:]
     return pl.pallas_call(
-        output_kernel,
-        out_shape=jax.ShapeDtypeStruct((rows, 4 * width), BF16),
-        in_specs=[HBM] * 10,
+        functools.partial(output_kernel, parts_of, len(pieces)),
+        out_shape=jax.ShapeDtypeStruct((rows, 4 * width), dtype),
+        in_specs=[HBM] * (len(pieces) + 1) + [VMEM] * len(start),
         out_specs=VMEM,
         scratch_shapes=[
-            pltpu.VMEM((rows, TP * part), BF16),
-            pltpu.VMEM((NZ, depth, 4 * width), BF16),
-            pltpu.SemaphoreType.DMA,
+            pltpu.VMEM((rows, parts * depth), BF16),
+            pltpu.VMEM((parts, depth, 4 * width), BF16),
             pltpu.SemaphoreType.DMA,
         ],
         compiler_params=pltpu.CompilerParams(vmem_limit_bytes=60 * MIB),
-        name="output",
-    )(*pieces, mine, other)
+        name="output%d" % parts,
+    )(*pieces, weights, *start)
 
 
 def pair_ylo(own):
@@ -410,20 +451,20 @@
     kv = jnp.concatenate([w_in[1], w_in[2]], axis=1)
     filt = jnp.concatenate([filters[:16], filters[16:]], axis=1)
     kv_mine = gather_z(pair_ylo(jnp.concatenate([kv, filt])))
-    pieces = gather_tp(tokens)
-    tail = last_rows(pieces)
-    tail = lax.ppermute(tail, "ctx", [(i, i + 1) for i in range(CTX - 1)])
-
-    kv_mine, tail, *pieces = barrier(kv_mine, tail, *pieces)
-    w_in, w_out, kv_mine = barrier(w_in, w_out, kv_mine)
-    kv_other = swap_core(kv_mine)
-    q_pair = pair_ylo(w_in[0])
     route = []
     for z in range(NZ):
         for r in range(4):
             for j in range(TP):
                 route.append(((4 * z + r) * TP + j, (4 * j + r) * TP + z))
     w_out = lax.ppermute(w_out, ("ctx", "tp"), route)
+    pieces, w_out = gather_tp(tokens, w_out)
+    tail = last_rows(pieces)
+    tail = lax.ppermute(tail, "ctx", [(i, i + 1) for i in range(CTX - 1)])
+
+    kv_mine, tail, *pieces = barrier(kv_mine, tail, *pieces)
+    w_in, kv_mine = barrier(w_in, kv_mine)
+    kv_other = swap_core(kv_mine)
+    q_mine = gather_z(pair_ylo(w_in[0]))
     mixed, blocks = project(
         pieces,
         tail,
@@ -435,15 +476,16 @@
         ],
     )
 
-    q_pair, w_out, blocks = barrier(q_pair, w_out, blocks)
-    q_mine = gather_z(q_pair)
-    o_pair = pair_ylo(w_out)
+    w_out, blocks = barrier(w_out, blocks)
+    o_pair = jnp.stack([w_out, swap_core(w_out)])
+    o_pair = jnp.concatenate([o_pair, swap_ylo(o_pair)])
     sent = lax.all_to_all(blocks, "ctx", 0, 0, tiled=True)
     table = toeplitz((kv_mine, kv_other))
     o_pair, sent, table = barrier(o_pair, sent, table)
     result = conv(sent.reshape(CTX * 32, 256), table)
-    q_mine, result = barrier(q_mine, result)
+    q_mine, o_pair, result = barrier(q_mine, o_pair, result)
     back = lax.all_to_all(result.reshape(CTX, 32, 256), "ctx", 0, 0, tiled=True)
+    o_mine = gather_z(o_pair)
     (query,) = project(
         pieces,
         tail,
@@ -453,10 +495,9 @@
     )
     gated = gate(back, mixed, query, skip[None, :])
 
-    o_pair, q_mine = barrier(o_pair, q_mine)
-    o_mine = gather_z(o_pair)
-    o_mine, *gathered = barrier(o_mine, *gather_tp(gated))
-    return output(gathered, o_mine, swap_core(o_mine))
+    gathered = gather_tp(gated)[0]
+    total = output(gathered[:6], near_parts, 6, o_mine, [], F32)
+    return output(gathered[6:], far_parts, 2, o_mine, [total], BF16)
 
 
 def solution(mesh):

time: 241 us -> 227 us (0.942)
  waiting for transfers between devices: 119 us -> 95.9 us
  starting transfers between devices: 44.3 us -> 57 us
  local copies, waits for them, and re-layouts: 10.7 us -> 6.8 us
    ppermute x12, starting transfers between devices: 17.8 us -> 33.8 us  [shift_x(): return lax.ppermute(block, 'tp', route)]
    ppermute x12, waiting for transfers between devices: 49.7 us -> 38.2 us  [shift_x(): return lax.ppermute(block, 'tp', route)]
    ppermute x2, waiting for transfers between devices: 18.5 us -> 11.8 us  [swap_yhi(): return lax.ppermute(block, 'tp', [(j, j ^ 1) for j in range(TP)])]
    all_gather x3, waiting for transfers between devices: 14.1 us -> 8.75 us  [gather_z(): lax.all_gather(block, 'ctx', axis=0, tiled=False, axis_index_groups=groups)]
    all_to_all x1, starting transfers between devices: 9.73 us -> 4.91 us  [local(): sent = lax.all_to_all(blocks, 'ctx', 0, 0, tiled=True)]
    unnamed x48 -> x38, local copies, waits for them, and re-layouts: 6.68 us -> 2.75 us
    ppermute x1, waiting for transfers between devices: 0.01 us -> 3.36 us  [local(): tail = lax.ppermute(tail, 'ctx', [(i, i + 1) for i in range(CTX - 1)])]
    all_to_all x1, waiting for transfers between devices: 11.7 us -> 9.24 us  [local(): sent = lax.all_to_all(blocks, 'ctx', 0, 0, tiled=True)]
  transfers between devices with their start and end apart: 27 -> 27, of which waited for: 18 -> 20; matrix products, arithmetic and copies ran while one was open for 2% -> 3% of each run, Pallas kernels for 18% -> 20%
where the time goes in v3:
time: 227 us
  waiting for transfers between devices  95.9 us (42%)
  starting transfers between devices  57 us (25%)
  Pallas kernels  49.2 us (22%)
  between operations  13.4 us (6%)
  local copies, waits for them, and re-layouts  6.8 us (3%)
  other arithmetic  4.49 us (2%)
    ppermute x12, waiting for transfers between devices, shift_x(): return lax.ppermute(block, 'tp', route)  38.2 us
    ppermute x12, starting transfers between devices, shift_x(): return lax.ppermute(block, 'tp', route)  33.8 us
    pallas_call x2, Pallas kernels, project(): pl.pallas_call(functools.partial(project_kernel, n_proj, len(out_shapes),...  20.2 us
    ppermute x6, waiting for transfers between devices, swap_ctx(): return lax.ppermute(block, 'ctx', [(i, i ^ mask) for i in range(CTX)])  13.9 us
    ppermute x2, waiting for transfers between devices, swap_yhi(): return lax.ppermute(block, 'tp', [(j, j ^ 1) for j in range(TP)])  11.8 us
    all_to_all x1, waiting for transfers between devices, local(): back = lax.all_to_all(result.reshape(CTX, 32, 256), 'ctx', 0, 0, tiled=True)  10.7 us
    pallas_call x1, Pallas kernels, conv(): pl.pallas_call(conv_kernel, out_shape=jax.ShapeDtypeStruct((rows, width),...  9.82 us
    pallas_call x2, Pallas kernels, output(): pl.pallas_call(functools.partial(output_kernel, parts_of, len(pieces)), o...  9.77 us
  transfers between devices with their start and end apart: 27, of which 20 were waited for; matrix products, arithmetic and copies ran while one was open for 3% of the time, Pallas kernels for 20%

profile of v3, /device:TPU:8, one launch (start us, length us, event | category | flops | bytes accessed | tf_op | source)
XLA Modules:
  0.0 226.8 jit_solution(600020359220247856)
XLA Ops:
  10.7 6.6 %collective-permute-done = bf16[144,1024]{1,0:T(8,128)(2,1)S(1)} collective-permute-done((bf16[144,1024]{1,0:T(8,128)(2,1)S(1)}, bf16[144,1024]{1,0:T(8,128)(2,1)S(1)}, u32[]{:S(2)}, u32[]{:S(2)}) %collective-permute-start) | collective-permute-done | bytes 294944 | tf_op jit(solution)/shard_map/ppermute | solution.py:32
  22.1 9.4 %collective-permute-start.4 = (bf16[512,512]{1,0:T(8,128)(2,1)}, bf16[512,512]{1,0:T(8,128)(2,1)S(1)}, u32[]{:S(2)}, u32[]{:S(2)}) collective-permute-start(bf16[512,512]{1,0:T(8,128)(2,1)} %refs_0_.3), channel_id=1, source_target_pairs={{0,6},{1,7},{2,0},{3,1},{4,2},{5,3},{6,4},{7,5},{8,14},{9,15},{10,... | collective-permute-start | bytes 1572872 | tf_op jit(solution)/shard_map/ppermute | solution.py:45
  34.0 9.7 %collective-permute-start.6 = (bf16[512,512]{1,0:T(8,128)(2,1)S(1)}, bf16[512,512]{1,0:T(8,128)(2,1)S(1)}, u32[]{:S(2)}, u32[]{:S(2)}) collective-permute-start(bf16[512,512]{1,0:T(8,128)(2,1)S(1)} %collective-permute-done.1.refs_1_), channel_id=1, source_target_pairs={{0,6},{1,7},{2,0},{3,1},{4,2},{5,3},{6,4},{7,5},{8,14},{9,15},{10,... | collective-permute-start | bytes 1572872 | tf_op jit(solution)/shard_map/ppermute | solution.py:45
  43.7 3.4 %collective-permute-done.4.refs_3_ = bf16[512,512]{1,0:T(8,128)(2,1)S(1)} collective-permute-done((bf16[512,512]{1,0:T(8,128)(2,1)}, bf16[512,512]{1,0:T(8,128)(2,1)S(1)}, u32[]{:S(2)}, u32[]{:S(2)}) %collective-permute-start.4) | collective-permute-done | bytes 524320 | tf_op jit(solution)/shard_map/ppermute | solution.py:45
  47.1 9.2 %collective-permute-done.6.refs_5_ = bf16[512,512]{1,0:T(8,128)(2,1)S(1)} collective-permute-done((bf16[512,512]{1,0:T(8,128)(2,1)S(1)}, bf16[512,512]{1,0:T(8,128)(2,1)S(1)}, u32[]{:S(2)}, u32[]{:S(2)}) %collective-permute-start.6) | collective-permute-done | bytes 524320 | tf_op jit(solution)/shard_map/ppermute | solution.py:45
  56.3 3.8 %collective-permute-start.7 = (bf16[512,512]{1,0:T(8,128)(2,1)S(1)}, bf16[512,512]{1,0:T(8,128)(2,1)S(1)}, u32[]{:S(2)}, u32[]{:S(2)}) collective-permute-start(bf16[512,512]{1,0:T(8,128)(2,1)S(1)} %pad_maximum_fusion.1), channel_id=1, source_target_pairs={{0,6},{1,7},{2,0},{3,1},{4,2},{5,3},{6,4},{7,5},{8,14},{9,15},{10,... | collective-permute-start | bytes 1572872 | tf_op jit(solution)/shard_map/ppermute | solution.py:45
  61.3 8.5 %collective-permute-done.7.refs_6_.refs_7_ = bf16[512,512]{1,0:T(8,128)(2,1)S(1)} collective-permute-done((bf16[512,512]{1,0:T(8,128)(2,1)S(1)}, bf16[512,512]{1,0:T(8,128)(2,1)S(1)}, u32[]{:S(2)}, u32[]{:S(2)}) %collective-permute-start.7) | collective-permute-done | bytes 524320 | tf_op jit(solution)/shard_map/ppermute | solution.py:45
  73.5 3.4 %collective-permute-done.8.refs_8_ = bf16[8,16,512]{2,1,0:T(8,128)(2,1)S(1)} collective-permute-done((bf16[8,16,512]{2,1,0:T(8,128)(2,1)S(1)}, bf16[8,16,512]{2,1,0:T(8,128)(2,1)S(1)}, u32[]{:S(2)}, u32[]{:S(2)}) %collective-permute-start.8) | collective-permute-done | bytes 131104 | tf_op jit(solution)/shard_map/ppermute | solution.py:462
  76.8 7.4 %all-gather.7.cloned.1.call-done = bf16[16,144,1024]{2,1,0:T(8,128)(2,1)} async-done(((bf16[2,144,1024]{2,1,0:T(8,128)(2,1)}), bf16[16,144,1024]{2,1,0:T(8,128)(2,1)}) %all-gather.7.cloned.1.call-update) | async-done | bytes 4718608 | tf_op jit(solution)/shard_map/all_gather | solution.py:54
  86.6 4.5 %collective-permute-done.10 = bf16[128,512]{1,0:T(8,128)(2,1)S(1)} collective-permute-done((bf16[128,512]{1,0:T(8,128)(2,1)S(1)}, bf16[128,512]{1,0:T(8,128)(2,1)S(1)}, u32[]{:S(2)}, u32[]{:S(2)}) %collective-permute-start.10) | collective-permute-done | bytes 131104 | tf_op jit(solution)/shard_map/ppermute | solution.py:32
  92.6 10.7 %project2.1 = (bf16[512,512]{1,0:T(8,128)(2,1)}, bf16[32,32,256]{2,1,0:T(8,128)(2,1)}) custom-call(bf16[512,512]{1,0:T(8,128)(2,1)} %refs_0_.3, bf16[512,512]{1,0:T(8,128)(2,1)} %copy-done.5, bf16[512,512]{1,0:T(8,128)(2,1)} %copy-done.2, bf16[512,512]{1,0:T(8,128)(2,1)} %copy-done, bf16[512,512]{1,0:T(8,128)(2,1)} %copy-done.3, bf16[512,512]{1,0:T(8,128)(2,1)} %copy-done.1, ...), custom_call_target="tpu_custom_call" | custom-call | tf_op jit(solution)/shard_map/project2/pallas_call | solution.py:212
  103.3 4.9 %all-to-all-start = ((bf16[32,32,256]{2,1,0:T(8,128)(2,1)}), bf16[32,32,256]{2,1,0:T(8,128)(2,1)S(1)}, u32[]{:S(2)}, u32[]{:S(2)}) async-start(bf16[32,32,256]{2,1,0:T(8,128)(2,1)} %get-tuple-element.45), calls=%async_computation | async-start | bytes 1048576 | tf_op jit(solution)/shard_map/all_to_all | solution.py:482
  110.3 9.0 %toeplitz.1 = bf16[64,256,256]{2,1,0:T(8,128)(2,1)} custom-call(bf16[8,2,144,1024]{3,2,1,0:T(8,128)(2,1)} %bitcast.24, bf16[8,2,144,1024]{3,2,1,0:T(8,128)(2,1)} %collective-permute-done.11.refs_10_.other), custom_call_target="tpu_custom_call" | custom-call | tf_op jit(solution)/shard_map/toeplitz/pallas_call | solution.py:285
  121.8 9.2 %all-to-all-done = bf16[32,32,256]{2,1,0:T(8,128)(2,1)S(1)} async-done(((bf16[32,32,256]{2,1,0:T(8,128)(2,1)}), bf16[32,32,256]{2,1,0:T(8,128)(2,1)S(1)}, u32[]{:S(2)}, u32[]{:S(2)}) %all-to-all-start) | async-done | bytes 524320 | tf_op jit(solution)/shard_map/all_to_all | solution.py:482
  131.9 9.8 %conv.1 = bf16[1024,256]{1,0:T(8,128)(2,1)} custom-call(bf16[1024,256]{1,0:T(8,128)(2,1)} %bitcast.27, bf16[16384,256]{1,0:T(8,128)(2,1)} %bitcast.21), custom_call_target="tpu_custom_call" | custom-call | tf_op jit(solution)/shard_map/conv/pallas_call | solution.py:340
  143.1 5.6 %all-to-all-start.1 = ((bf16[32,32,256]{2,1,0:T(8,128)(2,1)}), bf16[32,32,256]{2,1,0:T(8,128)(2,1)S(1)}, u32[]{:S(2)}, u32[]{:S(2)}) async-start(bf16[32,32,256]{2,1,0:T(8,128)(2,1)} %bitcast.28), calls=%async_computation.1 | async-start | bytes 1048576 | tf_op jit(solution)/shard_map/all_to_all | solution.py:487
  149.3 9.5 %project1.1.query_ref = f32[512,512]{1,0:T(8,128)} custom-call(bf16[512,512]{1,0:T(8,128)(2,1)} %refs_0_.3, bf16[512,512]{1,0:T(8,128)(2,1)} %copy-done.5, bf16[512,512]{1,0:T(8,128)(2,1)} %copy-done.2, bf16[512,512]{1,0:T(8,128)(2,1)} %copy-done, bf16[512,512]{1,0:T(8,128)(2,1)} %copy-done.3, bf16[512,512]{1,0:T(8,128)(2,1)} %copy-done.1, ...), custom_call_target="tpu_custom_call" | custom-call | tf_op jit(solution)/shard_map/project1/pallas_call | solution.py:212
  158.8 10.7 %all-to-all-done.1.back_ref = bf16[32,32,256]{2,1,0:T(8,128)(2,1)S(1)} async-done(((bf16[32,32,256]{2,1,0:T(8,128)(2,1)}), bf16[32,32,256]{2,1,0:T(8,128)(2,1)S(1)}, u32[]{:S(2)}, u32[]{:S(2)}) %all-to-all-start.1) | async-done | bytes 524320 | tf_op jit(solution)/shard_map/all_to_all | solution.py:487
  176.2 9.3 %collective-permute-done.16.refs_1_ = bf16[512,512]{1,0:T(8,128)(2,1)S(1)} collective-permute-done((bf16[512,512]{1,0:T(8,128)(2,1)S(1)}, bf16[512,512]{1,0:T(8,128)(2,1)S(1)}, u32[]{:S(2)}, u32[]{:S(2)}) %collective-permute-start.16) | collective-permute-done | bytes 524320 | tf_op jit(solution)/shard_map/ppermute | solution.py:49
  189.7 8.2 %collective-permute-done.20.refs_5_ = bf16[512,512]{1,0:T(8,128)(2,1)S(1)} collective-permute-done((bf16[512,512]{1,0:T(8,128)(2,1)S(1)}, bf16[512,512]{1,0:T(8,128)(2,1)S(1)}, u32[]{:S(2)}, u32[]{:S(2)}) %collective-permute-start.20) | collective-permute-done | bytes 524320 | tf_op jit(solution)/shard_map/ppermute | solution.py:45
  198.9 3.7 %collective-permute-start.21 = (bf16[512,512]{1,0:T(8,128)(2,1)}, bf16[512,512]{1,0:T(8,128)(2,1)}, u32[]{:S(2)}, u32[]{:S(2)}) collective-permute-start(bf16[512,512]{1,0:T(8,128)(2,1)} %pad_maximum_fusion.5), channel_id=1, source_target_pairs={{0,6},{1,7},{2,0},{3,1},{4,2},{5,3},{6,4},{7,5},{8,14},{9,15},{10,... | collective-permute-start | bytes 1572872 | tf_op jit(solution)/shard_map/ppermute | solution.py:45
  203.8 5.5 %output6.1.refs_3_ = f32[512,512]{1,0:T(8,128)} custom-call(bf16[512,512]{1,0:T(8,128)(2,1)} %copy-done.8, bf16[512,512]{1,0:T(8,128)(2,1)} %copy-done.17, bf16[512,512]{1,0:T(8,128)(2,1)} %copy-done.13, bf16[512,512]{1,0:T(8,128)(2,1)} %copy-done.12, bf16[512,512]{1,0:T(8,128)(2,1)} %copy-done.15, bf16[512,512]{1,0:T(8,128)(2,1)} %copy-done.14, ...), custom_call_target="tpu_custom_call" | custom-call | tf_op jit(solution)/shard_map/output6/pallas_call | solution.py:427
  209.3 3.4 %collective-permute-done.21.refs_1_ = bf16[512,512]{1,0:T(8,128)(2,1)} collective-permute-done((bf16[512,512]{1,0:T(8,128)(2,1)}, bf16[512,512]{1,0:T(8,128)(2,1)}, u32[]{:S(2)}, u32[]{:S(2)}) %collective-permute-start.21) | collective-permute-done | bytes 524320 | tf_op jit(solution)/shard_map/ppermute | solution.py:45
  216.0 4.2 %output2.1 = bf16[512,512]{1,0:T(8,128)(2,1)} custom-call(bf16[512,512]{1,0:T(8,128)(2,1)} %collective-permute-done.18.refs_0_, bf16[512,512]{1,0:T(8,128)(2,1)} %collective-permute-done.21.refs_1_, bf16[8,4,512,128]{3,2,1,0:T(8,128)(2,1)} %bitcast.26, f32[512,512]{1,0:T(8,128)} %output6.1.refs_3_), custom_call_target="tpu_custom_call" | custom-call | tf_op jit(solution)/shard_map/output2/pallas_call | solution.py:427
  (101 shorter events, 43.8 us)
Async XLA Ops:
  6.5 77.6 %all-gather.7.cloned.1.call-start = ((), (), s32[]{:S(2)}) async-start(), calls=%async_computation.2 | async-start | bytes 5308416 | tf_op jit(solution)/shard_map/all_gather | solution.py:54
  8.4 8.8 %collective-permute-start = (bf16[144,1024]{1,0:T(8,128)(2,1)S(1)}, bf16[144,1024]{1,0:T(8,128)(2,1)S(1)}, u32[]{:S(2)}, u32[]{:S(2)}) collective-permute-start(bf16[144,1024]{1,0:T(8,128)(2,1)S(1)} %get-tuple-element.58), channel_id=1, source_target_pairs={{0,16},{8,24},{16,0},{24,8},{32,48},{40,56},{48,32},{56,40},{64,80... | collective-permute-start | bytes 884744 | tf_op jit(solution)/shard_map/ppermute | solution.py:32
  18.2 124.8 %all-gather.9.cloned.1.call-start = ((), (), s32[]{:S(2)}) async-start(), calls=%async_computation.3 | async-start | bytes 2359296 | tf_op jit(solution)/shard_map/all_gather | solution.py:54
  18.2 15.8 %collective-permute-start.1 = (bf16[512,512]{1,0:T(8,128)(2,1)}, bf16[512,512]{1,0:T(8,128)(2,1)S(1)}, u32[]{:S(2)}, u32[]{:S(2)}) collective-permute-start(bf16[512,512]{1,0:T(8,128)(2,1)} %refs_0_.3), channel_id=1, source_target_pairs={{0,1},{1,0},{2,3},{3,2},{4,5},{5,4},{6,7},{7,6},{8,9},{9,8},{10,11... | collective-permute-start | bytes 1572872 | tf_op jit(solution)/shard_map/ppermute | solution.py:49
  20.6 11.0 %collective-permute-start.2 = (bf16[512,128]{1,0:T(8,128)(2,1)}, bf16[512,128]{1,0:T(8,128)(2,1)S(1)}, u32[]{:S(2)}, u32[]{:S(2)}) collective-permute-start(bf16[512,128]{1,0:T(8,128)(2,1)} %param.11), channel_id=1, source_target_pairs={{0,0},{1,32},{2,64},{3,96},{4,128},{5,160},{6,192},{7,224},{8,8},{... | collective-permute-start | bytes 393224 | tf_op jit(solution)/shard_map/ppermute | solution.py:459
  22.1 24.9 %collective-permute-start.4 = (bf16[512,512]{1,0:T(8,128)(2,1)}, bf16[512,512]{1,0:T(8,128)(2,1)S(1)}, u32[]{:S(2)}, u32[]{:S(2)}) collective-permute-start(bf16[512,512]{1,0:T(8,128)(2,1)} %refs_0_.3), channel_id=1, source_target_pairs={{0,6},{1,7},{2,0},{3,1},{4,2},{5,3},{6,4},{7,5},{8,14},{9,15},{10,... | collective-permute-start | bytes 1572872 | tf_op jit(solution)/shard_map/ppermute | solution.py:45
  34.0 22.2 %collective-permute-start.6 = (bf16[512,512]{1,0:T(8,128)(2,1)S(1)}, bf16[512,512]{1,0:T(8,128)(2,1)S(1)}, u32[]{:S(2)}, u32[]{:S(2)}) collective-permute-start(bf16[512,512]{1,0:T(8,128)(2,1)S(1)} %collective-permute-done.1.refs_1_), channel_id=1, source_target_pairs={{0,6},{1,7},{2,0},{3,1},{4,2},{5,3},{6,4},{7,5},{8,14},{9,15},{10,... | collective-permute-start | bytes 1572872 | tf_op jit(solution)/shard_map/ppermute | solution.py:45
  43.7 16.4 %collective-permute-start.3 = (bf16[512,512]{1,0:T(8,128)(2,1)}, bf16[512,512]{1,0:T(8,128)(2,1)S(1)}, u32[]{:S(2)}, u32[]{:S(2)}) collective-permute-start(bf16[512,512]{1,0:T(8,128)(2,1)} %refs_0_.3), channel_id=1, source_target_pairs={{0,2},{1,3},{2,4},{3,5},{4,6},{5,7},{6,0},{7,1},{8,10},{9,11},{10,... | collective-permute-start | bytes 1572872 | tf_op jit(solution)/shard_map/ppermute | solution.py:45
  43.7 16.4 %collective-permute-start.5 = (bf16[512,512]{1,0:T(8,128)(2,1)S(1)}, bf16[512,512]{1,0:T(8,128)(2,1)S(1)}, u32[]{:S(2)}, u32[]{:S(2)}) collective-permute-start(bf16[512,512]{1,0:T(8,128)(2,1)S(1)} %collective-permute-done.1.refs_1_), channel_id=1, source_target_pairs={{0,2},{1,3},{2,4},{3,5},{4,6},{5,7},{6,0},{7,1},{8,10},{9,11},{10,... | collective-permute-start | bytes 1572872 | tf_op jit(solution)/shard_map/ppermute | solution.py:45
  56.3 13.4 %collective-permute-start.7 = (bf16[512,512]{1,0:T(8,128)(2,1)S(1)}, bf16[512,512]{1,0:T(8,128)(2,1)S(1)}, u32[]{:S(2)}, u32[]{:S(2)}) collective-permute-start(bf16[512,512]{1,0:T(8,128)(2,1)S(1)} %pad_maximum_fusion.1), channel_id=1, source_target_pairs={{0,6},{1,7},{2,0},{3,1},{4,2},{5,3},{6,4},{7,5},{8,14},{9,15},{10,... | collective-permute-start | bytes 1572872 | tf_op jit(solution)/shard_map/ppermute | solution.py:45
  60.2 13.2 %collective-permute-start.9 = (bf16[512,512]{1,0:T(8,128)(2,1)S(1)}, bf16[512,512]{1,0:T(8,128)(2,1)}, u32[]{:S(2)}, u32[]{:S(2)}) collective-permute-start(bf16[512,512]{1,0:T(8,128)(2,1)S(1)} %pad_maximum_fusion.2), channel_id=1, source_target_pairs={{0,2},{1,3},{2,4},{3,5},{4,6},{5,7},{6,0},{7,1},{8,10},{9,11},{10,... | collective-permute-start | bytes 1572872 | tf_op jit(solution)/shard_map/ppermute | solution.py:45
  84.2 8.3 %collective-permute-start.11 = (bf16[8,2,144,1024]{3,2,1,0:T(8,128)(2,1)}, bf16[8,2,144,1024]{3,2,1,0:T(8,128)(2,1)}, u32[]{:S(2)}, u32[]{:S(2)}) collective-permute-start(bf16[8,2,144,1024]{3,2,1,0:T(8,128)(2,1)} %bitcast.22), channel_id=1, source_target_pairs={{0,8},{8,0},{16,24},{24,16},{32,40},{40,32},{48,56},{56,48},{64,72... | collective-permute-start | bytes 14155784 | tf_op jit(solution)/shard_map/ppermute | solution.py:32
  103.3 27.8 %all-to-all-start = ((bf16[32,32,256]{2,1,0:T(8,128)(2,1)}), bf16[32,32,256]{2,1,0:T(8,128)(2,1)S(1)}, u32[]{:S(2)}, u32[]{:S(2)}) async-start(bf16[32,32,256]{2,1,0:T(8,128)(2,1)} %get-tuple-element.45), calls=%async_computation | async-start | bytes 1048576 | tf_op jit(solution)/shard_map/all_to_all | solution.py:482
  108.2 95.6 %all-gather.11.cloned.1.call-start = ((), (), s32[]{:S(2)}) async-start(), calls=%async_computation.4 | async-start | bytes 4718592 | tf_op jit(solution)/shard_map/all_gather | solution.py:54
  109.9 11.1 %collective-permute-start.13 = (bf16[2,512,128]{2,1,0:T(8,128)(2,1)S(1)}, bf16[2,512,128]{2,1,0:T(8,128)(2,1)S(1)}, u32[]{:S(2)}, u32[]{:S(2)}) collective-permute-start(bf16[2,512,128]{2,1,0:T(8,128)(2,1)S(1)} %pad_maximum_fusion.7), channel_id=1, source_target_pairs={{0,16},{8,24},{16,0},{24,8},{32,48},{40,56},{48,32},{56,40},{64,80... | collective-permute-start | bytes 786440 | tf_op jit(solution)/shard_map/ppermute | solution.py:32
  143.0 6.3 %collective-permute-start.14 = (bf16[8,2,128,512]{3,2,1,0:T(8,128)(2,1)}, bf16[8,2,128,512]{3,2,1,0:T(8,128)(2,1)}, u32[]{:S(2)}, u32[]{:S(2)}) collective-permute-start(bf16[8,2,128,512]{3,2,1,0:T(8,128)(2,1)} %bitcast.29), channel_id=1, source_target_pairs={{0,8},{8,0},{16,24},{24,16},{32,40},{40,32},{48,56},{56,48},{64,72... | collective-permute-start | bytes 6291464 | tf_op jit(solution)/shard_map/ppermute | solution.py:32
  143.1 26.4 %all-to-all-start.1 = ((bf16[32,32,256]{2,1,0:T(8,128)(2,1)}), bf16[32,32,256]{2,1,0:T(8,128)(2,1)S(1)}, u32[]{:S(2)}, u32[]{:S(2)}) async-start(bf16[32,32,256]{2,1,0:T(8,128)(2,1)} %bitcast.28), calls=%async_computation.1 | async-start | bytes 1048576 | tf_op jit(solution)/shard_map/all_to_all | solution.py:487
  171.0 14.5 %collective-permute-start.16 = (bf16[512,512]{1,0:T(8,128)(2,1)S(1)}, bf16[512,512]{1,0:T(8,128)(2,1)S(1)}, u32[]{:S(2)}, u32[]{:S(2)}) collective-permute-start(bf16[512,512]{1,0:T(8,128)(2,1)S(1)} %gate.1.refs_0_), channel_id=1, source_target_pairs={{0,1},{1,0},{2,3},{3,2},{4,5},{5,4},{6,7},{7,6},{8,9},{9,8},{10,11... | collective-permute-start | bytes 1572872 | tf_op jit(solution)/shard_map/ppermute | solution.py:49
  173.0 15.4 %collective-permute-start.19 = (bf16[512,512]{1,0:T(8,128)(2,1)S(1)}, bf16[512,512]{1,0:T(8,128)(2,1)S(1)}, u32[]{:S(2)}, u32[]{:S(2)}) collective-permute-start(bf16[512,512]{1,0:T(8,128)(2,1)S(1)} %gate.1.refs_0_), channel_id=1, source_target_pairs={{0,6},{1,7},{2,0},{3,1},{4,2},{5,3},{6,4},{7,5},{8,14},{9,15},{10,... | collective-permute-start | bytes 1572872 | tf_op jit(solution)/shard_map/ppermute | solution.py:45
  176.2 13.5 %collective-permute-start.15 = (bf16[512,512]{1,0:T(8,128)(2,1)S(1)}, bf16[512,512]{1,0:T(8,128)(2,1)S(1)}, u32[]{:S(2)}, u32[]{:S(2)}) collective-permute-start(bf16[512,512]{1,0:T(8,128)(2,1)S(1)} %gate.1.refs_0_), channel_id=1, source_target_pairs={{0,2},{1,3},{2,4},{3,5},{4,6},{5,7},{6,0},{7,1},{8,10},{9,11},{10,... | collective-permute-start | bytes 1572872 | tf_op jit(solution)/shard_map/ppermute | solution.py:45
  185.5 12.4 %collective-permute-start.20 = (bf16[512,512]{1,0:T(8,128)(2,1)S(1)}, bf16[512,512]{1,0:T(8,128)(2,1)S(1)}, u32[]{:S(2)}, u32[]{:S(2)}) collective-permute-start(bf16[512,512]{1,0:T(8,128)(2,1)S(1)} %collective-permute-done.16.refs_1_), channel_id=1, source_target_pairs={{0,6},{1,7},{2,0},{3,1},{4,2},{5,3},{6,4},{7,5},{8,14},{9,15},{10,... | collective-permute-start | bytes 1572872 | tf_op jit(solution)/shard_map/ppermute | solution.py:45
  188.4 14.2 %collective-permute-start.17 = (bf16[512,512]{1,0:T(8,128)(2,1)S(1)}, bf16[512,512]{1,0:T(8,128)(2,1)S(1)}, u32[]{:S(2)}, u32[]{:S(2)}) collective-permute-start(bf16[512,512]{1,0:T(8,128)(2,1)S(1)} %collective-permute-done.16.refs_1_), channel_id=1, source_target_pairs={{0,2},{1,3},{2,4},{3,5},{4,6},{5,7},{6,0},{7,1},{8,10},{9,11},{10,... | collective-permute-start | bytes 1572872 | tf_op jit(solution)/shard_map/ppermute | solution.py:45
  198.9 13.9 %collective-permute-start.21 = (bf16[512,512]{1,0:T(8,128)(2,1)}, bf16[512,512]{1,0:T(8,128)(2,1)}, u32[]{:S(2)}, u32[]{:S(2)}) collective-permute-start(bf16[512,512]{1,0:T(8,128)(2,1)} %pad_maximum_fusion.5), channel_id=1, source_target_pairs={{0,6},{1,7},{2,0},{3,1},{4,2},{5,3},{6,4},{7,5},{8,14},{9,15},{10,... | collective-permute-start | bytes 1572872 | tf_op jit(solution)/shard_map/ppermute | solution.py:45
  203.5 12.5 %collective-permute-start.18 = (bf16[512,512]{1,0:T(8,128)(2,1)}, bf16[512,512]{1,0:T(8,128)(2,1)}, u32[]{:S(2)}, u32[]{:S(2)}) collective-permute-start(bf16[512,512]{1,0:T(8,128)(2,1)} %pad_maximum_fusion.4), channel_id=1, source_target_pairs={{0,2},{1,3},{2,4},{3,5},{4,6},{5,7},{6,0},{7,1},{8,10},{9,11},{10,... | collective-permute-start | bytes 1572872 | tf_op jit(solution)/shard_map/ppermute | solution.py:45
  (22 other events, 502.4 us)
Sparse Core Ops, SparseCore 0:
  18.3 65.8 all-gather.6
  92.0 50.8 all-gather.8
  144.8 58.9 all-gather.10

commit v4 on v3

--- a/solution.py
+++ b/solution.py
@@ -376,21 +376,24 @@
     me = lax.axis_index("tp")
     x, y = me // 2, me % 2
     offsets = [(0, 0), (0, 1), (-1, 0), (1, 0), (-1, 1), (1, 1)]
+    rows = pieces[0].shape[0]
     parts = []
-    for ref, (dx, dy) in zip(pieces, offsets):
-        parts.append((((x + dx + NX) % NX) * 2 + (y + dy) % 2, [(ref, 0)]))
+    for k, (dx, dy) in enumerate(offsets):
+        there = ((x + dx + NX) % NX) * 2 + (y + dy) % 2
+        parts.append((there, [(pieces[k], 0), (pieces[6 + k], rows)]))
     return parts
 
 
 def far_parts(pieces):
     me = lax.axis_index("tp")
     x, y = me // 2, me % 2
-    half = pieces[0].shape[0] // 2
+    count = pieces[0].shape[0] // 2
     parts = []
     for dy in (0, 1):
-        rows = pl.ds(dy * half, half)
+        rows = pl.ds(dy * count, count)
         there = ((x + 2) % NX) * 2 + (y + dy) % 2
-        parts.append((there, [(pieces[0].at[rows], 0), (pieces[1].at[rows], half)]))
+        sources = [(piece.at[rows], k * count) for k, piece in enumerate(pieces)]
+        parts.append((there, sources))
     return parts
 
 
@@ -422,7 +425,7 @@
 
 
 def output(pieces, parts_of, parts, weights, start, dtype):
-    rows = pieces[0].shape[0]
+    rows = 2 * pieces[0].shape[0]
     depth, width = weights.shape[2:]
     return pl.pallas_call(
         functools.partial(output_kernel, parts_of, len(pieces)),
@@ -495,9 +498,10 @@
     )
     gated = gate(back, mixed, query, skip[None, :])
 
-    gathered = gather_tp(gated)[0]
-    total = output(gathered[:6], near_parts, 6, o_mine, [], F32)
-    return output(gathered[6:], far_parts, 2, o_mine, [total], BF16)
+    half = rows // 2
+    first, second = gather_tp(gated[:half])[0], gather_tp(gated[half:])[0]
+    total = output(first[:6] + second[:6], near_parts, 6, o_mine, [], F32)
+    return output(first[6:] + second[6:], far_parts, 2, o_mine, [total], BF16)
 
 
 def solution(mesh):

time: 227 us -> 226 us (level)
  waiting for transfers between devices: 95.9 us -> 80.3 us
  starting transfers between devices: 57 us -> 68.8 us
    ppermute x12 -> x18, starting transfers between devices: 33.8 us -> 44 us  [shift_x(): return lax.ppermute(block, 'tp', route)]
    ppermute x12 -> x18, waiting for transfers between devices: 38.2 us -> 30.5 us  [shift_x(): return lax.ppermute(block, 'tp', route)]
    ppermute x2 -> x3, waiting for transfers between devices: 11.8 us -> 5.23 us  [swap_yhi(): return lax.ppermute(block, 'tp', [(j, j ^ 1) for j in range(TP)])]
    ppermute x2 -> x3, starting transfers between devices: 4.36 us -> 6 us  [swap_yhi(): return lax.ppermute(block, 'tp', [(j, j ^ 1) for j in range(TP)])]
  transfers between devices with their start and end apart: 27 -> 34, of which waited for: 20 -> 20; matrix products, arithmetic and copies ran while one was open for 3% -> 3% of each run, Pallas kernels for 20% -> 20%
where the time goes in v4:
time: 226 us; the launch traced here: 225 us
  waiting for transfers between devices  80.3 us (36%)
  starting transfers between devices  68.8 us (30%)
  Pallas kernels  49.3 us (22%)
  between operations  13.6 us (6%)
  local copies, waits for them, and re-layouts  8.19 us (4%)
  other arithmetic  4.98 us (2%)
    ppermute x18, starting transfers between devices, shift_x(): return lax.ppermute(block, 'tp', route)  44 us
    ppermute x18, waiting for transfers between devices, shift_x(): return lax.ppermute(block, 'tp', route)  30.5 us
    pallas_call x2, Pallas kernels, project(): pl.pallas_call(functools.partial(project_kernel, n_proj, len(out_shapes),...  20.2 us
    ppermute x6, waiting for transfers between devices, swap_ctx(): return lax.ppermute(block, 'ctx', [(i, i ^ mask) for i in range(CTX)])  13.9 us
    pallas_call x2, Pallas kernels, output(): pl.pallas_call(functools.partial(output_kernel, parts_of, len(pieces)), o...  9.89 us
    pallas_call x1, Pallas kernels, conv(): pl.pallas_call(conv_kernel, out_shape=jax.ShapeDtypeStruct((rows, width),...  9.81 us
    all_to_all x1, waiting for transfers between devices, local(): back = lax.all_to_all(result.reshape(CTX, 32, 256), 'ctx', 0, 0, tiled=True)  9.39 us
    all_to_all x1, waiting for transfers between devices, local(): sent = lax.all_to_all(blocks, 'ctx', 0, 0, tiled=True)  9.21 us
  transfers between devices with their start and end apart: 34, of which 20 were waited for; matrix products, arithmetic and copies ran while one was open for 3% of the time, Pallas kernels for 20%

profile of v4, /device:TPU:8, one launch (start us, length us, event | category | flops | bytes accessed | tf_op | source)
XLA Modules:
  0.0 225.1 jit_solution(14844709578472405230)
XLA Ops:
  10.7 6.6 %collective-permute-done = bf16[144,1024]{1,0:T(8,128)(2,1)S(1)} collective-permute-done((bf16[144,1024]{1,0:T(8,128)(2,1)S(1)}, bf16[144,1024]{1,0:T(8,128)(2,1)S(1)}, u32[]{:S(2)}, u32[]{:S(2)}) %collective-permute-start) | collective-permute-done | bytes 294944 | tf_op jit(solution)/shard_map/ppermute | solution.py:32
  22.2 9.4 %collective-permute-start.4 = (bf16[512,512]{1,0:T(8,128)(2,1)}, bf16[512,512]{1,0:T(8,128)(2,1)S(1)}, u32[]{:S(2)}, u32[]{:S(2)}) collective-permute-start(bf16[512,512]{1,0:T(8,128)(2,1)} %refs_0_.3), channel_id=1, source_target_pairs={{0,6},{1,7},{2,0},{3,1},{4,2},{5,3},{6,4},{7,5},{8,14},{9,15},{10,... | collective-permute-start | bytes 1572872 | tf_op jit(solution)/shard_map/ppermute | solution.py:45
  34.0 9.7 %collective-permute-start.6 = (bf16[512,512]{1,0:T(8,128)(2,1)S(1)}, bf16[512,512]{1,0:T(8,128)(2,1)S(1)}, u32[]{:S(2)}, u32[]{:S(2)}) collective-permute-start(bf16[512,512]{1,0:T(8,128)(2,1)S(1)} %collective-permute-done.1.refs_1_), channel_id=1, source_target_pairs={{0,6},{1,7},{2,0},{3,1},{4,2},{5,3},{6,4},{7,5},{8,14},{9,15},{10,... | collective-permute-start | bytes 1572872 | tf_op jit(solution)/shard_map/ppermute | solution.py:45
  43.7 3.4 %collective-permute-done.4.refs_3_ = bf16[512,512]{1,0:T(8,128)(2,1)S(1)} collective-permute-done((bf16[512,512]{1,0:T(8,128)(2,1)}, bf16[512,512]{1,0:T(8,128)(2,1)S(1)}, u32[]{:S(2)}, u32[]{:S(2)}) %collective-permute-start.4) | collective-permute-done | bytes 524320 | tf_op jit(solution)/shard_map/ppermute | solution.py:45
  47.1 9.2 %collective-permute-done.6.refs_5_ = bf16[512,512]{1,0:T(8,128)(2,1)S(1)} collective-permute-done((bf16[512,512]{1,0:T(8,128)(2,1)S(1)}, bf16[512,512]{1,0:T(8,128)(2,1)S(1)}, u32[]{:S(2)}, u32[]{:S(2)}) %collective-permute-start.6) | collective-permute-done | bytes 524320 | tf_op jit(solution)/shard_map/ppermute | solution.py:45
  56.4 3.8 %collective-permute-start.7 = (bf16[512,512]{1,0:T(8,128)(2,1)S(1)}, bf16[512,512]{1,0:T(8,128)(2,1)S(1)}, u32[]{:S(2)}, u32[]{:S(2)}) collective-permute-start(bf16[512,512]{1,0:T(8,128)(2,1)S(1)} %pad_maximum_fusion.1), channel_id=1, source_target_pairs={{0,6},{1,7},{2,0},{3,1},{4,2},{5,3},{6,4},{7,5},{8,14},{9,15},{10,... | collective-permute-start | bytes 1572872 | tf_op jit(solution)/shard_map/ppermute | solution.py:45
  61.3 8.5 %collective-permute-done.7.refs_6_.refs_7_ = bf16[512,512]{1,0:T(8,128)(2,1)S(1)} collective-permute-done((bf16[512,512]{1,0:T(8,128)(2,1)S(1)}, bf16[512,512]{1,0:T(8,128)(2,1)S(1)}, u32[]{:S(2)}, u32[]{:S(2)}) %collective-permute-start.7) | collective-permute-done | bytes 524320 | tf_op jit(solution)/shard_map/ppermute | solution.py:45
  73.5 3.4 %collective-permute-done.8.refs_8_ = bf16[8,16,512]{2,1,0:T(8,128)(2,1)S(1)} collective-permute-done((bf16[8,16,512]{2,1,0:T(8,128)(2,1)S(1)}, bf16[8,16,512]{2,1,0:T(8,128)(2,1)S(1)}, u32[]{:S(2)}, u32[]{:S(2)}) %collective-permute-start.8) | collective-permute-done | bytes 131104 | tf_op jit(solution)/shard_map/ppermute | solution.py:465
  76.9 7.3 %all-gather.7.cloned.1.call-done = bf16[16,144,1024]{2,1,0:T(8,128)(2,1)} async-done(((bf16[2,144,1024]{2,1,0:T(8,128)(2,1)}), bf16[16,144,1024]{2,1,0:T(8,128)(2,1)}) %all-gather.7.cloned.1.call-update) | async-done | bytes 4718608 | tf_op jit(solution)/shard_map/all_gather | solution.py:54
  86.6 4.5 %collective-permute-done.10 = bf16[128,512]{1,0:T(8,128)(2,1)S(1)} collective-permute-done((bf16[128,512]{1,0:T(8,128)(2,1)S(1)}, bf16[128,512]{1,0:T(8,128)(2,1)S(1)}, u32[]{:S(2)}, u32[]{:S(2)}) %collective-permute-start.10) | collective-permute-done | bytes 131104 | tf_op jit(solution)/shard_map/ppermute | solution.py:32
  92.6 10.7 %project2.1 = (bf16[512,512]{1,0:T(8,128)(2,1)}, bf16[32,32,256]{2,1,0:T(8,128)(2,1)}) custom-call(bf16[512,512]{1,0:T(8,128)(2,1)} %refs_0_.3, bf16[512,512]{1,0:T(8,128)(2,1)} %copy-done.5, bf16[512,512]{1,0:T(8,128)(2,1)} %copy-done.2, bf16[512,512]{1,0:T(8,128)(2,1)} %copy-done, bf16[512,512]{1,0:T(8,128)(2,1)} %copy-done.3, bf16[512,512]{1,0:T(8,128)(2,1)} %copy-done.1, ...), custom_call_target="tpu_custom_call" | custom-call | tf_op jit(solution)/shard_map/project2/pallas_call | solution.py:212
  103.3 4.9 %all-to-all-start = ((bf16[32,32,256]{2,1,0:T(8,128)(2,1)}), bf16[32,32,256]{2,1,0:T(8,128)(2,1)S(1)}, u32[]{:S(2)}, u32[]{:S(2)}) async-start(bf16[32,32,256]{2,1,0:T(8,128)(2,1)} %get-tuple-element.45), calls=%async_computation | async-start | bytes 1048576 | tf_op jit(solution)/shard_map/all_to_all | solution.py:485
  110.3 9.0 %toeplitz.1 = bf16[64,256,256]{2,1,0:T(8,128)(2,1)} custom-call(bf16[8,2,144,1024]{3,2,1,0:T(8,128)(2,1)} %bitcast.24, bf16[8,2,144,1024]{3,2,1,0:T(8,128)(2,1)} %collective-permute-done.11.refs_10_.other), custom_call_target="tpu_custom_call" | custom-call | tf_op jit(solution)/shard_map/toeplitz/pallas_call | solution.py:285
  121.8 9.2 %all-to-all-done = bf16[32,32,256]{2,1,0:T(8,128)(2,1)S(1)} async-done(((bf16[32,32,256]{2,1,0:T(8,128)(2,1)}), bf16[32,32,256]{2,1,0:T(8,128)(2,1)S(1)}, u32[]{:S(2)}, u32[]{:S(2)}) %all-to-all-start) | async-done | bytes 524320 | tf_op jit(solution)/shard_map/all_to_all | solution.py:485
  131.8 9.8 %conv.1 = bf16[1024,256]{1,0:T(8,128)(2,1)} custom-call(bf16[1024,256]{1,0:T(8,128)(2,1)} %bitcast.27, bf16[16384,256]{1,0:T(8,128)(2,1)} %bitcast.21), custom_call_target="tpu_custom_call" | custom-call | tf_op jit(solution)/shard_map/conv/pallas_call | solution.py:340
  143.1 5.6 %all-to-all-start.1 = ((bf16[32,32,256]{2,1,0:T(8,128)(2,1)}), bf16[32,32,256]{2,1,0:T(8,128)(2,1)S(1)}, u32[]{:S(2)}, u32[]{:S(2)}) async-start(bf16[32,32,256]{2,1,0:T(8,128)(2,1)} %bitcast.28), calls=%async_computation.1 | async-start | bytes 1048576 | tf_op jit(solution)/shard_map/all_to_all | solution.py:490
  150.7 9.5 %project1.1.query_ref = f32[512,512]{1,0:T(8,128)} custom-call(bf16[512,512]{1,0:T(8,128)(2,1)} %refs_0_.3, bf16[512,512]{1,0:T(8,128)(2,1)} %copy-done.5, bf16[512,512]{1,0:T(8,128)(2,1)} %copy-done.2, bf16[512,512]{1,0:T(8,128)(2,1)} %copy-done, bf16[512,512]{1,0:T(8,128)(2,1)} %copy-done.3, bf16[512,512]{1,0:T(8,128)(2,1)} %copy-done.1, ...), custom_call_target="tpu_custom_call" | custom-call | tf_op jit(solution)/shard_map/project1/pallas_call | solution.py:212
  160.2 9.4 %all-to-all-done.1.back_ref = bf16[32,32,256]{2,1,0:T(8,128)(2,1)S(1)} async-done(((bf16[32,32,256]{2,1,0:T(8,128)(2,1)}), bf16[32,32,256]{2,1,0:T(8,128)(2,1)S(1)}, u32[]{:S(2)}, u32[]{:S(2)}) %all-to-all-start.1) | async-done | bytes 524320 | tf_op jit(solution)/shard_map/all_to_all | solution.py:490
  177.9 3.3 %collective-permute-start.19 = (bf16[256,512]{1,0:T(8,128)(2,1)S(1)}, bf16[256,512]{1,0:T(8,128)(2,1)S(1)}, u32[]{:S(2)}, u32[]{:S(2)}) collective-permute-start(bf16[256,512]{1,0:T(8,128)(2,1)S(1)} %get-tuple-element.54.refs_0_), channel_id=1, source_target_pairs={{0,6},{1,7},{2,0},{3,1},{4,2},{5,3},{6,4},{7,5},{8,14},{9,15},{10,... | collective-permute-start | bytes 786440 | tf_op jit(solution)/shard_map/ppermute | solution.py:45
  185.6 2.9 %collective-permute-start.27 = (bf16[256,512]{1,0:T(8,128)(2,1)S(1)}, bf16[256,512]{1,0:T(8,128)(2,1)S(1)}, u32[]{:S(2)}, u32[]{:S(2)}) collective-permute-start(bf16[256,512]{1,0:T(8,128)(2,1)S(1)} %collective-permute-done.23.refs_7_), channel_id=1, source_target_pairs={{0,6},{1,7},{2,0},{3,1},{4,2},{5,3},{6,4},{7,5},{8,14},{9,15},{10,... | collective-permute-start | bytes 786440 | tf_op jit(solution)/shard_map/ppermute | solution.py:45
  188.5 3.7 %collective-permute-start.20 = (bf16[256,512]{1,0:T(8,128)(2,1)S(1)}, bf16[256,512]{1,0:T(8,128)(2,1)S(1)}, u32[]{:S(2)}, u32[]{:S(2)}) collective-permute-start(bf16[256,512]{1,0:T(8,128)(2,1)S(1)} %collective-permute-done.16.refs_1_), channel_id=1, source_target_pairs={{0,6},{1,7},{2,0},{3,1},{4,2},{5,3},{6,4},{7,5},{8,14},{9,15},{10,... | collective-permute-start | bytes 786440 | tf_op jit(solution)/shard_map/ppermute | solution.py:45
  194.8 4.3 %collective-permute-done.27.refs_11_ = bf16[256,512]{1,0:T(8,128)(2,1)S(1)} collective-permute-done((bf16[256,512]{1,0:T(8,128)(2,1)S(1)}, bf16[256,512]{1,0:T(8,128)(2,1)S(1)}, u32[]{:S(2)}, u32[]{:S(2)}) %collective-permute-start.27) | collective-permute-done | bytes 262176 | tf_op jit(solution)/shard_map/ppermute | solution.py:45
  208.4 5.6 %output6.1.refs_5_ = f32[512,512]{1,0:T(8,128)} custom-call(bf16[256,512]{1,0:T(8,128)(2,1)} %copy-done.13, bf16[256,512]{1,0:T(8,128)(2,1)} %copy-done.23, bf16[256,512]{1,0:T(8,128)(2,1)} %copy-done.17, bf16[256,512]{1,0:T(8,128)(2,1)} %copy-done.16, bf16[256,512]{1,0:T(8,128)(2,1)} %copy-done.21, bf16[256,512]{1,0:T(8,128)(2,1)} %copy-done.20, ...), custom_call_target="tpu_custom_call" | custom-call | tf_op jit(solution)/shard_map/output6/pallas_call | solution.py:430
  214.2 4.3 %output2.1 = bf16[512,512]{1,0:T(8,128)(2,1)} custom-call(bf16[256,512]{1,0:T(8,128)(2,1)} %collective-permute-done.18.refs_0_, bf16[256,512]{1,0:T(8,128)(2,1)} %collective-permute-done.21.refs_1_, bf16[256,512]{1,0:T(8,128)(2,1)} %collective-permute-done.25.refs_2_, bf16[256,512]{1,0:T(8,128)(2,1)} %collective-permute-done.28.refs_3_, ...), custom_call_target="tpu_custom_call" | custom-call | tf_op jit(solution)/shard_map/output2/pallas_call | solution.py:430
  (136 shorter events, 53.5 us)
Async XLA Ops:
  6.5 77.7 %all-gather.7.cloned.1.call-start = ((), (), s32[]{:S(2)}) async-start(), calls=%async_computation.2 | async-start | bytes 5308416 | tf_op jit(solution)/shard_map/all_gather | solution.py:54
  18.2 124.8 %all-gather.9.cloned.1.call-start = ((), (), s32[]{:S(2)}) async-start(), calls=%async_computation.3 | async-start | bytes 2359296 | tf_op jit(solution)/shard_map/all_gather | solution.py:54
  18.2 15.8 %collective-permute-start.1 = (bf16[512,512]{1,0:T(8,128)(2,1)}, bf16[512,512]{1,0:T(8,128)(2,1)S(1)}, u32[]{:S(2)}, u32[]{:S(2)}) collective-permute-start(bf16[512,512]{1,0:T(8,128)(2,1)} %refs_0_.3), channel_id=1, source_target_pairs={{0,1},{1,0},{2,3},{3,2},{4,5},{5,4},{6,7},{7,6},{8,9},{9,8},{10,11... | collective-permute-start | bytes 1572872 | tf_op jit(solution)/shard_map/ppermute | solution.py:49
  20.6 11.0 %collective-permute-start.2 = (bf16[512,128]{1,0:T(8,128)(2,1)}, bf16[512,128]{1,0:T(8,128)(2,1)S(1)}, u32[]{:S(2)}, u32[]{:S(2)}) collective-permute-start(bf16[512,128]{1,0:T(8,128)(2,1)} %param.11), channel_id=1, source_target_pairs={{0,0},{1,32},{2,64},{3,96},{4,128},{5,160},{6,192},{7,224},{8,8},{... | collective-permute-start | bytes 393224 | tf_op jit(solution)/shard_map/ppermute | solution.py:462
  22.2 24.9 %collective-permute-start.4 = (bf16[512,512]{1,0:T(8,128)(2,1)}, bf16[512,512]{1,0:T(8,128)(2,1)S(1)}, u32[]{:S(2)}, u32[]{:S(2)}) collective-permute-start(bf16[512,512]{1,0:T(8,128)(2,1)} %refs_0_.3), channel_id=1, source_target_pairs={{0,6},{1,7},{2,0},{3,1},{4,2},{5,3},{6,4},{7,5},{8,14},{9,15},{10,... | collective-permute-start | bytes 1572872 | tf_op jit(solution)/shard_map/ppermute | solution.py:45
  34.0 22.2 %collective-permute-start.6 = (bf16[512,512]{1,0:T(8,128)(2,1)S(1)}, bf16[512,512]{1,0:T(8,128)(2,1)S(1)}, u32[]{:S(2)}, u32[]{:S(2)}) collective-permute-start(bf16[512,512]{1,0:T(8,128)(2,1)S(1)} %collective-permute-done.1.refs_1_), channel_id=1, source_target_pairs={{0,6},{1,7},{2,0},{3,1},{4,2},{5,3},{6,4},{7,5},{8,14},{9,15},{10,... | collective-permute-start | bytes 1572872 | tf_op jit(solution)/shard_map/ppermute | solution.py:45
  43.7 16.4 %collective-permute-start.3 = (bf16[512,512]{1,0:T(8,128)(2,1)}, bf16[512,512]{1,0:T(8,128)(2,1)S(1)}, u32[]{:S(2)}, u32[]{:S(2)}) collective-permute-start(bf16[512,512]{1,0:T(8,128)(2,1)} %refs_0_.3), channel_id=1, source_target_pairs={{0,2},{1,3},{2,4},{3,5},{4,6},{5,7},{6,0},{7,1},{8,10},{9,11},{10,... | collective-permute-start | bytes 1572872 | tf_op jit(solution)/shard_map/ppermute | solution.py:45
  43.7 16.4 %collective-permute-start.5 = (bf16[512,512]{1,0:T(8,128)(2,1)S(1)}, bf16[512,512]{1,0:T(8,128)(2,1)S(1)}, u32[]{:S(2)}, u32[]{:S(2)}) collective-permute-start(bf16[512,512]{1,0:T(8,128)(2,1)S(1)} %collective-permute-done.1.refs_1_), channel_id=1, source_target_pairs={{0,2},{1,3},{2,4},{3,5},{4,6},{5,7},{6,0},{7,1},{8,10},{9,11},{10,... | collective-permute-start | bytes 1572872 | tf_op jit(solution)/shard_map/ppermute | solution.py:45
  56.4 13.4 %collective-permute-start.7 = (bf16[512,512]{1,0:T(8,128)(2,1)S(1)}, bf16[512,512]{1,0:T(8,128)(2,1)S(1)}, u32[]{:S(2)}, u32[]{:S(2)}) collective-permute-start(bf16[512,512]{1,0:T(8,128)(2,1)S(1)} %pad_maximum_fusion.1), channel_id=1, source_target_pairs={{0,6},{1,7},{2,0},{3,1},{4,2},{5,3},{6,4},{7,5},{8,14},{9,15},{10,... | collective-permute-start | bytes 1572872 | tf_op jit(solution)/shard_map/ppermute | solution.py:45
  60.2 13.2 %collective-permute-start.9 = (bf16[512,512]{1,0:T(8,128)(2,1)S(1)}, bf16[512,512]{1,0:T(8,128)(2,1)}, u32[]{:S(2)}, u32[]{:S(2)}) collective-permute-start(bf16[512,512]{1,0:T(8,128)(2,1)S(1)} %pad_maximum_fusion.2), channel_id=1, source_target_pairs={{0,2},{1,3},{2,4},{3,5},{4,6},{5,7},{6,0},{7,1},{8,10},{9,11},{10,... | collective-permute-start | bytes 1572872 | tf_op jit(solution)/shard_map/ppermute | solution.py:45
  103.3 27.7 %all-to-all-start = ((bf16[32,32,256]{2,1,0:T(8,128)(2,1)}), bf16[32,32,256]{2,1,0:T(8,128)(2,1)S(1)}, u32[]{:S(2)}, u32[]{:S(2)}) async-start(bf16[32,32,256]{2,1,0:T(8,128)(2,1)} %get-tuple-element.45), calls=%async_computation | async-start | bytes 1048576 | tf_op jit(solution)/shard_map/all_to_all | solution.py:485
  108.2 100.1 %all-gather.11.cloned.1.call-start = ((), (), s32[]{:S(2)}) async-start(), calls=%async_computation.4 | async-start | bytes 4718592 | tf_op jit(solution)/shard_map/all_gather | solution.py:54
  109.9 11.1 %collective-permute-start.13 = (bf16[2,512,128]{2,1,0:T(8,128)(2,1)S(1)}, bf16[2,512,128]{2,1,0:T(8,128)(2,1)S(1)}, u32[]{:S(2)}, u32[]{:S(2)}) collective-permute-start(bf16[2,512,128]{2,1,0:T(8,128)(2,1)S(1)} %pad_maximum_fusion.5), channel_id=1, source_target_pairs={{0,16},{8,24},{16,0},{24,8},{32,48},{40,56},{48,32},{56,40},{64,80... | collective-permute-start | bytes 786440 | tf_op jit(solution)/shard_map/ppermute | solution.py:32
  143.1 26.5 %all-to-all-start.1 = ((bf16[32,32,256]{2,1,0:T(8,128)(2,1)}), bf16[32,32,256]{2,1,0:T(8,128)(2,1)S(1)}, u32[]{:S(2)}, u32[]{:S(2)}) async-start(bf16[32,32,256]{2,1,0:T(8,128)(2,1)} %bitcast.28), calls=%async_computation.1 | async-start | bytes 1048576 | tf_op jit(solution)/shard_map/all_to_all | solution.py:490
  172.7 12.9 %collective-permute-start.23 = (bf16[256,512]{1,0:T(8,128)(2,1)S(1)}, bf16[256,512]{1,0:T(8,128)(2,1)S(1)}, u32[]{:S(2)}, u32[]{:S(2)}) collective-permute-start(bf16[256,512]{1,0:T(8,128)(2,1)S(1)} %get-tuple-element.53.refs_6_), channel_id=1, source_target_pairs={{0,1},{1,0},{2,3},{3,2},{4,5},{5,4},{6,7},{7,6},{8,9},{9,8},{10,11... | collective-permute-start | bytes 786440 | tf_op jit(solution)/shard_map/ppermute | solution.py:49
  174.7 13.7 %collective-permute-start.22 = (bf16[256,512]{1,0:T(8,128)(2,1)S(1)}, bf16[256,512]{1,0:T(8,128)(2,1)S(1)}, u32[]{:S(2)}, u32[]{:S(2)}) collective-permute-start(bf16[256,512]{1,0:T(8,128)(2,1)S(1)} %get-tuple-element.53.refs_6_), channel_id=1, source_target_pairs={{0,2},{1,3},{2,4},{3,5},{4,6},{5,7},{6,0},{7,1},{8,10},{9,11},{10,... | collective-permute-start | bytes 786440 | tf_op jit(solution)/shard_map/ppermute | solution.py:45
  176.2 12.2 %collective-permute-start.26 = (bf16[256,512]{1,0:T(8,128)(2,1)S(1)}, bf16[256,512]{1,0:T(8,128)(2,1)S(1)}, u32[]{:S(2)}, u32[]{:S(2)}) collective-permute-start(bf16[256,512]{1,0:T(8,128)(2,1)S(1)} %get-tuple-element.53.refs_6_), channel_id=1, source_target_pairs={{0,6},{1,7},{2,0},{3,1},{4,2},{5,3},{6,4},{7,5},{8,14},{9,15},{10,... | collective-permute-start | bytes 786440 | tf_op jit(solution)/shard_map/ppermute | solution.py:45
  177.9 15.6 %collective-permute-start.19 = (bf16[256,512]{1,0:T(8,128)(2,1)S(1)}, bf16[256,512]{1,0:T(8,128)(2,1)S(1)}, u32[]{:S(2)}, u32[]{:S(2)}) collective-permute-start(bf16[256,512]{1,0:T(8,128)(2,1)S(1)} %get-tuple-element.54.refs_0_), channel_id=1, source_target_pairs={{0,6},{1,7},{2,0},{3,1},{4,2},{5,3},{6,4},{7,5},{8,14},{9,15},{10,... | collective-permute-start | bytes 786440 | tf_op jit(solution)/shard_map/ppermute | solution.py:45
  181.9 12.8 %collective-permute-start.15 = (bf16[256,512]{1,0:T(8,128)(2,1)S(1)}, bf16[256,512]{1,0:T(8,128)(2,1)S(1)}, u32[]{:S(2)}, u32[]{:S(2)}) collective-permute-start(bf16[256,512]{1,0:T(8,128)(2,1)S(1)} %get-tuple-element.54.refs_0_), channel_id=1, source_target_pairs={{0,2},{1,3},{2,4},{3,5},{4,6},{5,7},{6,0},{7,1},{8,10},{9,11},{10,... | collective-permute-start | bytes 786440 | tf_op jit(solution)/shard_map/ppermute | solution.py:45
  185.6 13.5 %collective-permute-start.27 = (bf16[256,512]{1,0:T(8,128)(2,1)S(1)}, bf16[256,512]{1,0:T(8,128)(2,1)S(1)}, u32[]{:S(2)}, u32[]{:S(2)}) collective-permute-start(bf16[256,512]{1,0:T(8,128)(2,1)S(1)} %collective-permute-done.23.refs_7_), channel_id=1, source_target_pairs={{0,6},{1,7},{2,0},{3,1},{4,2},{5,3},{6,4},{7,5},{8,14},{9,15},{10,... | collective-permute-start | bytes 786440 | tf_op jit(solution)/shard_map/ppermute | solution.py:45
  188.5 16.3 %collective-permute-start.20 = (bf16[256,512]{1,0:T(8,128)(2,1)S(1)}, bf16[256,512]{1,0:T(8,128)(2,1)S(1)}, u32[]{:S(2)}, u32[]{:S(2)}) collective-permute-start(bf16[256,512]{1,0:T(8,128)(2,1)S(1)} %collective-permute-done.16.refs_1_), channel_id=1, source_target_pairs={{0,6},{1,7},{2,0},{3,1},{4,2},{5,3},{6,4},{7,5},{8,14},{9,15},{10,... | collective-permute-start | bytes 786440 | tf_op jit(solution)/shard_map/ppermute | solution.py:45
  193.5 12.0 %collective-permute-start.17 = (bf16[256,512]{1,0:T(8,128)(2,1)S(1)}, bf16[256,512]{1,0:T(8,128)(2,1)S(1)}, u32[]{:S(2)}, u32[]{:S(2)}) collective-permute-start(bf16[256,512]{1,0:T(8,128)(2,1)S(1)} %collective-permute-done.16.refs_1_), channel_id=1, source_target_pairs={{0,2},{1,3},{2,4},{3,5},{4,6},{5,7},{6,0},{7,1},{8,10},{9,11},{10,... | collective-permute-start | bytes 786440 | tf_op jit(solution)/shard_map/ppermute | solution.py:45
  199.2 14.9 %collective-permute-start.28 = (bf16[256,512]{1,0:T(8,128)(2,1)S(1)}, bf16[256,512]{1,0:T(8,128)(2,1)}, u32[]{:S(2)}, u32[]{:S(2)}) collective-permute-start(bf16[256,512]{1,0:T(8,128)(2,1)S(1)} %pad_maximum_fusion.9), channel_id=1, source_target_pairs={{0,6},{1,7},{2,0},{3,1},{4,2},{5,3},{6,4},{7,5},{8,14},{9,15},{10,... | collective-permute-start | bytes 786440 | tf_op jit(solution)/shard_map/ppermute | solution.py:45
  200.0 14.0 %collective-permute-start.25 = (bf16[256,512]{1,0:T(8,128)(2,1)}, bf16[256,512]{1,0:T(8,128)(2,1)}, u32[]{:S(2)}, u32[]{:S(2)}) collective-permute-start(bf16[256,512]{1,0:T(8,128)(2,1)} %pad_maximum_fusion.8), channel_id=1, source_target_pairs={{0,2},{1,3},{2,4},{3,5},{4,6},{5,7},{6,0},{7,1},{8,10},{9,11},{10,... | collective-permute-start | bytes 786440 | tf_op jit(solution)/shard_map/ppermute | solution.py:45
  (36 other events, 694.9 us)
Sparse Core Ops, SparseCore 0:
  18.3 65.8 all-gather.6
  92.0 50.8 all-gather.8
  144.8 58.9 all-gather.10

commit v5 on v4

--- a/solution.py
+++ b/solution.py
@@ -94,14 +94,14 @@
     return me // 4, (me // 2) % 2, me % 2
 
 
-def weight_copies(weights, wts, lanes):
-    z, y, core = weight_slots()
+def weight_copies(weights, proj, cols, dst):
+    _, y, core = weight_slots()
     copies = []
     for dc, ref in enumerate(weights):
         for dy in (0, 1):
             slot = ((y + dy) % 2) * 2 + (core + dc) % 2
-            src = ref.at[:, dy, pl.ds(0, wts.shape[2]), lanes]
-            copies.append((src, wts.at[:, slot, :, lanes]))
+            src = ref.at[:, dy, proj, pl.ds(0, dst.shape[2]), cols]
+            copies.append((src, dst.at[:, slot]))
     return copies
 
 
@@ -169,7 +169,8 @@
         group = []
         for proj in range(n_proj):
             lanes = pl.ds(proj * chan + tile * width, width)
-            for src, to in weight_copies(weights, wts, lanes):
+            cols = pl.ds(tile * width, width)
+            for src, to in weight_copies(weights, proj, cols, wts.at[:, :, :, lanes]):
                 group.append(pltpu.make_async_copy(src, to, w_sems.at[tile]))
         for copy in group:
             copy.start()
@@ -204,7 +205,7 @@
 
 def project(pieces, tail, weights, taps, out_shapes):
     n_proj = taps.shape[0]
-    total = weights[0].shape[-1]
+    total = weights[0].shape[-1] * n_proj
     width = 256
     n_tiles = total // n_proj // width
     rows = pieces[0].shape[0]
@@ -231,13 +232,12 @@
     _, y, core = weight_slots()
     group = lax.axis_index("ctx")
     width = rows_ref.shape[3]
-    lanes = pl.ds(pl.multiple_of(group // 16 * width, width), width)
-    filter_rows = pl.ds(mine.shape[2] - 16, 16)
+    filter_rows = pl.ds(mine.shape[3] - 16, 16)
     copies = []
     for dc, ref in enumerate((mine, other)):
         for dy in (0, 1):
             slot = ((y + dy) % 2) * 2 + (core + dc) % 2
-            src = ref.at[:, dy, filter_rows, lanes]
+            src = ref.at[:, dy, group // 16, filter_rows]
             copies.append(pltpu.make_async_copy(src, rows_ref.at[:, slot], row_sem))
     for copy in copies:
         copy.start()
@@ -304,35 +304,48 @@
 FETCHES = 4
 
 
-def conv_kernel(x_ref, h_hbm, y_ref, h_ref, sems):
+def conv_kernel(x_hbm, h_hbm, y_ref, x_ref, h_ref, acc, x_sem, sems):
     rows, width = x_ref.shape
     tiles = rows // TILE
+    count = h_ref.shape[0] // FETCHES
+    lags = count // width
 
     def fetch(g):
-        count = h_ref.shape[0] // FETCHES
         here = pl.ds(g * count, count)
         return pltpu.make_async_copy(h_hbm.at[here], h_ref.at[here], sems.at[g])
 
+    x_copy = pltpu.make_async_copy(x_hbm, x_ref, x_sem)
+    x_copy.start()
     for g in range(FETCHES):
         fetch(g).start()
-    for tile in range(tiles):
-        if tile % (tiles // FETCHES) == 0:
-            fetch(tile // (tiles // FETCHES)).wait()
-        lags = (tile + 1) * LAGS
-        shifted = []
-        for lag in range(lags):
-            first = tile * TILE - 16 * lag
-            if first >= 0:
-                shifted.append(x_ref[first : first + TILE, :])
+    x_copy.wait()
+    for g in range(FETCHES):
+        fetch(g).wait()
+        for tile in range(tiles):
+            last = (tile + 1) * LAGS
+            shifted = []
+            for lag in range(g * lags, min(g * lags + lags, last)):
+                first = tile * TILE - 16 * lag
+                if first >= 0:
+                    shifted.append(x_ref[first : first + TILE, :])
+                else:
+                    empty = jnp.zeros((-first, width), BF16)
+                    shifted.append(jnp.concatenate([empty, x_ref[0 : TILE + first, :]], axis=0))
+            if not shifted:
+                continue
+            begin = g * count
+            product = jnp.dot(
+                jnp.concatenate(shifted, axis=1),
+                h_ref[begin : begin + len(shifted) * width, :],
+                preferred_element_type=F32,
+            )
+            here = slice(tile * TILE, tile * TILE + TILE)
+            if g:
+                product = product + acc[here, :]
+            if g * lags + lags >= last:
+                y_ref[here, :] = product.astype(BF16)
             else:
-                empty = jnp.zeros((-first, width), BF16)
-                shifted.append(jnp.concatenate([empty, x_ref[0 : TILE + first, :]], axis=0))
-        product = jnp.dot(
-            jnp.concatenate(shifted, axis=1),
-            h_ref[0 : lags * width, :],
-            preferred_element_type=F32,
-        )
-        y_ref[tile * TILE : tile * TILE + TILE, :] = product.astype(BF16)
+                acc[here, :] = product
 
 
 def conv(x, table):
@@ -340,10 +353,13 @@
     return pl.pallas_call(
         conv_kernel,
         out_shape=jax.ShapeDtypeStruct((rows, width), BF16),
-        in_specs=[VMEM, HBM],
+        in_specs=[HBM, HBM],
         out_specs=VMEM,
         scratch_shapes=[
+            pltpu.VMEM((rows, width), BF16),
             pltpu.VMEM((64 * width, width), BF16),
+            pltpu.VMEM((rows, width), F32),
+            pltpu.SemaphoreType.DMA,
             pltpu.SemaphoreType.DMA((FETCHES,)),
         ],
         compiler_params=pltpu.CompilerParams(vmem_limit_bytes=60 * MIB),
@@ -351,24 +367,23 @@
     )(x, table.reshape(64 * width, width))
 
 
-def gate_kernel(back_ref, mixed_ref, query_ref, skip_ref, out_ref):
-    chan = mixed_ref.shape[1]
-    for a in range(2):
-        block = back_ref[:, 16 * a : 16 * a + 16, :].reshape(chan, 256)
-        turned = block.astype(F32).T
-        here = pl.ds(256 * a, 256)
-        mixed = mixed_ref[here, :].astype(F32)
-        out_ref[here, :] = (query_ref[here, :] * (turned + skip_ref[...] * mixed)).astype(BF16)
-
-
-def gate(back, mixed, query, skip):
+def gate_kernel(half, back_ref, mixed_ref, query_ref, skip_ref, out_ref):
+    rows, chan = out_ref.shape
+    here = pl.ds(half * rows, rows)
+    block = back_ref[:, 16 * half : 16 * half + 16, :].reshape(chan, rows)
+    turned = block.astype(F32).T
+    mixed = mixed_ref[here, :].astype(F32)
+    out_ref[...] = (query_ref[here, :] * (turned + skip_ref[...] * mixed)).astype(BF16)
+
+
+def gate(back, mixed, query, skip, half):
     return pl.pallas_call(
-        gate_kernel,
-        out_shape=jax.ShapeDtypeStruct(mixed.shape, BF16),
+        functools.partial(gate_kernel, half),
+        out_shape=jax.ShapeDtypeStruct((back.shape[2], mixed.shape[1]), BF16),
         in_specs=[VMEM] * 4,
         out_specs=VMEM,
         compiler_params=pltpu.CompilerParams(vmem_limit_bytes=8 * MIB),
-        name="gate",
+        name="gate%d" % half,
     )(back, mixed, query, skip)
 
 
@@ -398,8 +413,8 @@
 
 
 def output_kernel(parts_of, n_pieces, *refs):
-    pieces, (weights, *start) = refs[:n_pieces], refs[n_pieces:-4]
-    out_ref, act, wts, sem = refs[-4:]
+    pieces, (weights, *start) = refs[:n_pieces], refs[n_pieces:-5]
+    out_ref, act, wts, before, sem = refs[-5:]
     _, y, core = weight_slots()
     width = weights.shape[3]
     depth = wts.shape[1]
@@ -413,6 +428,8 @@
             lanes = pl.ds(pl.multiple_of(slot * width, width), width)
             to = wts.at[p, :, lanes]
             copies.append(pltpu.make_async_copy(weights.at[there, k], to, sem))
+    if start:
+        copies.append(pltpu.make_async_copy(start[0], before, sem))
     for copy in copies:
         copy.start()
     for copy in copies:
@@ -420,7 +437,7 @@
     matrix = wts[...].reshape(-1, wts.shape[2])
     total = jnp.dot(act[...], matrix, preferred_element_type=F32)
     if start:
-        total = total + start[0][...]
+        total = total + before[...]
     out_ref[...] = total.astype(out_ref.dtype)
 
 
@@ -430,11 +447,12 @@
     return pl.pallas_call(
         functools.partial(output_kernel, parts_of, len(pieces)),
         out_shape=jax.ShapeDtypeStruct((rows, 4 * width), dtype),
-        in_specs=[HBM] * (len(pieces) + 1) + [VMEM] * len(start),
+        in_specs=[HBM] * (len(pieces) + 1 + len(start)),
         out_specs=VMEM,
         scratch_shapes=[
             pltpu.VMEM((rows, parts * depth), BF16),
             pltpu.VMEM((parts, depth, 4 * width), BF16),
+            pltpu.VMEM((rows, 4 * width) if start else (8, 128), F32),
             pltpu.SemaphoreType.DMA,
         ],
         compiler_params=pltpu.CompilerParams(vmem_limit_bytes=60 * MIB),
@@ -451,9 +469,8 @@
     depth, chan = w_in.shape[1:]
     taps = short_taps.transpose(0, 2, 1)
 
-    kv = jnp.concatenate([w_in[1], w_in[2]], axis=1)
-    filt = jnp.concatenate([filters[:16], filters[16:]], axis=1)
-    kv_mine = gather_z(pair_ylo(jnp.concatenate([kv, filt])))
+    kv = jnp.concatenate([w_in[1:], filters.reshape(2, 16, -1)], axis=1)
+    kv_mine = gather_z(pair_ylo(kv))
     route = []
     for z in range(NZ):
         for r in range(4):
@@ -467,7 +484,7 @@
     kv_mine, tail, *pieces = barrier(kv_mine, tail, *pieces)
     w_in, kv_mine = barrier(w_in, kv_mine)
     kv_other = swap_core(kv_mine)
-    q_mine = gather_z(pair_ylo(w_in[0]))
+    q_mine = gather_z(pair_ylo(w_in[:1]))
     mixed, blocks = project(
         pieces,
         tail,
@@ -496,10 +513,9 @@
         taps[:1],
         [jax.ShapeDtypeStruct((rows, chan), F32)],
     )
-    gated = gate(back, mixed, query, skip[None, :])
-
-    half = rows // 2
-    first, second = gather_tp(gated[:half])[0], gather_tp(gated[half:])[0]
+    gated = [gate(back, mixed, query, skip[None, :], half) for half in range(2)]
+
+    first, second = gather_tp(gated[0])[0], gather_tp(gated[1])[0]
     total = output(first[:6] + second[:6], near_parts, 6, o_mine, [], F32)
     return output(first[6:] + second[6:], far_parts, 2, o_mine, [total], BF16)
 

time: 226 us -> 223 us (0.987)
  waiting for transfers between devices: 80.3 us -> 76.9 us
  starting transfers between devices: 68.8 us -> 71.8 us
    ppermute x18, starting transfers between devices: 44 us -> 47.1 us  [shift_x(): return lax.ppermute(block, 'tp', route)]
    ppermute x3, waiting for transfers between devices: 5.23 us -> 2.48 us  [swap_yhi(): return lax.ppermute(block, 'tp', [(j, j ^ 1) for j in range(TP)])]
  transfers between devices with their start and end apart: 34 -> 34, of which waited for: 20 -> 18; matrix products, arithmetic and copies ran while one was open for 3% -> 3% of each run, Pallas kernels for 20% -> 20%
where the time goes in v5:
time: 223 us; the launch traced here: 222 us
  waiting for transfers between devices  76.9 us (34%)
  starting transfers between devices  71.8 us (32%)
  Pallas kernels  48.5 us (22%)
  between operations  13.5 us (6%)
  local copies, waits for them, and re-layouts  6.07 us (3%)
  other arithmetic  5.72 us (3%)
    ppermute x18, starting transfers between devices, shift_x(): return lax.ppermute(block, 'tp', route)  47.1 us
    ppermute x18, waiting for transfers between devices, shift_x(): return lax.ppermute(block, 'tp', route)  28.4 us
    pallas_call x2, Pallas kernels, project(): pl.pallas_call(functools.partial(project_kernel, n_proj, len(out_shapes),...  20.2 us
    ppermute x6, waiting for transfers between devices, swap_ctx(): return lax.ppermute(block, 'ctx', [(i, i ^ mask) for i in range(CTX)])  13.9 us
    all_to_all x1, waiting for transfers between devices, local(): back = lax.all_to_all(result.reshape(CTX, 32, 256), 'ctx', 0, 0, tiled=True)  10.7 us
    pallas_call x1, Pallas kernels, conv(): pl.pallas_call(conv_kernel, out_shape=jax.ShapeDtypeStruct((rows, width),...  9.78 us
    all_to_all x1, waiting for transfers between devices, local(): sent = lax.all_to_all(blocks, 'ctx', 0, 0, tiled=True)  9.22 us
    pallas_call x2, Pallas kernels, output(): pl.pallas_call(functools.partial(output_kernel, parts_of, len(pieces)), o...  9.1 us
  transfers between devices with their start and end apart: 34, of which 18 were waited for; matrix products, arithmetic and copies ran while one was open for 3% of the time, Pallas kernels for 20%

profile of v5, /device:TPU:8, one launch (start us, length us, event | category | flops | bytes accessed | tf_op | source)
XLA Modules:
  0.0 222.5 jit_solution(4772007744419019740)
XLA Ops:
  10.6 6.6 %collective-permute-done = bf16[2,144,512]{2,1,0:T(8,128)(2,1)S(1)} collective-permute-done((bf16[2,144,512]{2,1,0:T(8,128)(2,1)S(1)}, bf16[2,144,512]{2,1,0:T(8,128)(2,1)S(1)}, u32[]{:S(2)}, u32[]{:S(2)}) %collective-permute-start) | collective-permute-done | bytes 294944 | tf_op jit(solution)/shard_map/ppermute | solution.py:32
  22.1 9.4 %collective-permute-start.4 = (bf16[512,512]{1,0:T(8,128)(2,1)}, bf16[512,512]{1,0:T(8,128)(2,1)S(1)}, u32[]{:S(2)}, u32[]{:S(2)}) collective-permute-start(bf16[512,512]{1,0:T(8,128)(2,1)} %refs_0_.3), channel_id=1, source_target_pairs={{0,6},{1,7},{2,0},{3,1},{4,2},{5,3},{6,4},{7,5},{8,14},{9,15},{10,... | collective-permute-start | bytes 1572872 | tf_op jit(solution)/shard_map/ppermute | solution.py:45
  31.5 2.5 %collective-permute-done.1.refs_1_ = bf16[512,512]{1,0:T(8,128)(2,1)S(1)} collective-permute-done((bf16[512,512]{1,0:T(8,128)(2,1)}, bf16[512,512]{1,0:T(8,128)(2,1)S(1)}, u32[]{:S(2)}, u32[]{:S(2)}) %collective-permute-start.1) | collective-permute-done | bytes 524320 | tf_op jit(solution)/shard_map/ppermute | solution.py:49
  34.0 9.7 %collective-permute-start.6 = (bf16[512,512]{1,0:T(8,128)(2,1)S(1)}, bf16[512,512]{1,0:T(8,128)(2,1)S(1)}, u32[]{:S(2)}, u32[]{:S(2)}) collective-permute-start(bf16[512,512]{1,0:T(8,128)(2,1)S(1)} %collective-permute-done.1.refs_1_), channel_id=1, source_target_pairs={{0,6},{1,7},{2,0},{3,1},{4,2},{5,3},{6,4},{7,5},{8,14},{9,15},{10,... | collective-permute-start | bytes 1572872 | tf_op jit(solution)/shard_map/ppermute | solution.py:45
  43.7 3.4 %collective-permute-done.4.refs_3_ = bf16[512,512]{1,0:T(8,128)(2,1)S(1)} collective-permute-done((bf16[512,512]{1,0:T(8,128)(2,1)}, bf16[512,512]{1,0:T(8,128)(2,1)S(1)}, u32[]{:S(2)}, u32[]{:S(2)}) %collective-permute-start.4) | collective-permute-done | bytes 524320 | tf_op jit(solution)/shard_map/ppermute | solution.py:45
  47.1 9.2 %collective-permute-done.6.refs_5_ = bf16[512,512]{1,0:T(8,128)(2,1)S(1)} collective-permute-done((bf16[512,512]{1,0:T(8,128)(2,1)S(1)}, bf16[512,512]{1,0:T(8,128)(2,1)S(1)}, u32[]{:S(2)}, u32[]{:S(2)}) %collective-permute-start.6) | collective-permute-done | bytes 524320 | tf_op jit(solution)/shard_map/ppermute | solution.py:45
  56.3 3.8 %collective-permute-start.7 = (bf16[512,512]{1,0:T(8,128)(2,1)S(1)}, bf16[512,512]{1,0:T(8,128)(2,1)S(1)}, u32[]{:S(2)}, u32[]{:S(2)}) collective-permute-start(bf16[512,512]{1,0:T(8,128)(2,1)S(1)} %pad_maximum_fusion.1), channel_id=1, source_target_pairs={{0,6},{1,7},{2,0},{3,1},{4,2},{5,3},{6,4},{7,5},{8,14},{9,15},{10,... | collective-permute-start | bytes 1572872 | tf_op jit(solution)/shard_map/ppermute | solution.py:45
  61.3 8.5 %collective-permute-done.7.refs_6_.refs_7_ = bf16[512,512]{1,0:T(8,128)(2,1)S(1)} collective-permute-done((bf16[512,512]{1,0:T(8,128)(2,1)S(1)}, bf16[512,512]{1,0:T(8,128)(2,1)S(1)}, u32[]{:S(2)}, u32[]{:S(2)}) %collective-permute-start.7) | collective-permute-done | bytes 524320 | tf_op jit(solution)/shard_map/ppermute | solution.py:45
  73.4 3.4 %collective-permute-done.8.refs_8_ = bf16[8,16,512]{2,1,0:T(8,128)(2,1)S(1)} collective-permute-done((bf16[8,16,512]{2,1,0:T(8,128)(2,1)S(1)}, bf16[8,16,512]{2,1,0:T(8,128)(2,1)S(1)}, u32[]{:S(2)}, u32[]{:S(2)}) %collective-permute-start.8) | collective-permute-done | bytes 131104 | tf_op jit(solution)/shard_map/ppermute | solution.py:482
  76.8 7.3 %all-gather.7.cloned.1.call-done = bf16[16,2,144,512]{3,2,1,0:T(8,128)(2,1)} async-done(((bf16[2,2,144,512]{3,2,1,0:T(8,128)(2,1)}), bf16[16,2,144,512]{3,2,1,0:T(8,128)(2,1)}) %all-gather.7.cloned.1.call-update) | async-done | bytes 4718608 | tf_op jit(solution)/shard_map/all_gather | solution.py:54
  86.6 4.5 %collective-permute-done.10 = bf16[1,128,512]{2,1,0:T(8,128)(2,1)S(1)} collective-permute-done((bf16[1,128,512]{2,1,0:T(8,128)(2,1)S(1)}, bf16[1,128,512]{2,1,0:T(8,128)(2,1)S(1)}, u32[]{:S(2)}, u32[]{:S(2)}) %collective-permute-start.10) | collective-permute-done | bytes 131104 | tf_op jit(solution)/shard_map/ppermute | solution.py:32
  92.5 10.7 %project2.1 = (bf16[512,512]{1,0:T(8,128)(2,1)}, bf16[32,32,256]{2,1,0:T(8,128)(2,1)}) custom-call(bf16[512,512]{1,0:T(8,128)(2,1)} %refs_0_.3, bf16[512,512]{1,0:T(8,128)(2,1)} %copy-done.6, bf16[512,512]{1,0:T(8,128)(2,1)} %copy-done.3, bf16[512,512]{1,0:T(8,128)(2,1)} %copy-done.1, bf16[512,512]{1,0:T(8,128)(2,1)} %copy-done.4, ...), custom_call_target="tpu_custom_call" | custom-call | tf_op jit(solution)/shard_map/project2/pallas_call | solution.py:213
  103.2 4.9 %all-to-all-start = ((bf16[32,32,256]{2,1,0:T(8,128)(2,1)}), bf16[32,32,256]{2,1,0:T(8,128)(2,1)S(1)}, u32[]{:S(2)}, u32[]{:S(2)}) async-start(bf16[32,32,256]{2,1,0:T(8,128)(2,1)} %get-tuple-element.45), calls=%async_computation | async-start | bytes 1048576 | tf_op jit(solution)/shard_map/all_to_all | solution.py:502
  110.3 9.0 %toeplitz.1 = bf16[64,256,256]{2,1,0:T(8,128)(2,1)} custom-call(bf16[8,2,2,144,512]{4,3,2,1,0:T(8,128)(2,1)} %bitcast.22, bf16[8,2,2,144,512]{4,3,2,1,0:T(8,128)(2,1)} %collective-permute-done.11.refs_10_.other), custom_call_target="tpu_custom_call" | custom-call | tf_op jit(solution)/shard_map/toeplitz/pallas_call | solution.py:285
  121.8 9.2 %all-to-all-done = bf16[32,32,256]{2,1,0:T(8,128)(2,1)S(1)} async-done(((bf16[32,32,256]{2,1,0:T(8,128)(2,1)}), bf16[32,32,256]{2,1,0:T(8,128)(2,1)S(1)}, u32[]{:S(2)}, u32[]{:S(2)}) %all-to-all-start) | async-done | bytes 524320 | tf_op jit(solution)/shard_map/all_to_all | solution.py:502
  131.8 9.8 %conv.1 = bf16[1024,256]{1,0:T(8,128)(2,1)} custom-call(bf16[1024,256]{1,0:T(8,128)(2,1)} %bitcast.25, bf16[16384,256]{1,0:T(8,128)(2,1)} %bitcast.19), custom_call_target="tpu_custom_call" | custom-call | tf_op jit(solution)/shard_map/conv/pallas_call | solution.py:353
  143.1 5.7 %all-to-all-start.1 = ((bf16[32,32,256]{2,1,0:T(8,128)(2,1)}), bf16[32,32,256]{2,1,0:T(8,128)(2,1)S(1)}, u32[]{:S(2)}, u32[]{:S(2)}) async-start(bf16[32,32,256]{2,1,0:T(8,128)(2,1)} %bitcast.26), calls=%async_computation.1 | async-start | bytes 1048576 | tf_op jit(solution)/shard_map/all_to_all | solution.py:507
  149.4 9.5 %project1.1.query_ref = f32[512,512]{1,0:T(8,128)} custom-call(bf16[512,512]{1,0:T(8,128)(2,1)} %refs_0_.3, bf16[512,512]{1,0:T(8,128)(2,1)} %copy-done.6, bf16[512,512]{1,0:T(8,128)(2,1)} %copy-done.3, bf16[512,512]{1,0:T(8,128)(2,1)} %copy-done.1, bf16[512,512]{1,0:T(8,128)(2,1)} %copy-done.4, bf16[512,512]{1,0:T(8,128)(2,1)} %copy-done.2, ...), custom_call_target="tpu_custom_call" | custom-call | tf_op jit(solution)/shard_map/project1/pallas_call | solution.py:213
  158.9 10.7 %all-to-all-done.1.back_ref = bf16[32,32,256]{2,1,0:T(8,128)(2,1)S(1)} async-done(((bf16[32,32,256]{2,1,0:T(8,128)(2,1)}), bf16[32,32,256]{2,1,0:T(8,128)(2,1)S(1)}, u32[]{:S(2)}, u32[]{:S(2)}) %all-to-all-start.1) | async-done | bytes 524320 | tf_op jit(solution)/shard_map/all_to_all | solution.py:507
  178.1 3.2 %collective-permute-start.19 = (bf16[256,512]{1,0:T(8,128)(2,1)S(1)}, bf16[256,512]{1,0:T(8,128)(2,1)S(1)}, u32[]{:S(2)}, u32[]{:S(2)}) collective-permute-start(bf16[256,512]{1,0:T(8,128)(2,1)S(1)} %gate0.1.refs_0_), channel_id=1, source_target_pairs={{0,6},{1,7},{2,0},{3,1},{4,2},{5,3},{6,4},{7,5},{8,14},{9,15},{10,... | collective-permute-start | bytes 786440 | tf_op jit(solution)/shard_map/ppermute | solution.py:45
  184.5 3.2 %collective-permute-start.24 = (bf16[256,512]{1,0:T(8,128)(2,1)S(1)}, bf16[256,512]{1,0:T(8,128)(2,1)S(1)}, u32[]{:S(2)}, u32[]{:S(2)}) collective-permute-start(bf16[256,512]{1,0:T(8,128)(2,1)S(1)} %collective-permute-done.23.refs_7_), channel_id=1, source_target_pairs={{0,2},{1,3},{2,4},{3,5},{4,6},{5,7},{6,0},{7,1},{8,10},{9,11},{10,... | collective-permute-start | bytes 786440 | tf_op jit(solution)/shard_map/ppermute | solution.py:45
  191.9 3.5 %collective-permute-done.27.refs_11_ = bf16[256,512]{1,0:T(8,128)(2,1)S(1)} collective-permute-done((bf16[256,512]{1,0:T(8,128)(2,1)S(1)}, bf16[256,512]{1,0:T(8,128)(2,1)S(1)}, u32[]{:S(2)}, u32[]{:S(2)}) %collective-permute-start.27) | collective-permute-done | bytes 262176 | tf_op jit(solution)/shard_map/ppermute | solution.py:45
  205.7 5.6 %output6.1.refs_5_ = f32[512,512]{1,0:T(8,128)} custom-call(bf16[256,512]{1,0:T(8,128)(2,1)} %copy-done.10, bf16[256,512]{1,0:T(8,128)(2,1)} %copy-done.23, bf16[256,512]{1,0:T(8,128)(2,1)} %copy-done.16, bf16[256,512]{1,0:T(8,128)(2,1)} %copy-done.15, bf16[256,512]{1,0:T(8,128)(2,1)} %copy-done.20, bf16[256,512]{1,0:T(8,128)(2,1)} %copy-done.19, ...), custom_call_target="tpu_custom_call" | custom-call | tf_op jit(solution)/shard_map/output6/pallas_call | solution.py:447
  212.5 3.5 %output2.1 = bf16[512,512]{1,0:T(8,128)(2,1)} custom-call(bf16[256,512]{1,0:T(8,128)(2,1)} %collective-permute-done.18.refs_0_, bf16[256,512]{1,0:T(8,128)(2,1)} %collective-permute-done.21.refs_1_, bf16[256,512]{1,0:T(8,128)(2,1)} %collective-permute-done.25.refs_2_, bf16[256,512]{1,0:T(8,128)(2,1)} %collective-permute-done.28.refs_3_, ...), custom_call_target="tpu_custom_call" | custom-call | tf_op jit(solution)/shard_map/output2/pallas_call | solution.py:447
  (133 shorter events, 52.2 us)
Async XLA Ops:
  6.5 77.6 %all-gather.7.cloned.1.call-start = ((), (), s32[]{:S(2)}) async-start(), calls=%async_computation.2 | async-start | bytes 5308416 | tf_op jit(solution)/shard_map/all_gather | solution.py:54
  18.1 124.8 %all-gather.9.cloned.1.call-start = ((), (), s32[]{:S(2)}) async-start(), calls=%async_computation.3 | async-start | bytes 2359296 | tf_op jit(solution)/shard_map/all_gather | solution.py:54
  18.2 15.8 %collective-permute-start.1 = (bf16[512,512]{1,0:T(8,128)(2,1)}, bf16[512,512]{1,0:T(8,128)(2,1)S(1)}, u32[]{:S(2)}, u32[]{:S(2)}) collective-permute-start(bf16[512,512]{1,0:T(8,128)(2,1)} %refs_0_.3), channel_id=1, source_target_pairs={{0,1},{1,0},{2,3},{3,2},{4,5},{5,4},{6,7},{7,6},{8,9},{9,8},{10,11... | collective-permute-start | bytes 1572872 | tf_op jit(solution)/shard_map/ppermute | solution.py:49
  20.6 11.0 %collective-permute-start.2 = (bf16[512,128]{1,0:T(8,128)(2,1)}, bf16[512,128]{1,0:T(8,128)(2,1)S(1)}, u32[]{:S(2)}, u32[]{:S(2)}) collective-permute-start(bf16[512,128]{1,0:T(8,128)(2,1)} %param.11), channel_id=1, source_target_pairs={{0,0},{1,32},{2,64},{3,96},{4,128},{5,160},{6,192},{7,224},{8,8},{... | collective-permute-start | bytes 393224 | tf_op jit(solution)/shard_map/ppermute | solution.py:479
  22.1 24.9 %collective-permute-start.4 = (bf16[512,512]{1,0:T(8,128)(2,1)}, bf16[512,512]{1,0:T(8,128)(2,1)S(1)}, u32[]{:S(2)}, u32[]{:S(2)}) collective-permute-start(bf16[512,512]{1,0:T(8,128)(2,1)} %refs_0_.3), channel_id=1, source_target_pairs={{0,6},{1,7},{2,0},{3,1},{4,2},{5,3},{6,4},{7,5},{8,14},{9,15},{10,... | collective-permute-start | bytes 1572872 | tf_op jit(solution)/shard_map/ppermute | solution.py:45
  34.0 22.2 %collective-permute-start.6 = (bf16[512,512]{1,0:T(8,128)(2,1)S(1)}, bf16[512,512]{1,0:T(8,128)(2,1)S(1)}, u32[]{:S(2)}, u32[]{:S(2)}) collective-permute-start(bf16[512,512]{1,0:T(8,128)(2,1)S(1)} %collective-permute-done.1.refs_1_), channel_id=1, source_target_pairs={{0,6},{1,7},{2,0},{3,1},{4,2},{5,3},{6,4},{7,5},{8,14},{9,15},{10,... | collective-permute-start | bytes 1572872 | tf_op jit(solution)/shard_map/ppermute | solution.py:45
  43.7 16.4 %collective-permute-start.3 = (bf16[512,512]{1,0:T(8,128)(2,1)}, bf16[512,512]{1,0:T(8,128)(2,1)S(1)}, u32[]{:S(2)}, u32[]{:S(2)}) collective-permute-start(bf16[512,512]{1,0:T(8,128)(2,1)} %refs_0_.3), channel_id=1, source_target_pairs={{0,2},{1,3},{2,4},{3,5},{4,6},{5,7},{6,0},{7,1},{8,10},{9,11},{10,... | collective-permute-start | bytes 1572872 | tf_op jit(solution)/shard_map/ppermute | solution.py:45
  43.7 16.4 %collective-permute-start.5 = (bf16[512,512]{1,0:T(8,128)(2,1)S(1)}, bf16[512,512]{1,0:T(8,128)(2,1)S(1)}, u32[]{:S(2)}, u32[]{:S(2)}) collective-permute-start(bf16[512,512]{1,0:T(8,128)(2,1)S(1)} %collective-permute-done.1.refs_1_), channel_id=1, source_target_pairs={{0,2},{1,3},{2,4},{3,5},{4,6},{5,7},{6,0},{7,1},{8,10},{9,11},{10,... | collective-permute-start | bytes 1572872 | tf_op jit(solution)/shard_map/ppermute | solution.py:45
  56.3 13.4 %collective-permute-start.7 = (bf16[512,512]{1,0:T(8,128)(2,1)S(1)}, bf16[512,512]{1,0:T(8,128)(2,1)S(1)}, u32[]{:S(2)}, u32[]{:S(2)}) collective-permute-start(bf16[512,512]{1,0:T(8,128)(2,1)S(1)} %pad_maximum_fusion.1), channel_id=1, source_target_pairs={{0,6},{1,7},{2,0},{3,1},{4,2},{5,3},{6,4},{7,5},{8,14},{9,15},{10,... | collective-permute-start | bytes 1572872 | tf_op jit(solution)/shard_map/ppermute | solution.py:45
  60.2 13.2 %collective-permute-start.9 = (bf16[512,512]{1,0:T(8,128)(2,1)S(1)}, bf16[512,512]{1,0:T(8,128)(2,1)}, u32[]{:S(2)}, u32[]{:S(2)}) collective-permute-start(bf16[512,512]{1,0:T(8,128)(2,1)S(1)} %pad_maximum_fusion.2), channel_id=1, source_target_pairs={{0,2},{1,3},{2,4},{3,5},{4,6},{5,7},{6,0},{7,1},{8,10},{9,11},{10,... | collective-permute-start | bytes 1572872 | tf_op jit(solution)/shard_map/ppermute | solution.py:45
  103.2 27.7 %all-to-all-start = ((bf16[32,32,256]{2,1,0:T(8,128)(2,1)}), bf16[32,32,256]{2,1,0:T(8,128)(2,1)S(1)}, u32[]{:S(2)}, u32[]{:S(2)}) async-start(bf16[32,32,256]{2,1,0:T(8,128)(2,1)} %get-tuple-element.45), calls=%async_computation | async-start | bytes 1048576 | tf_op jit(solution)/shard_map/all_to_all | solution.py:502
  108.2 97.4 %all-gather.11.cloned.1.call-start = ((), (), s32[]{:S(2)}) async-start(), calls=%async_computation.4 | async-start | bytes 4718592 | tf_op jit(solution)/shard_map/all_gather | solution.py:54
  109.9 11.1 %collective-permute-start.13 = (bf16[2,512,128]{2,1,0:T(8,128)(2,1)S(1)}, bf16[2,512,128]{2,1,0:T(8,128)(2,1)S(1)}, u32[]{:S(2)}, u32[]{:S(2)}) collective-permute-start(bf16[2,512,128]{2,1,0:T(8,128)(2,1)S(1)} %pad_maximum_fusion.6), channel_id=1, source_target_pairs={{0,16},{8,24},{16,0},{24,8},{32,48},{40,56},{48,32},{56,40},{64,80... | collective-permute-start | bytes 786440 | tf_op jit(solution)/shard_map/ppermute | solution.py:32
  143.1 26.6 %all-to-all-start.1 = ((bf16[32,32,256]{2,1,0:T(8,128)(2,1)}), bf16[32,32,256]{2,1,0:T(8,128)(2,1)S(1)}, u32[]{:S(2)}, u32[]{:S(2)}) async-start(bf16[32,32,256]{2,1,0:T(8,128)(2,1)} %bitcast.26), calls=%async_computation.1 | async-start | bytes 1048576 | tf_op jit(solution)/shard_map/all_to_all | solution.py:507
  171.0 10.3 %collective-permute-start.23 = (bf16[256,512]{1,0:T(8,128)(2,1)S(1)}, bf16[256,512]{1,0:T(8,128)(2,1)S(1)}, u32[]{:S(2)}, u32[]{:S(2)}) collective-permute-start(bf16[256,512]{1,0:T(8,128)(2,1)S(1)} %gate1.1.refs_6_), channel_id=1, source_target_pairs={{0,1},{1,0},{2,3},{3,2},{4,5},{5,4},{6,7},{7,6},{8,9},{9,8},{10,11... | collective-permute-start | bytes 786440 | tf_op jit(solution)/shard_map/ppermute | solution.py:49
  176.2 11.5 %collective-permute-start.16 = (bf16[256,512]{1,0:T(8,128)(2,1)S(1)}, bf16[256,512]{1,0:T(8,128)(2,1)S(1)}, u32[]{:S(2)}, u32[]{:S(2)}) collective-permute-start(bf16[256,512]{1,0:T(8,128)(2,1)S(1)} %gate0.1.refs_0_), channel_id=1, source_target_pairs={{0,1},{1,0},{2,3},{3,2},{4,5},{5,4},{6,7},{7,6},{8,9},{9,8},{10,11... | collective-permute-start | bytes 786440 | tf_op jit(solution)/shard_map/ppermute | solution.py:49
  178.1 11.7 %collective-permute-start.19 = (bf16[256,512]{1,0:T(8,128)(2,1)S(1)}, bf16[256,512]{1,0:T(8,128)(2,1)S(1)}, u32[]{:S(2)}, u32[]{:S(2)}) collective-permute-start(bf16[256,512]{1,0:T(8,128)(2,1)S(1)} %gate0.1.refs_0_), channel_id=1, source_target_pairs={{0,6},{1,7},{2,0},{3,1},{4,2},{5,3},{6,4},{7,5},{8,14},{9,15},{10,... | collective-permute-start | bytes 786440 | tf_op jit(solution)/shard_map/ppermute | solution.py:45
  181.3 10.6 %collective-permute-start.15 = (bf16[256,512]{1,0:T(8,128)(2,1)S(1)}, bf16[256,512]{1,0:T(8,128)(2,1)S(1)}, u32[]{:S(2)}, u32[]{:S(2)}) collective-permute-start(bf16[256,512]{1,0:T(8,128)(2,1)S(1)} %gate0.1.refs_0_), channel_id=1, source_target_pairs={{0,2},{1,3},{2,4},{3,5},{4,6},{5,7},{6,0},{7,1},{8,10},{9,11},{10,... | collective-permute-start | bytes 786440 | tf_op jit(solution)/shard_map/ppermute | solution.py:45
  182.6 12.9 %collective-permute-start.27 = (bf16[256,512]{1,0:T(8,128)(2,1)S(1)}, bf16[256,512]{1,0:T(8,128)(2,1)S(1)}, u32[]{:S(2)}, u32[]{:S(2)}) collective-permute-start(bf16[256,512]{1,0:T(8,128)(2,1)S(1)} %collective-permute-done.23.refs_7_), channel_id=1, source_target_pairs={{0,6},{1,7},{2,0},{3,1},{4,2},{5,3},{6,4},{7,5},{8,14},{9,15},{10,... | collective-permute-start | bytes 786440 | tf_op jit(solution)/shard_map/ppermute | solution.py:45
  184.5 12.9 %collective-permute-start.24 = (bf16[256,512]{1,0:T(8,128)(2,1)S(1)}, bf16[256,512]{1,0:T(8,128)(2,1)S(1)}, u32[]{:S(2)}, u32[]{:S(2)}) collective-permute-start(bf16[256,512]{1,0:T(8,128)(2,1)S(1)} %collective-permute-done.23.refs_7_), channel_id=1, source_target_pairs={{0,2},{1,3},{2,4},{3,5},{4,6},{5,7},{6,0},{7,1},{8,10},{9,11},{10,... | collective-permute-start | bytes 786440 | tf_op jit(solution)/shard_map/ppermute | solution.py:45
  187.8 13.3 %collective-permute-start.20 = (bf16[256,512]{1,0:T(8,128)(2,1)S(1)}, bf16[256,512]{1,0:T(8,128)(2,1)S(1)}, u32[]{:S(2)}, u32[]{:S(2)}) collective-permute-start(bf16[256,512]{1,0:T(8,128)(2,1)S(1)} %collective-permute-done.16.refs_1_), channel_id=1, source_target_pairs={{0,6},{1,7},{2,0},{3,1},{4,2},{5,3},{6,4},{7,5},{8,14},{9,15},{10,... | collective-permute-start | bytes 786440 | tf_op jit(solution)/shard_map/ppermute | solution.py:45
  189.8 13.9 %collective-permute-start.17 = (bf16[256,512]{1,0:T(8,128)(2,1)S(1)}, bf16[256,512]{1,0:T(8,128)(2,1)S(1)}, u32[]{:S(2)}, u32[]{:S(2)}) collective-permute-start(bf16[256,512]{1,0:T(8,128)(2,1)S(1)} %collective-permute-done.16.refs_1_), channel_id=1, source_target_pairs={{0,2},{1,3},{2,4},{3,5},{4,6},{5,7},{6,0},{7,1},{8,10},{9,11},{10,... | collective-permute-start | bytes 786440 | tf_op jit(solution)/shard_map/ppermute | solution.py:45
  195.5 15.8 %collective-permute-start.28 = (bf16[256,512]{1,0:T(8,128)(2,1)S(1)}, bf16[256,512]{1,0:T(8,128)(2,1)}, u32[]{:S(2)}, u32[]{:S(2)}) collective-permute-start(bf16[256,512]{1,0:T(8,128)(2,1)S(1)} %pad_maximum_fusion.10), channel_id=1, source_target_pairs={{0,6},{1,7},{2,0},{3,1},{4,2},{5,3},{6,4},{7,5},{8,14},{9,15},{10,... | collective-permute-start | bytes 786440 | tf_op jit(solution)/shard_map/ppermute | solution.py:45
  198.3 13.1 %collective-permute-start.25 = (bf16[256,512]{1,0:T(8,128)(2,1)}, bf16[256,512]{1,0:T(8,128)(2,1)}, u32[]{:S(2)}, u32[]{:S(2)}) collective-permute-start(bf16[256,512]{1,0:T(8,128)(2,1)} %pad_maximum_fusion.9), channel_id=1, source_target_pairs={{0,2},{1,3},{2,4},{3,5},{4,6},{5,7},{6,0},{7,1},{8,10},{9,11},{10,... | collective-permute-start | bytes 786440 | tf_op jit(solution)/shard_map/ppermute | solution.py:45
  (35 other events, 680.2 us)
Sparse Core Ops, SparseCore 0:
  18.2 65.8 all-gather.6
  92.0 50.8 all-gather.8
  144.7 59.0 all-gather.10

commit v6 on v5

--- a/solution.py
+++ b/solution.py
@@ -455,7 +455,7 @@
             pltpu.VMEM((rows, 4 * width) if start else (8, 128), F32),
             pltpu.SemaphoreType.DMA,
         ],
-        compiler_params=pltpu.CompilerParams(vmem_limit_bytes=60 * MIB),
+        compiler_params=pltpu.CompilerParams(vmem_limit_bytes=20 * MIB),
         name="output%d" % parts,
     )(*pieces, weights, *start)
 

time: 223 us -> 222 us (level)
  Pallas kernels: 48.5 us -> 44.8 us
    pallas_call x2, Pallas kernels: 9.1 us -> 5.34 us  [output(): pl.pallas_call(functools.partial(output_kernel, parts_of, len(pieces)), o...]
    unnamed x50 -> x30, local copies, waits for them, and re-layouts: 2.76 us -> 4.91 us
  transfers between devices with their start and end apart: 34 -> 34, of which waited for: 18 -> 18; matrix products, arithmetic and copies ran while one was open for 3% -> 3% of each run, Pallas kernels for 20% -> 19%
where the time goes in v6:
time: 222 us
  waiting for transfers between devices  78.3 us (35%)
  starting transfers between devices  70.8 us (32%)
  Pallas kernels  44.8 us (20%)
  between operations  13.4 us (6%)
  local copies, waits for them, and re-layouts  8.2 us (4%)
  other arithmetic  6.29 us (3%)
    ppermute x18, starting transfers between devices, shift_x(): return lax.ppermute(block, 'tp', route)  45.9 us
    ppermute x18, waiting for transfers between devices, shift_x(): return lax.ppermute(block, 'tp', route)  29.9 us
    pallas_call x2, Pallas kernels, project(): pl.pallas_call(functools.partial(project_kernel, n_proj, len(out_shapes),...  20.2 us
    ppermute x6, waiting for transfers between devices, swap_ctx(): return lax.ppermute(block, 'ctx', [(i, i ^ mask) for i in range(CTX)])  13.9 us
    all_to_all x1, waiting for transfers between devices, local(): back = lax.all_to_all(result.reshape(CTX, 32, 256), 'ctx', 0, 0, tiled=True)  10.7 us
    pallas_call x1, Pallas kernels, conv(): pl.pallas_call(conv_kernel, out_shape=jax.ShapeDtypeStruct((rows, width),...  9.81 us
    all_to_all x1, waiting for transfers between devices, local(): sent = lax.all_to_all(blocks, 'ctx', 0, 0, tiled=True)  9.29 us
    pallas_call x1, Pallas kernels, toeplitz(): pl.pallas_call(toeplitz_kernel, out_shape=jax.ShapeDtypeStruct((64, 256,...  9 us
  transfers between devices with their start and end apart: 34, of which 18 were waited for; matrix products, arithmetic and copies ran while one was open for 3% of the time, Pallas kernels for 19%

profile of v6, /device:TPU:8, one launch (start us, length us, event | category | flops | bytes accessed | tf_op | source)
XLA Modules:
  0.0 221.7 jit_solution(3740555328209003090)
XLA Ops:
  10.6 6.6 %collective-permute-done = bf16[2,144,512]{2,1,0:T(8,128)(2,1)S(1)} collective-permute-done((bf16[2,144,512]{2,1,0:T(8,128)(2,1)S(1)}, bf16[2,144,512]{2,1,0:T(8,128)(2,1)S(1)}, u32[]{:S(2)}, u32[]{:S(2)}) %collective-permute-start) | collective-permute-done | bytes 294944 | tf_op jit(solution)/shard_map/ppermute | solution.py:32
  22.1 9.4 %collective-permute-start.4 = (bf16[512,512]{1,0:T(8,128)(2,1)}, bf16[512,512]{1,0:T(8,128)(2,1)S(1)}, u32[]{:S(2)}, u32[]{:S(2)}) collective-permute-start(bf16[512,512]{1,0:T(8,128)(2,1)} %refs_0_.3), channel_id=1, source_target_pairs={{0,6},{1,7},{2,0},{3,1},{4,2},{5,3},{6,4},{7,5},{8,14},{9,15},{10,... | collective-permute-start | bytes 1572872 | tf_op jit(solution)/shard_map/ppermute | solution.py:45
  34.0 9.7 %collective-permute-start.6 = (bf16[512,512]{1,0:T(8,128)(2,1)S(1)}, bf16[512,512]{1,0:T(8,128)(2,1)S(1)}, u32[]{:S(2)}, u32[]{:S(2)}) collective-permute-start(bf16[512,512]{1,0:T(8,128)(2,1)S(1)} %collective-permute-done.1.refs_1_), channel_id=1, source_target_pairs={{0,6},{1,7},{2,0},{3,1},{4,2},{5,3},{6,4},{7,5},{8,14},{9,15},{10,... | collective-permute-start | bytes 1572872 | tf_op jit(solution)/shard_map/ppermute | solution.py:45
  43.7 3.4 %collective-permute-done.4.refs_3_ = bf16[512,512]{1,0:T(8,128)(2,1)S(1)} collective-permute-done((bf16[512,512]{1,0:T(8,128)(2,1)}, bf16[512,512]{1,0:T(8,128)(2,1)S(1)}, u32[]{:S(2)}, u32[]{:S(2)}) %collective-permute-start.4) | collective-permute-done | bytes 524320 | tf_op jit(solution)/shard_map/ppermute | solution.py:45
  47.1 9.2 %collective-permute-done.6.refs_5_ = bf16[512,512]{1,0:T(8,128)(2,1)S(1)} collective-permute-done((bf16[512,512]{1,0:T(8,128)(2,1)S(1)}, bf16[512,512]{1,0:T(8,128)(2,1)S(1)}, u32[]{:S(2)}, u32[]{:S(2)}) %collective-permute-start.6) | collective-permute-done | bytes 524320 | tf_op jit(solution)/shard_map/ppermute | solution.py:45
  56.3 3.8 %collective-permute-start.7 = (bf16[512,512]{1,0:T(8,128)(2,1)S(1)}, bf16[512,512]{1,0:T(8,128)(2,1)S(1)}, u32[]{:S(2)}, u32[]{:S(2)}) collective-permute-start(bf16[512,512]{1,0:T(8,128)(2,1)S(1)} %pad_maximum_fusion.1), channel_id=1, source_target_pairs={{0,6},{1,7},{2,0},{3,1},{4,2},{5,3},{6,4},{7,5},{8,14},{9,15},{10,... | collective-permute-start | bytes 1572872 | tf_op jit(solution)/shard_map/ppermute | solution.py:45
  61.3 8.5 %collective-permute-done.7.refs_6_.refs_7_ = bf16[512,512]{1,0:T(8,128)(2,1)S(1)} collective-permute-done((bf16[512,512]{1,0:T(8,128)(2,1)S(1)}, bf16[512,512]{1,0:T(8,128)(2,1)S(1)}, u32[]{:S(2)}, u32[]{:S(2)}) %collective-permute-start.7) | collective-permute-done | bytes 524320 | tf_op jit(solution)/shard_map/ppermute | solution.py:45
  73.4 3.4 %collective-permute-done.8.refs_8_ = bf16[8,16,512]{2,1,0:T(8,128)(2,1)S(1)} collective-permute-done((bf16[8,16,512]{2,1,0:T(8,128)(2,1)S(1)}, bf16[8,16,512]{2,1,0:T(8,128)(2,1)S(1)}, u32[]{:S(2)}, u32[]{:S(2)}) %collective-permute-start.8) | collective-permute-done | bytes 131104 | tf_op jit(solution)/shard_map/ppermute | solution.py:482
  76.8 7.3 %all-gather.7.cloned.1.call-done = bf16[16,2,144,512]{3,2,1,0:T(8,128)(2,1)} async-done(((bf16[2,2,144,512]{3,2,1,0:T(8,128)(2,1)}), bf16[16,2,144,512]{3,2,1,0:T(8,128)(2,1)}) %all-gather.7.cloned.1.call-update) | async-done | bytes 4718608 | tf_op jit(solution)/shard_map/all_gather | solution.py:54
  86.6 4.5 %collective-permute-done.10 = bf16[1,128,512]{2,1,0:T(8,128)(2,1)S(1)} collective-permute-done((bf16[1,128,512]{2,1,0:T(8,128)(2,1)S(1)}, bf16[1,128,512]{2,1,0:T(8,128)(2,1)S(1)}, u32[]{:S(2)}, u32[]{:S(2)}) %collective-permute-start.10) | collective-permute-done | bytes 131104 | tf_op jit(solution)/shard_map/ppermute | solution.py:32
  92.5 10.7 %project2.1 = (bf16[512,512]{1,0:T(8,128)(2,1)}, bf16[32,32,256]{2,1,0:T(8,128)(2,1)}) custom-call(bf16[512,512]{1,0:T(8,128)(2,1)} %refs_0_.3, bf16[512,512]{1,0:T(8,128)(2,1)} %copy-done.8, bf16[512,512]{1,0:T(8,128)(2,1)} %copy-done.5, bf16[512,512]{1,0:T(8,128)(2,1)} %copy-done.3, bf16[512,512]{1,0:T(8,128)(2,1)} %copy-done.6, ...), custom_call_target="tpu_custom_call" | custom-call | tf_op jit(solution)/shard_map/project2/pallas_call | solution.py:213
  103.2 4.9 %all-to-all-start = ((bf16[32,32,256]{2,1,0:T(8,128)(2,1)}), bf16[32,32,256]{2,1,0:T(8,128)(2,1)S(1)}, u32[]{:S(2)}, u32[]{:S(2)}) async-start(bf16[32,32,256]{2,1,0:T(8,128)(2,1)} %get-tuple-element.45), calls=%async_computation | async-start | bytes 1048576 | tf_op jit(solution)/shard_map/all_to_all | solution.py:502
  110.3 9.0 %toeplitz.1 = bf16[64,256,256]{2,1,0:T(8,128)(2,1)} custom-call(bf16[8,2,2,144,512]{4,3,2,1,0:T(8,128)(2,1)} %bitcast.24, bf16[8,2,2,144,512]{4,3,2,1,0:T(8,128)(2,1)} %collective-permute-done.11.refs_10_.other), custom_call_target="tpu_custom_call" | custom-call | tf_op jit(solution)/shard_map/toeplitz/pallas_call | solution.py:285
  121.7 9.3 %all-to-all-done = bf16[32,32,256]{2,1,0:T(8,128)(2,1)S(1)} async-done(((bf16[32,32,256]{2,1,0:T(8,128)(2,1)}), bf16[32,32,256]{2,1,0:T(8,128)(2,1)S(1)}, u32[]{:S(2)}, u32[]{:S(2)}) %all-to-all-start) | async-done | bytes 524320 | tf_op jit(solution)/shard_map/all_to_all | solution.py:502
  131.9 9.8 %conv.1 = bf16[1024,256]{1,0:T(8,128)(2,1)} custom-call(bf16[1024,256]{1,0:T(8,128)(2,1)} %bitcast.25, bf16[16384,256]{1,0:T(8,128)(2,1)} %bitcast.21), custom_call_target="tpu_custom_call" | custom-call | tf_op jit(solution)/shard_map/conv/pallas_call | solution.py:353
  143.1 5.6 %all-to-all-start.1 = ((bf16[32,32,256]{2,1,0:T(8,128)(2,1)}), bf16[32,32,256]{2,1,0:T(8,128)(2,1)S(1)}, u32[]{:S(2)}, u32[]{:S(2)}) async-start(bf16[32,32,256]{2,1,0:T(8,128)(2,1)} %bitcast.26), calls=%async_computation.1 | async-start | bytes 1048576 | tf_op jit(solution)/shard_map/all_to_all | solution.py:507
  149.2 9.5 %project1.1.query_ref = f32[512,512]{1,0:T(8,128)} custom-call(bf16[512,512]{1,0:T(8,128)(2,1)} %refs_0_.3, bf16[512,512]{1,0:T(8,128)(2,1)} %copy-done.8, bf16[512,512]{1,0:T(8,128)(2,1)} %copy-done.5, bf16[512,512]{1,0:T(8,128)(2,1)} %copy-done.3, bf16[512,512]{1,0:T(8,128)(2,1)} %copy-done.6, bf16[512,512]{1,0:T(8,128)(2,1)} %copy-done.4, ...), custom_call_target="tpu_custom_call" | custom-call | tf_op jit(solution)/shard_map/project1/pallas_call | solution.py:213
  158.7 10.7 %all-to-all-done.1.back_ref = bf16[32,32,256]{2,1,0:T(8,128)(2,1)S(1)} async-done(((bf16[32,32,256]{2,1,0:T(8,128)(2,1)}), bf16[32,32,256]{2,1,0:T(8,128)(2,1)S(1)}, u32[]{:S(2)}, u32[]{:S(2)}) %all-to-all-start.1) | async-done | bytes 524320 | tf_op jit(solution)/shard_map/all_to_all | solution.py:507
  170.8 2.5 %collective-permute-start.23 = (bf16[256,512]{1,0:T(8,128)(2,1)S(1)}, bf16[256,512]{1,0:T(8,128)(2,1)S(1)}, u32[]{:S(2)}, u32[]{:S(2)}) collective-permute-start(bf16[256,512]{1,0:T(8,128)(2,1)S(1)} %gate1.1.refs_6_), channel_id=1, source_target_pairs={{0,1},{1,0},{2,3},{3,2},{4,5},{5,4},{6,7},{7,6},{8,9},{9,8},{10,11... | collective-permute-start | bytes 786440 | tf_op jit(solution)/shard_map/ppermute | solution.py:49
  177.9 3.5 %collective-permute-start.19 = (bf16[256,512]{1,0:T(8,128)(2,1)S(1)}, bf16[256,512]{1,0:T(8,128)(2,1)S(1)}, u32[]{:S(2)}, u32[]{:S(2)}) collective-permute-start(bf16[256,512]{1,0:T(8,128)(2,1)S(1)} %gate0.1.refs_0_), channel_id=1, source_target_pairs={{0,6},{1,7},{2,0},{3,1},{4,2},{5,3},{6,4},{7,5},{8,14},{9,15},{10,... | collective-permute-start | bytes 786440 | tf_op jit(solution)/shard_map/ppermute | solution.py:45
  184.6 3.2 %collective-permute-start.24 = (bf16[256,512]{1,0:T(8,128)(2,1)S(1)}, bf16[256,512]{1,0:T(8,128)(2,1)S(1)}, u32[]{:S(2)}, u32[]{:S(2)}) collective-permute-start(bf16[256,512]{1,0:T(8,128)(2,1)S(1)} %collective-permute-done.23.refs_7_), channel_id=1, source_target_pairs={{0,2},{1,3},{2,4},{3,5},{4,6},{5,7},{6,0},{7,1},{8,10},{9,11},{10,... | collective-permute-start | bytes 786440 | tf_op jit(solution)/shard_map/ppermute | solution.py:45
  192.0 3.6 %collective-permute-done.27.refs_11_ = bf16[256,512]{1,0:T(8,128)(2,1)S(1)} collective-permute-done((bf16[256,512]{1,0:T(8,128)(2,1)S(1)}, bf16[256,512]{1,0:T(8,128)(2,1)S(1)}, u32[]{:S(2)}, u32[]{:S(2)}) %collective-permute-start.27) | collective-permute-done | bytes 262176 | tf_op jit(solution)/shard_map/ppermute | solution.py:45
  207.9 2.6 %output6.1.refs_5_ = f32[512,512]{1,0:T(8,128)S(1)} custom-call(bf16[256,512]{1,0:T(8,128)(2,1)S(1)} %gate0.1.refs_0_, bf16[256,512]{1,0:T(8,128)(2,1)S(1)} %collective-permute-done.16.refs_1_, bf16[256,512]{1,0:T(8,128)(2,1)S(1)} %collective-permute-done.15.refs_2_, bf16[256,512]{1,0:T(8,128)(2,1)S(1)} %collective-permute-done.19.refs_3_, ...), custom_call_target="tpu_custom_call" | custom-call | tf_op jit(solution)/shard_map/output6/pallas_call | solution.py:447
  212.4 2.7 %output2.1 = bf16[512,512]{1,0:T(8,128)(2,1)} custom-call(bf16[256,512]{1,0:T(8,128)(2,1)} %collective-permute-done.18.refs_0_, bf16[256,512]{1,0:T(8,128)(2,1)} %collective-permute-done.21.refs_1_, bf16[256,512]{1,0:T(8,128)(2,1)} %collective-permute-done.25.refs_2_, bf16[256,512]{1,0:T(8,128)(2,1)S(1)} %collective-permute-done.28.refs_3_, ...), custom_call_target="tpu_custom_call" | custom-call | tf_op jit(solution)/shard_map/output2/pallas_call | solution.py:447
  (113 shorter events, 55.1 us)
Async XLA Ops:
  6.5 77.6 %all-gather.7.cloned.1.call-start = ((), (), s32[]{:S(2)}) async-start(), calls=%async_computation.2 | async-start | bytes 5308416 | tf_op jit(solution)/shard_map/all_gather | solution.py:54
  18.1 124.8 %all-gather.9.cloned.1.call-start = ((), (), s32[]{:S(2)}) async-start(), calls=%async_computation.3 | async-start | bytes 2359296 | tf_op jit(solution)/shard_map/all_gather | solution.py:54
  18.2 15.8 %collective-permute-start.1 = (bf16[512,512]{1,0:T(8,128)(2,1)}, bf16[512,512]{1,0:T(8,128)(2,1)S(1)}, u32[]{:S(2)}, u32[]{:S(2)}) collective-permute-start(bf16[512,512]{1,0:T(8,128)(2,1)} %refs_0_.3), channel_id=1, source_target_pairs={{0,1},{1,0},{2,3},{3,2},{4,5},{5,4},{6,7},{7,6},{8,9},{9,8},{10,11... | collective-permute-start | bytes 1572872 | tf_op jit(solution)/shard_map/ppermute | solution.py:49
  20.6 11.0 %collective-permute-start.2 = (bf16[512,128]{1,0:T(8,128)(2,1)}, bf16[512,128]{1,0:T(8,128)(2,1)S(1)}, u32[]{:S(2)}, u32[]{:S(2)}) collective-permute-start(bf16[512,128]{1,0:T(8,128)(2,1)} %param.11), channel_id=1, source_target_pairs={{0,0},{1,32},{2,64},{3,96},{4,128},{5,160},{6,192},{7,224},{8,8},{... | collective-permute-start | bytes 393224 | tf_op jit(solution)/shard_map/ppermute | solution.py:479
  22.1 24.9 %collective-permute-start.4 = (bf16[512,512]{1,0:T(8,128)(2,1)}, bf16[512,512]{1,0:T(8,128)(2,1)S(1)}, u32[]{:S(2)}, u32[]{:S(2)}) collective-permute-start(bf16[512,512]{1,0:T(8,128)(2,1)} %refs_0_.3), channel_id=1, source_target_pairs={{0,6},{1,7},{2,0},{3,1},{4,2},{5,3},{6,4},{7,5},{8,14},{9,15},{10,... | collective-permute-start | bytes 1572872 | tf_op jit(solution)/shard_map/ppermute | solution.py:45
  34.0 22.2 %collective-permute-start.6 = (bf16[512,512]{1,0:T(8,128)(2,1)S(1)}, bf16[512,512]{1,0:T(8,128)(2,1)S(1)}, u32[]{:S(2)}, u32[]{:S(2)}) collective-permute-start(bf16[512,512]{1,0:T(8,128)(2,1)S(1)} %collective-permute-done.1.refs_1_), channel_id=1, source_target_pairs={{0,6},{1,7},{2,0},{3,1},{4,2},{5,3},{6,4},{7,5},{8,14},{9,15},{10,... | collective-permute-start | bytes 1572872 | tf_op jit(solution)/shard_map/ppermute | solution.py:45
  43.7 16.4 %collective-permute-start.3 = (bf16[512,512]{1,0:T(8,128)(2,1)}, bf16[512,512]{1,0:T(8,128)(2,1)S(1)}, u32[]{:S(2)}, u32[]{:S(2)}) collective-permute-start(bf16[512,512]{1,0:T(8,128)(2,1)} %refs_0_.3), channel_id=1, source_target_pairs={{0,2},{1,3},{2,4},{3,5},{4,6},{5,7},{6,0},{7,1},{8,10},{9,11},{10,... | collective-permute-start | bytes 1572872 | tf_op jit(solution)/shard_map/ppermute | solution.py:45
  43.7 16.4 %collective-permute-start.5 = (bf16[512,512]{1,0:T(8,128)(2,1)S(1)}, bf16[512,512]{1,0:T(8,128)(2,1)S(1)}, u32[]{:S(2)}, u32[]{:S(2)}) collective-permute-start(bf16[512,512]{1,0:T(8,128)(2,1)S(1)} %collective-permute-done.1.refs_1_), channel_id=1, source_target_pairs={{0,2},{1,3},{2,4},{3,5},{4,6},{5,7},{6,0},{7,1},{8,10},{9,11},{10,... | collective-permute-start | bytes 1572872 | tf_op jit(solution)/shard_map/ppermute | solution.py:45
  56.3 13.4 %collective-permute-start.7 = (bf16[512,512]{1,0:T(8,128)(2,1)S(1)}, bf16[512,512]{1,0:T(8,128)(2,1)S(1)}, u32[]{:S(2)}, u32[]{:S(2)}) collective-permute-start(bf16[512,512]{1,0:T(8,128)(2,1)S(1)} %pad_maximum_fusion.1), channel_id=1, source_target_pairs={{0,6},{1,7},{2,0},{3,1},{4,2},{5,3},{6,4},{7,5},{8,14},{9,15},{10,... | collective-permute-start | bytes 1572872 | tf_op jit(solution)/shard_map/ppermute | solution.py:45
  60.2 13.2 %collective-permute-start.9 = (bf16[512,512]{1,0:T(8,128)(2,1)S(1)}, bf16[512,512]{1,0:T(8,128)(2,1)}, u32[]{:S(2)}, u32[]{:S(2)}) collective-permute-start(bf16[512,512]{1,0:T(8,128)(2,1)S(1)} %pad_maximum_fusion.2), channel_id=1, source_target_pairs={{0,2},{1,3},{2,4},{3,5},{4,6},{5,7},{6,0},{7,1},{8,10},{9,11},{10,... | collective-permute-start | bytes 1572872 | tf_op jit(solution)/shard_map/ppermute | solution.py:45
  103.2 27.8 %all-to-all-start = ((bf16[32,32,256]{2,1,0:T(8,128)(2,1)}), bf16[32,32,256]{2,1,0:T(8,128)(2,1)S(1)}, u32[]{:S(2)}, u32[]{:S(2)}) async-start(bf16[32,32,256]{2,1,0:T(8,128)(2,1)} %get-tuple-element.45), calls=%async_computation | async-start | bytes 1048576 | tf_op jit(solution)/shard_map/all_to_all | solution.py:502
  108.1 97.6 %all-gather.11.cloned.1.call-start = ((), (), s32[]{:S(2)}) async-start(), calls=%async_computation.4 | async-start | bytes 4718592 | tf_op jit(solution)/shard_map/all_gather | solution.py:54
  109.8 11.1 %collective-permute-start.13 = (bf16[2,512,128]{2,1,0:T(8,128)(2,1)S(1)}, bf16[2,512,128]{2,1,0:T(8,128)(2,1)S(1)}, u32[]{:S(2)}, u32[]{:S(2)}) collective-permute-start(bf16[2,512,128]{2,1,0:T(8,128)(2,1)S(1)} %pad_maximum_fusion.6), channel_id=1, source_target_pairs={{0,16},{8,24},{16,0},{24,8},{32,48},{40,56},{48,32},{56,40},{64,80... | collective-permute-start | bytes 786440 | tf_op jit(solution)/shard_map/ppermute | solution.py:32
  143.1 26.4 %all-to-all-start.1 = ((bf16[32,32,256]{2,1,0:T(8,128)(2,1)}), bf16[32,32,256]{2,1,0:T(8,128)(2,1)S(1)}, u32[]{:S(2)}, u32[]{:S(2)}) async-start(bf16[32,32,256]{2,1,0:T(8,128)(2,1)} %bitcast.26), calls=%async_computation.1 | async-start | bytes 1048576 | tf_op jit(solution)/shard_map/all_to_all | solution.py:507
  170.8 10.5 %collective-permute-start.23 = (bf16[256,512]{1,0:T(8,128)(2,1)S(1)}, bf16[256,512]{1,0:T(8,128)(2,1)S(1)}, u32[]{:S(2)}, u32[]{:S(2)}) collective-permute-start(bf16[256,512]{1,0:T(8,128)(2,1)S(1)} %gate1.1.refs_6_), channel_id=1, source_target_pairs={{0,1},{1,0},{2,3},{3,2},{4,5},{5,4},{6,7},{7,6},{8,9},{9,8},{10,11... | collective-permute-start | bytes 786440 | tf_op jit(solution)/shard_map/ppermute | solution.py:49
  176.7 11.1 %collective-permute-start.16 = (bf16[256,512]{1,0:T(8,128)(2,1)S(1)}, bf16[256,512]{1,0:T(8,128)(2,1)S(1)}, u32[]{:S(2)}, u32[]{:S(2)}) collective-permute-start(bf16[256,512]{1,0:T(8,128)(2,1)S(1)} %gate0.1.refs_0_), channel_id=1, source_target_pairs={{0,1},{1,0},{2,3},{3,2},{4,5},{5,4},{6,7},{7,6},{8,9},{9,8},{10,11... | collective-permute-start | bytes 786440 | tf_op jit(solution)/shard_map/ppermute | solution.py:49
  177.9 12.0 %collective-permute-start.19 = (bf16[256,512]{1,0:T(8,128)(2,1)S(1)}, bf16[256,512]{1,0:T(8,128)(2,1)S(1)}, u32[]{:S(2)}, u32[]{:S(2)}) collective-permute-start(bf16[256,512]{1,0:T(8,128)(2,1)S(1)} %gate0.1.refs_0_), channel_id=1, source_target_pairs={{0,6},{1,7},{2,0},{3,1},{4,2},{5,3},{6,4},{7,5},{8,14},{9,15},{10,... | collective-permute-start | bytes 786440 | tf_op jit(solution)/shard_map/ppermute | solution.py:45
  181.4 10.6 %collective-permute-start.15 = (bf16[256,512]{1,0:T(8,128)(2,1)S(1)}, bf16[256,512]{1,0:T(8,128)(2,1)S(1)}, u32[]{:S(2)}, u32[]{:S(2)}) collective-permute-start(bf16[256,512]{1,0:T(8,128)(2,1)S(1)} %gate0.1.refs_0_), channel_id=1, source_target_pairs={{0,2},{1,3},{2,4},{3,5},{4,6},{5,7},{6,0},{7,1},{8,10},{9,11},{10,... | collective-permute-start | bytes 786440 | tf_op jit(solution)/shard_map/ppermute | solution.py:45
  182.4 13.1 %collective-permute-start.27 = (bf16[256,512]{1,0:T(8,128)(2,1)S(1)}, bf16[256,512]{1,0:T(8,128)(2,1)S(1)}, u32[]{:S(2)}, u32[]{:S(2)}) collective-permute-start(bf16[256,512]{1,0:T(8,128)(2,1)S(1)} %collective-permute-done.23.refs_7_), channel_id=1, source_target_pairs={{0,6},{1,7},{2,0},{3,1},{4,2},{5,3},{6,4},{7,5},{8,14},{9,15},{10,... | collective-permute-start | bytes 786440 | tf_op jit(solution)/shard_map/ppermute | solution.py:45
  184.6 13.6 %collective-permute-start.24 = (bf16[256,512]{1,0:T(8,128)(2,1)S(1)}, bf16[256,512]{1,0:T(8,128)(2,1)S(1)}, u32[]{:S(2)}, u32[]{:S(2)}) collective-permute-start(bf16[256,512]{1,0:T(8,128)(2,1)S(1)} %collective-permute-done.23.refs_7_), channel_id=1, source_target_pairs={{0,2},{1,3},{2,4},{3,5},{4,6},{5,7},{6,0},{7,1},{8,10},{9,11},{10,... | collective-permute-start | bytes 786440 | tf_op jit(solution)/shard_map/ppermute | solution.py:45
  187.8 13.3 %collective-permute-start.20 = (bf16[256,512]{1,0:T(8,128)(2,1)S(1)}, bf16[256,512]{1,0:T(8,128)(2,1)S(1)}, u32[]{:S(2)}, u32[]{:S(2)}) collective-permute-start(bf16[256,512]{1,0:T(8,128)(2,1)S(1)} %collective-permute-done.16.refs_1_), channel_id=1, source_target_pairs={{0,6},{1,7},{2,0},{3,1},{4,2},{5,3},{6,4},{7,5},{8,14},{9,15},{10,... | collective-permute-start | bytes 786440 | tf_op jit(solution)/shard_map/ppermute | solution.py:45
  189.9 13.9 %collective-permute-start.17 = (bf16[256,512]{1,0:T(8,128)(2,1)S(1)}, bf16[256,512]{1,0:T(8,128)(2,1)S(1)}, u32[]{:S(2)}, u32[]{:S(2)}) collective-permute-start(bf16[256,512]{1,0:T(8,128)(2,1)S(1)} %collective-permute-done.16.refs_1_), channel_id=1, source_target_pairs={{0,2},{1,3},{2,4},{3,5},{4,6},{5,7},{6,0},{7,1},{8,10},{9,11},{10,... | collective-permute-start | bytes 786440 | tf_op jit(solution)/shard_map/ppermute | solution.py:45
  196.3 14.3 %collective-permute-start.28 = (bf16[256,512]{1,0:T(8,128)(2,1)}, bf16[256,512]{1,0:T(8,128)(2,1)S(1)}, u32[]{:S(2)}, u32[]{:S(2)}) collective-permute-start(bf16[256,512]{1,0:T(8,128)(2,1)} %pad_maximum_fusion.10), channel_id=1, source_target_pairs={{0,6},{1,7},{2,0},{3,1},{4,2},{5,3},{6,4},{7,5},{8,14},{9,15},{10,... | collective-permute-start | bytes 786440 | tf_op jit(solution)/shard_map/ppermute | solution.py:45
  198.9 11.7 %collective-permute-start.25 = (bf16[256,512]{1,0:T(8,128)(2,1)}, bf16[256,512]{1,0:T(8,128)(2,1)}, u32[]{:S(2)}, u32[]{:S(2)}) collective-permute-start(bf16[256,512]{1,0:T(8,128)(2,1)} %pad_maximum_fusion.9), channel_id=1, source_target_pairs={{0,2},{1,3},{2,4},{3,5},{4,6},{5,7},{6,0},{7,1},{8,10},{9,11},{10,... | collective-permute-start | bytes 786440 | tf_op jit(solution)/shard_map/ppermute | solution.py:45
  (25 other events, 480.4 us)
Sparse Core Ops, SparseCore 0:
  18.2 65.8 all-gather.6
  92.0 50.8 all-gather.8
  144.7 58.9 all-gather.10
